TPU v7x, 32 devices: a whole 2x2x4 slice. The times are simulated.
32 devices in a mesh: blk: 16 (over z, x, core), rel: 2 (over y).
Axes of the slice: x: 2, y: 2, z: 4, core: 2. Of those that a mesh axis runs over, the one named last changes fastest.
Arguments:
- left_slab: float32 [65536, 400], P(('blk', 'rel')), may hold values from -1.3 to 1.3
- left_state: float32 [65536], P(('blk', 'rel')), may hold values from 1e-05 to 0.0001
- right_slab: float32 [65536, 400], P(('blk', 'rel')), may hold values from -1.3 to 1.3
- right_state: float32 [65536], P(('blk', 'rel')), may hold values from 1e-05 to 0.0001
- relations: float32 [32, 400], replicated, may hold values from 0.1 to 1.9
- relation_state: float32 [32], replicated, may hold values from 0.01 to 0.2
- src_index: int32 [2, 8192], P(None, ('blk', 'rel')), may hold values from 0 to 2047
- dst_index: int32 [2, 8192], P(None, ('blk', 'rel')), may hold values from 0 to 2047
- relation_id: int32 [2, 8192], P(None, ('blk', 'rel')), may hold values from 0 to 31
- neg_source: int32 [2, 32000], P(None, ('blk', 'rel')), may hold values from 0 to 2047
- neg_target: int32 [2, 32000], P(None, ('blk', 'rel')), may hold values from 0 to 2047
Outputs:
- left_out: float32 [65536, 400], P(('blk', 'rel'))
- right_out: float32 [65536, 400], P(('blk', 'rel'))
- relations_out: float32 [16, 32, 400], P('blk')
All inputs are finite; a program needn't handle non-finite values.
Results may differ from a plain program's by a relative error of at most 0.00069.
Values sent between devices are 32-bit elements; how exact they have to be, the bound alone decides.
No kernel may reach another device: no remote copies, remote signals or barrier semaphores. Data moves between devices by JAX's collectives and lax.ppermute only.
A program may use at most 64 MiB of HBM per device.

v0:
```python
import functools

import jax
import jax.numpy as jnp
from jax import lax
from jax.experimental import pallas as pl
from jax.experimental.pallas import tpu as pltpu
from jax.sharding import PartitionSpec as P

rate = 0.1
F32 = jnp.float32
BF16 = jnp.bfloat16
LANES = 128
STEP = 256
NEAR = (4, 4)
FAR = (5, 2, 1)
VMEM_LIMIT = 30 * 2**20

NN = (((1,), (0,)), ((), ()))
NT = (((1,), (1,)), ((), ()))
TN = (((0,), (0,)), ((), ()))


def mul(a, b, dims):
    return lax.dot_general(a, b, dims, preferred_element_type=F32)


def split(x, parts):
    out = []
    for _ in range(parts):
        part = x.astype(BF16)
        out.append(part)
        x = x - part.astype(F32)
    return out


def lanes_at(i, size):
    return pl.ds(pl.multiple_of(i * size, size), size)


def row_onehot(idx, table):
    count, rows = table.shape
    col = jnp.broadcast_to(idx, (LANES, count)).T
    lane = lax.broadcasted_iota(jnp.int32, (count, LANES), 1)

    def tile(t, carry):
        hit = col == lane + t * LANES
        table[:, lanes_at(t, LANES)] = jnp.where(hit, 1.0, 0.0).astype(BF16)
        return carry

    lax.fori_loop(0, rows // LANES, tile, 0)


def row_counts(idx, rows):
    count = idx.shape[1]
    high = lax.broadcasted_iota(jnp.int32, (rows // LANES, count), 0)
    low = lax.broadcasted_iota(jnp.int32, (LANES, count), 0)
    high_hit = jnp.where(idx // LANES == high, 1.0, 0.0).astype(BF16)
    low_hit = jnp.where(idx % LANES == low, 1.0, 0.0).astype(BF16)
    return mul(high_hit, low_hit, NT)


def times_at(counts, i):
    tiles = STEP // LANES
    return jnp.concatenate([counts[pl.ds(i * tiles + t, 1), :] for t in range(tiles)], axis=1)


def half_rows(x):
    return (0.5 * x).T.astype(BF16)


def negatives(rows16, query, query_rows, times, number):
    half = 0.5 / number
    weight = (jnp.tanh(mul(query_rows, rows16, NN)) * half + half).astype(BF16)
    often = (weight.astype(F32) * times).astype(BF16)
    return mul(query, weight, NN) * times, mul(rows16, often, NT)


def prepare(step, left, relations, src, dst, rid, nsrc, ndst,
            weight, source, query, query_rows, left16, oh_src, oh_dst, count_l, count_r, kind):
    rows = left.shape[1]
    here = slice(step, step + 1)
    row_onehot(src[here, :], oh_src)
    row_onehot(dst[here, :], oh_dst)
    count_l[...] = row_counts(nsrc[here, :], rows)
    count_r[...] = row_counts(ndst[here, :], rows)
    kinds = lax.broadcasted_iota(jnp.int32, kind.shape, 0)
    kind[...] = jnp.where(rid[here, :] == kinds, 1.0, 0.0).astype(BF16)
    weight[...] = sum(mul(part, kind[...], TN) for part in split(relations[...], 3))
    source[...] = jnp.zeros_like(source)

    def part(i, carry):
        cut = lanes_at(i, STEP)
        parts = split(left[:, cut], 3)
        left16[:, cut] = parts[0]
        source[...] += sum(mul(p, oh_src[:, cut], NT) for p in parts)
        return carry

    lax.fori_loop(0, rows // STEP, part, 0)
    product = source[...] * weight[...]
    query[...] = product.astype(BF16)
    query_rows[...] = half_rows(product.astype(BF16).astype(F32))


def take_piece(number, start, piece, query, query_rows, oh_dst, count_r, target, gq, rgrad):
    depth = target.shape[0]
    if start == 0:
        target[...] = jnp.zeros_like(target)
        gq[...] = jnp.zeros_like(gq)

    def part(i, carry):
        cut = lanes_at(i, STEP)
        parts = split(piece[0:depth, cut], 3)
        hits = oh_dst[:, lanes_at(i + start // STEP, STEP)]
        target[...] += sum(mul(p, hits, NT) for p in parts)
        times = times_at(count_r, i + start // STEP)
        rgrad[:, cut], more = negatives(parts[0], query[...], query_rows[...], times, number)
        gq[...] += more
        return carry

    lax.fori_loop(0, piece.shape[1] // STEP, part, 0)


def join(number, weight, source, target, gq, left16, count_l, kind, rel_in, probe, probe_rows, gp, lgrad, to_src, to_dst, rel_out):
    rows = left16.shape[1]
    product = weight[...] * target[...]
    probe[...] = product.astype(BF16)
    probe_rows[...] = half_rows(product.astype(BF16).astype(F32))
    gp[...] = jnp.zeros_like(gp)

    def part(i, carry):
        cut = lanes_at(i, STEP)
        lgrad[:, cut], more = negatives(left16[:, cut], probe[...], probe_rows[...], times_at(count_l, i), number)
        gp[...] += more
        return carry

    lax.fori_loop(0, rows // STEP, part, 0)
    depth = weight.shape[0]
    w, s, t = weight[...], source[...], target[...]
    coef = -jax.nn.sigmoid(-jnp.sum(s * w * t, axis=0, keepdims=True))
    to_src[0:depth, :], to_src[depth:, :] = split(coef * w * t + gq[...] * w, 2)
    to_dst[0:depth, :], to_dst[depth:, :] = split(coef * w * s + gp[...] * w, 2)
    g_weight = coef * s * t + gq[...] * s + gp[...] * t
    rel_out[...] = rel_in[...] + sum(mul(kind[...], p, NT) for p in split(g_weight, 2))


def adagrad(slab, state, grad, edges, table, start, out, new_state, send=None):
    depth = grad.shape[0]

    def part(i, carry):
        cut = lanes_at(i, STEP)
        hits = table[:, lanes_at(i + start // STEP, STEP)]
        g = grad[:, cut] + mul(edges[0:depth, :], hits, NN) + mul(edges[depth:, :], hits, NN)
        new = state[:, cut] + jnp.sum(g * g, axis=0, keepdims=True) * (1.0 / depth)
        new_state[:, cut] = new
        out[0:depth, cut] = slab[0:depth, cut] - g * (rate * lax.rsqrt(new))
        if send is not None:
            send(i).start()
        return carry

    lax.fori_loop(0, grad.shape[1] // STEP, part, 0)


def sender(result, to, start, sems):
    def copy(i):
        here = lanes_at(i, STEP)
        there = lanes_at(i + start // STEP, STEP)
        return pltpu.make_async_copy(result.at[:, here], to.at[:, there], sems.at[i + start // STEP])

    return copy


def wait_all(copy, count):
    def one(i, carry):
        copy(i).wait()
        return carry

    lax.fori_loop(0, count, one, 0)


def finish_last(left, lstate, right, rstate, lgrad, rgrads, to_src, to_dst, oh_src, oh_dst, spare, left_out, right_out, sems):
    start = 0
    sent = []
    for piece, state, grad in zip(right, rstate, rgrads):
        copy = sender(grad, right_out, start, sems.at[0])
        adagrad(piece, state, grad, to_dst, oh_dst, start, grad, spare, copy)
        sent.append((copy, piece.shape[1] // STEP))
        start += piece.shape[1]
    copy = sender(lgrad, left_out, 0, sems.at[1])
    adagrad(left, lstate, lgrad, to_src, oh_src, 0, lgrad, spare, copy)
    sent.append((copy, left.shape[1] // STEP))
    for copy, count in sent:
        wait_all(copy, count)


def on_parity(parity):
    return pl.when(lax.axis_index("blk") % 2 == parity)


def pieces_of(rows, eighths):
    sizes = [rows // 8 * n for n in eighths]
    return [(sum(sizes[:i]), size) for i, size in enumerate(sizes)]


def train(parity, step, number, last, kept, takes, gives, *refs):
    refs = list(refs)
    (left, lstate, rstate_in, relations, rel_in, src, dst, rid, nsrc, ndst) = refs[:10]
    right = refs[10 : 10 + takes]
    refs = refs[10 + takes + kept :]
    left_out, lstate_out, rel_out = refs[:3]
    right_out = refs[3 : 3 + len(gives)]
    (weight, source, query, query_rows, left16, oh_src, oh_dst, count_l, count_r, kind,
     target, gq, rgrad, probe, probe_rows, gp, lgrad, to_src, to_dst, spare, sems) = refs[3 + len(gives) :]
    depth, rows = left.shape
    lstate_out[...] = lstate[...]
    rel_out[...] = rel_in[...]

    @on_parity(parity)
    def _():
        prepare(step, left, relations, src, dst, rid, nsrc, ndst,
                weight, source, query, query_rows, left16, oh_src, oh_dst, count_l, count_r, kind)
        grads = []
        at = 0
        for piece in right:
            grads.append(rgrad.at[:, at : at + piece.shape[1]])
            take_piece(number, at, piece, query, query_rows, oh_dst, count_r, target, gq, grads[-1])
            at += piece.shape[1]
        join(number, weight, source, target, gq, left16, count_l, kind, rel_in, probe, probe_rows, gp, lgrad, to_src, to_dst, rel_out)
        if last:
            states = [piece.at[depth : depth + 1] for piece in right]
            finish_last(left, lstate, right, states, lgrad, grads, to_src, to_dst, oh_src, oh_dst, spare, left_out, right_out[0], sems)
        else:
            for (at, size), out in zip(pieces_of(rows, gives), right_out):
                cut = slice(at, at + size)
                adagrad(right[0].at[:, cut], rstate_in.at[:, cut], rgrad.at[:, cut], to_dst, oh_dst, at, out, spare)
                out[depth : depth + 8, :] = jnp.broadcast_to(spare[:, 0:size], (8, size))
            adagrad(left, lstate, lgrad, to_src, oh_src, 0, left_out, lstate_out)


def shape(*dims, dtype=F32):
    return jax.ShapeDtypeStruct(dims, dtype)


def prepared_shapes(depth, rows, edges, kinds):
    return (
        shape(depth, edges), shape(depth, edges), shape(depth, edges, dtype=BF16), shape(edges, depth, dtype=BF16),
        shape(depth, rows, dtype=BF16), shape(edges, rows, dtype=BF16), shape(edges, rows, dtype=BF16),
        shape(rows // LANES, LANES), shape(rows // LANES, LANES), shape(kinds, edges, dtype=BF16),
    )


def scratch(shapes):
    return [pltpu.VMEM(s.shape, s.dtype) for s in shapes]


def call(kernel, name, operands, shapes, in_large=(), out_large=(), scratch_shapes=(), aliases=None):
    vmem = pl.BlockSpec(memory_space=pltpu.VMEM)
    large = pl.BlockSpec(memory_space=pl.ANY)
    return pl.pallas_call(
        kernel,
        out_shape=tuple(shapes),
        in_specs=[large if i in in_large else vmem for i in range(len(operands))],
        out_specs=tuple(large if i in out_large else vmem for i in range(len(shapes))),
        scratch_shapes=list(scratch_shapes),
        input_output_aliases=aliases or {},
        compiler_params=pltpu.CompilerParams(vmem_limit_bytes=VMEM_LIMIT),
        cost_estimate=pl.CostEstimate(flops=1_000_000, bytes_accessed=100_000, transcendentals=0),
        name=name,
    )(*operands)


def trained(parity, step, gives, left, lstate, right, rstate, relations, rel, index, keep=()):
    depth, rows = left.shape
    edges = index[0].shape[1]
    number = float(index[3].shape[1])
    last = not gives
    blocks = [shape(depth + 8, size) for _at, size in pieces_of(rows, gives)] or [shape(depth, rows)]
    edge = shape(depth, edges)
    edge16 = shape(depth, edges, dtype=BF16)
    pair16 = shape(2 * depth, edges, dtype=BF16)
    slab = shape(depth, rows)
    inner = [edge, edge, slab, edge16, shape(edges, depth, dtype=BF16), edge, slab, pair16, pair16, shape(1, rows)]
    left_out, lstate_out, rel_out, *right_out = call(
        functools.partial(train, parity, step, number, last, len(keep), len(right), gives or (8,)),
        "round%d_parity%d" % (step, parity),
        [left, lstate, rstate, relations, rel, *index, *right, *keep],
        [slab, shape(1, rows), shape(*relations.shape), *blocks],
        out_large=(0, 3) if last else (),
        scratch_shapes=[
            *scratch(prepared_shapes(depth, rows, edges, relations.shape[0])),
            *scratch(inner),
            pltpu.SemaphoreType.DMA((2, rows // STEP)),
        ],
        aliases={10 + len(right) + i: 0 for i in range(len(keep))},
    )
    return left_out, lstate_out, right_out, rel_out


def last_round(parity, step, left, lstate, far, relations, rel, index, keep):
    depth, rows = left.shape
    edges = index[0].shape[1]
    number = float(index[3].shape[1])
    edge = shape(depth, edges)
    pair16 = shape(2 * depth, edges, dtype=BF16)
    slab = shape(depth, rows)

    def run(body):
        def kernel(*refs):
            @on_parity(parity)
            def _():
                body(*refs)

        return kernel

    (weight, source, query, query_rows, left16, oh_src, oh_dst, count_l, count_r, kind) = call(
        run(functools.partial(prepare, step)), "last_prepare",
        [left, relations, *index], prepared_shapes(depth, rows, edges, relations.shape[0]),
    )
    target = gq = None
    rgrads = []
    at = 0
    for i, piece in enumerate(far):
        held = [] if i == 0 else [target, gq]

        def body(piece, query, query_rows, oh_dst, count_r, *rest, at=at, held=len(held)):
            take_piece(number, at, piece, query, query_rows, oh_dst, count_r, *rest[held:])

        target, gq, rgrad = call(
            run(body), "last_piece%d" % i,
            [piece, query, query_rows, oh_dst, count_r, *held],
            [edge, edge, shape(depth, piece.shape[1])],
            aliases={5 + k: k for k in range(len(held))},
        )
        rgrads.append(rgrad)
        at += piece.shape[1]

    def join_body(weight, source, target, gq, left16, count_l, kind, rel_in, lgrad, to_src, to_dst, rel_out, probe, probe_rows, gp):
        rel_out[...] = rel_in[...]

        @on_parity(parity)
        def _():
            join(number, weight, source, target, gq, left16, count_l, kind, rel_in,
                 probe, probe_rows, gp, lgrad, to_src, to_dst, rel_out)

    lgrad, to_src, to_dst, rel = call(
        join_body, "last_join",
        [weight, source, target, gq, left16, count_l, kind, rel],
        [slab, pair16, pair16, shape(*relations.shape)],
        scratch_shapes=scratch([shape(depth, edges, dtype=BF16), shape(edges, depth, dtype=BF16), edge]),
    )

    def update():
        count = len(far)

        def body(left, lstate, lgrad, to_src, to_dst, oh_src, oh_dst, *rest):
            pieces = rest[:count]
            grads = rest[count : 2 * count]
            left_out, right_out, spare, sems = rest[2 * count + 2 :]
            states = [piece.at[depth : depth + 1] for piece in pieces]
            finish_last(left, lstate, pieces, states, lgrad, grads, to_src, to_dst, oh_src, oh_dst, spare, left_out, right_out, sems)

        operands = [left, lstate, lgrad, to_src, to_dst, oh_src, oh_dst, *far, *rgrads, *keep]
        places = (len(operands) - 2, len(operands) - 1)
        return call(
            run(body), "last_update", operands, [slab, slab], in_large=places, out_large=(0, 1),
            scratch_shapes=[pltpu.VMEM((1, rows), F32), pltpu.SemaphoreType.DMA((2, rows // STEP))],
            aliases={places[0]: 0, places[1]: 1},
        )

    return rel, update


def local(
    left_slab, left_state, right_slab, right_state, relations, relation_state,
    src_index, dst_index, relation_id, neg_source, neg_target,
):
    peers = lax.axis_size("blk")
    inside = [(i, i + 1) for i in range(0, peers, 2)]
    swap = inside + [(i + 1, i) for i in range(0, peers, 2)]
    across = [(i, (i + 1) % peers) for i in range(1, peers, 2)]
    skip = [(i, (i + 2) % peers) for i in range(0, peers, 2)]
    index = (src_index, dst_index, relation_id, neg_source, neg_target)
    left = left_slab.T
    right = right_slab.T
    rows = left.shape[1]
    lstate = left_state.reshape(1, rows)
    right_far = lax.ppermute(right, "blk", across)
    right_near = lax.ppermute(right, "blk", inside)
    state_near = lax.ppermute(right_state, "blk", swap)
    state_far = lax.ppermute(state_near, "blk", skip).reshape(1, rows)
    state_near = state_near.reshape(1, rows)
    rel = jnp.zeros(relations.shape, F32)
    left_a, lstate, far, rel = trained(1, 0, FAR, left, lstate, [right_near], state_near, relations, rel, index)
    far = [lax.ppermute(piece, "blk", across) for piece in far]
    left_a, lstate, near, rel = trained(
        0, 0, NEAR, left, lstate, [right_far], state_far, relations, rel, index, (left_a,)
    )
    near = [lax.ppermute(piece, "blk", inside) for piece in near]
    left_b, lstate, right_b, rel = trained(1, 1, (), left_a, lstate, near, state_near, relations, rel, index)
    rel, update = last_round(0, 1, left_a, lstate, far, relations, rel, index, (left_b, *right_b))
    if lax.axis_size("rel") == 2:
        rel = rel + lax.ppermute(rel, "rel", [(0, 1), (1, 0)])
    else:
        rel = lax.psum(rel, "rel")
    left_b, right_b = update()
    new_rstate = relation_state + jnp.mean(rel * rel, axis=1)
    relations_out = relations - rate * rel / jnp.sqrt(new_rstate)[:, None]
    return (left_b.T, right_b.T, relations_out[None])


def solution(mesh):
    in_specs = (
        P(("blk", "rel"), None),
        P(("blk", "rel")),
        P(("blk", "rel"), None),
        P(("blk", "rel")),
        P(),
        P(),
        P(None, ("blk", "rel")),
        P(None, ("blk", "rel")),
        P(None, ("blk", "rel")),
        P(None, ("blk", "rel")),
        P(None, ("blk", "rel")),
    )
    out_specs = (P(("blk", "rel"), None), P(("blk", "rel"), None), P("blk", None, None))
    return jax.shard_map(local, mesh=mesh, in_specs=in_specs, out_specs=out_specs, check_vma=False)
```

profile of v0, /device:TPU:0, one launch (start us, length us, event | category | flops | bytes accessed | tf_op | source)
XLA Modules:
  0.0 107.4 jit_solution(15276035553671358222)
XLA Ops:
  0.6 2.6 %collective-permute-start.1 = (f32[400,2048]{1,0:T(8,128)}, f32[400,2048]{1,0:T(8,128)S(1)}, u32[]{:S(2)}, u32[]{:S(2)}) collective-permute-start(f32[400,2048]{1,0:T(8,128)} %bitcast.17), channel_id=1, source_target_pairs={{0,2},{4,6},{8,10},{12,14},{16,18},{20,22},{24,26},{28,30},{1,3},{... | collective-permute-start | bytes 9830408 | tf_op jit(solution)/shard_map/ppermute | solution.py:388
  3.2 1.3 %collective-permute-start.3 = (f32[400,2048]{1,0:T(8,128)}, f32[400,2048]{1,0:T(8,128)S(1)}, u32[]{:S(2)}, u32[]{:S(2)}) collective-permute-start(f32[400,2048]{1,0:T(8,128)} %bitcast.18), channel_id=1, source_target_pairs={{2,4},{6,8},{10,12},{14,16},{18,20},{22,24},{26,28},{30,0},{3,5},{... | collective-permute-start | bytes 9830408 | tf_op jit(solution)/shard_map/ppermute | solution.py:387
  4.5 3.3 %collective-permute-start = (f32[2048]{0:T(1024)}, f32[2048]{0:T(1024)S(1)}, u32[]{:S(2)}, u32[]{:S(2)}) collective-permute-start(f32[2048]{0:T(1024)} %param.14), channel_id=1, source_target_pairs={{0,2},{4,6},{8,10},{12,14},{16,18},{20,22},{24,26},{28,30},{2,0},{... | collective-permute-start | bytes 24584 | tf_op jit(solution)/shard_map/ppermute | solution.py:389
  7.8 1.0 collective-permute-done
  8.9 0.0 collective-permute-done.1.refs_10_
  8.9 0.0 copy-start
  8.9 1.9 %copy-done = f32[2048,400]{0,1:T(8,128)S(1)} copy-done((f32[2048,400]{0,1:T(8,128)S(1)}, f32[2048,400]{0,1:T(8,128)}, u32[]{:S(2)}) %copy-start) | copy-done | bytes 3276824
  10.8 0.0 copy-start.1
  10.8 0.8 copy-done.1
  11.6 0.0 copy-start.3
  11.6 0.7 copy-done.3
  12.3 0.0 copy-start.5
  12.3 0.7 copy-done.5
  13.0 0.0 copy-start.6
  13.0 0.7 copy-done.6
  13.7 0.0 copy-start.7
  13.7 0.7 copy-done.7
  14.4 0.0 copy-start.8
  14.4 0.7 copy-done.8
  15.1 0.0 copy-start.9
  15.1 0.7 copy-done.9
  15.8 0.0 copy-start.2
  15.8 0.2 round0_parity1.1
  16.0 1.3 %collective-permute-start.8 = (f32[408,1280]{1,0:T(8,128)S(1)}, f32[408,1280]{1,0:T(8,128)S(1)}, u32[]{:S(2)}, u32[]{:S(2)}) collective-permute-start(f32[408,1280]{1,0:T(8,128)S(1)} %get-tuple-element.60), channel_id=1, source_target_pairs={{2,4},{6,8},{10,12},{14,16},{18,20},{22,24},{26,28},{30,0},{3,5},{... | collective-permute-start | bytes 6266888 | tf_op jit(solution)/shard_map/ppermute | solution.py:394
  17.3 4.0 %collective-permute-start.2 = (f32[2048]{0:T(1024)S(1)}, f32[2048]{0:T(1024)S(1)}, u32[]{:S(2)}, u32[]{:S(2)}) collective-permute-start(f32[2048]{0:T(1024)S(1)} %collective-permute-done), channel_id=1, source_target_pairs={{0,4},{4,8},{8,12},{12,16},{16,20},{20,24},{24,28},{28,0},{1,5},{5... | collective-permute-start | bytes 24584 | tf_op jit(solution)/shard_map/ppermute | solution.py:390
  21.3 4.8 %collective-permute-done.2 = f32[2048]{0:T(1024)S(1)} collective-permute-done((f32[2048]{0:T(1024)S(1)}, f32[2048]{0:T(1024)S(1)}, u32[]{:S(2)}, u32[]{:S(2)}) %collective-permute-start.2) | collective-permute-done | bytes 8224 | tf_op jit(solution)/shard_map/ppermute | solution.py:390
  26.1 20.1 %collective-permute-done.3.refs_10_ = f32[400,2048]{1,0:T(8,128)S(1)} collective-permute-done((f32[400,2048]{1,0:T(8,128)}, f32[400,2048]{1,0:T(8,128)S(1)}, u32[]{:S(2)}, u32[]{:S(2)}) %collective-permute-start.3) | collective-permute-done | bytes 3276832 | tf_op jit(solution)/shard_map/ppermute | solution.py:387
  46.2 0.0 copy-done.2
  46.2 21.1 %round0_parity0.1 = (f32[400,2048]{1,0:T(8,128)S(1)}, f32[1,2048]{1,0:T(1,128)S(1)}, f32[32,400]{1,0:T(8,128)S(1)}, f32[408,1024]{1,0:T(8,128)S(1)}, f32[408,1024]{1,0:T(8,128)S(1)}) custom-call(f32[400,2048]{1,0:T(8,128)S(1)} %bitcast.10, f32[1,2048]{1,0:T(1,128)S(1)} %get-tuple-element.43.refs_1_, ...), custom_call_target="tpu_custom_call", output_to_operand_aliasing={{0}: (11, {})} | custom-call | flops 1000000 | bytes 100000 | tf_op jit(solution)/shard_map/round0_parity0/pallas_call | solution.py:259
  67.3 0.0 copy-start.4
  67.3 1.4 %collective-permute-start.4 = (f32[408,1024]{1,0:T(8,128)S(1)}, f32[408,1024]{1,0:T(8,128)S(1)}, u32[]{:S(2)}, u32[]{:S(2)}) collective-permute-start(f32[408,1024]{1,0:T(8,128)S(1)} %get-tuple-element.49), channel_id=1, source_target_pairs={{0,2},{4,6},{8,10},{12,14},{16,18},{20,22},{24,26},{28,30},{1,3},{... | collective-permute-start | bytes 5013512 | tf_op jit(solution)/shard_map/ppermute | solution.py:398
  68.7 1.4 %collective-permute-start.5 = (f32[408,1024]{1,0:T(8,128)S(1)}, f32[408,1024]{1,0:T(8,128)S(1)}, u32[]{:S(2)}, u32[]{:S(2)}) collective-permute-start(f32[408,1024]{1,0:T(8,128)S(1)} %get-tuple-element.50), channel_id=1, source_target_pairs={{0,2},{4,6},{8,10},{12,14},{16,18},{20,22},{24,26},{28,30},{1,3},{... | collective-permute-start | bytes 5013512 | tf_op jit(solution)/shard_map/ppermute | solution.py:398
  70.1 1.3 %collective-permute-start.7 = (f32[408,512]{1,0:T(8,128)S(1)}, f32[408,512]{1,0:T(8,128)S(1)}, u32[]{:S(2)}, u32[]{:S(2)}) collective-permute-start(f32[408,512]{1,0:T(8,128)S(1)} %get-tuple-element.59), channel_id=1, source_target_pairs={{2,4},{6,8},{10,12},{14,16},{18,20},{22,24},{26,28},{30,0},{3,5},{... | collective-permute-start | bytes 2506760 | tf_op jit(solution)/shard_map/ppermute | solution.py:394
  71.4 1.3 %collective-permute-start.6 = (f32[408,256]{1,0:T(8,128)S(1)}, f32[408,256]{1,0:T(8,128)S(1)}, u32[]{:S(2)}, u32[]{:S(2)}) collective-permute-start(f32[408,256]{1,0:T(8,128)S(1)} %get-tuple-element.54), channel_id=1, source_target_pairs={{2,4},{6,8},{10,12},{14,16},{18,20},{22,24},{26,28},{30,0},{3,5},{... | collective-permute-start | bytes 1253384 | tf_op jit(solution)/shard_map/ppermute | solution.py:394
  72.7 4.4 %last_prepare.1 = (f32[400,256]{1,0:T(8,128)S(1)}, f32[400,256]{1,0:T(8,128)S(1)}, bf16[400,256]{1,0:T(8,128)(2,1)S(1)}, bf16[256,400]{1,0:T(8,128)(2,1)S(1)}, b...) custom-call(f32[400,2048]{1,0:T(8,128)S(1)} %get-tuple-element.46.re, ...), custom_call_target="tpu_custom_call" | custom-call | flops 1000000 | bytes 100000 | tf_op jit(solution)/shard_map/last_prepare/pallas_call | solution.py:259
  77.2 0.0 collective-permute-done.4.refs_10_
  77.2 0.0 collective-permute-done.5.refs_11_
  77.2 0.0 copy-done.4
  77.2 0.3 round1_parity1.1
  77.6 0.0 collective-permute-done.8.refs_0_.refs_7_
  77.6 3.3 %last_piece0.1 = (f32[400,256]{1,0:T(8,128)S(1)}, f32[400,256]{1,0:T(8,128)S(1)}, f32[400,1280]{1,0:T(8,128)S(1)}) custom-call(f32[408,1280]{1,0:T(8,128)S(1)} %collective-permute-done.8.refs_0_.refs_7_, bf16[400,256]{1,0:T(8,128)(2,1)S(1)} %get-tuple-element.55.refs_1_, bf16[256,400]{1,0:T(8,128)(2,1)S(1)} %get-tuple-element.56.refs_2_, ...), custom_call_target="tpu_custom_call" | custom-call | flops 1000000 | bytes 100000 | tf_op jit(solution)/shard_map/last_piece0/pallas_call | solution.py:259
  80.8 5.8 %collective-permute-done.7.refs_0_.refs_8_ = f32[408,512]{1,0:T(8,128)S(1)} collective-permute-done((f32[408,512]{1,0:T(8,128)S(1)}, f32[408,512]{1,0:T(8,128)S(1)}, u32[]{:S(2)}, u32[]{:S(2)}) %collective-permute-start.7) | collective-permute-done | bytes 835616 | tf_op jit(solution)/shard_map/ppermute | solution.py:394
  86.7 1.3 %last_piece1.1 = (f32[400,256]{1,0:T(8,128)S(1)}, f32[400,256]{1,0:T(8,128)S(1)}, f32[400,512]{1,0:T(8,128)S(1)}) custom-call(f32[408,512]{1,0:T(8,128)S(1)} %collective-permute-done.7.refs_0_.refs_8_, bf16[400,256]{1,0:T(8,128)(2,1)S(1)} %get-tuple-element.55.refs_1_, ...), custom_call_target="tpu_custom_call", output_to_operand_aliasing={{0}: (5, {}), {1}: (6, {})} | custom-call | flops 1000000 | bytes 100000 | tf_op jit(solution)/shard_map/last_piece1/pallas_call | solution.py:259
  87.9 3.2 %collective-permute-done.6.refs_0_.refs_9_ = f32[408,256]{1,0:T(8,128)S(1)} collective-permute-done((f32[408,256]{1,0:T(8,128)S(1)}, f32[408,256]{1,0:T(8,128)S(1)}, u32[]{:S(2)}, u32[]{:S(2)}) %collective-permute-start.6) | collective-permute-done | bytes 417824 | tf_op jit(solution)/shard_map/ppermute | solution.py:394
  91.1 0.6 last_piece2.1
  91.8 5.6 %last_join.1 = (f32[400,2048]{1,0:T(8,128)S(1)}, bf16[800,256]{1,0:T(8,128)(2,1)S(1)}, bf16[800,256]{1,0:T(8,128)(2,1)S(1)}, f32[32,400]{1,0:T(8,128)S(1)}) custom-call(f32[400,256]{1,0:T(8,128)S(1)} %get-tuple-element.52.weight, f32[400,256]{1,0:T(8,128)S(1)} %get-tuple-element.53.source, f32[400,256]{1,0:T(8,128)S(1)} %get-tuple-element.65.target, ...), custom_call_target="tpu_custom_call" | custom-call | flops 1000000 | bytes 100000 | tf_op jit(solution)/shard_map/last_join/pallas_call | solution.py:259
  97.4 2.4 %collective-permute-start.9 = (f32[32,400]{1,0:T(8,128)S(1)}, f32[32,400]{1,0:T(8,128)S(1)}, u32[]{:S(2)}, u32[]{:S(2)}) collective-permute-start(f32[32,400]{1,0:T(8,128)S(1)} %get-tuple-element.82), channel_id=1, source_target_pairs={{0,1},{1,0},{2,3},{3,2},{4,5},{5,4},{6,7},{7,6},{8,9},{9,8},{10,11... | collective-permute-start | bytes 153608 | tf_op jit(solution)/shard_map/ppermute | solution.py:402
  99.9 0.0 copy-start.10
  99.9 6.7 %last_update.1 = (f32[400,2048]{1,0:T(8,128)}, f32[400,2048]{1,0:T(8,128)}) custom-call(f32[400,2048]{1,0:T(8,128)S(1)} %get-tuple-element.46.refs_0_, f32[1,2048]{1,0:T(1,128)S(1)} %get-tuple-element.51.refs_1_, f32[400,2048]{1,0:T(8,128)S(1)} %get-tuple-element.71.refs_2_, ...), custom_call_target="tpu_custom_call", output_to_operand_aliasing={{0}: (13, {}), {1}: (14, {})} | custom-call | flops 1000000 | bytes 100000 | tf_op jit(solution)/shard_map/last_update/pallas_call | solution.py:259
  106.5 0.0 collective-permute-done.9
  106.5 0.1 multiply_reduce_fusion
  106.7 0.0 copy-done.10
  106.7 0.7 subtract_bitcast_fusion
  (2 shorter events, 0.0 us)
Async XLA Ops:
  0.6 8.2 %collective-permute-start.1 = (f32[400,2048]{1,0:T(8,128)}, f32[400,2048]{1,0:T(8,128)S(1)}, u32[]{:S(2)}, u32[]{:S(2)}) collective-permute-start(f32[400,2048]{1,0:T(8,128)} %bitcast.17), channel_id=1, source_target_pairs={{0,2},{4,6},{8,10},{12,14},{16,18},{20,22},{24,26},{28,30},{1,3},{... | collective-permute-start | bytes 9830408 | tf_op jit(solution)/shard_map/ppermute | solution.py:388
  3.2 43.0 %collective-permute-start.3 = (f32[400,2048]{1,0:T(8,128)}, f32[400,2048]{1,0:T(8,128)S(1)}, u32[]{:S(2)}, u32[]{:S(2)}) collective-permute-start(f32[400,2048]{1,0:T(8,128)} %bitcast.18), channel_id=1, source_target_pairs={{2,4},{6,8},{10,12},{14,16},{18,20},{22,24},{26,28},{30,0},{3,5},{... | collective-permute-start | bytes 9830408 | tf_op jit(solution)/shard_map/ppermute | solution.py:387
  4.5 4.4 %collective-permute-start = (f32[2048]{0:T(1024)}, f32[2048]{0:T(1024)S(1)}, u32[]{:S(2)}, u32[]{:S(2)}) collective-permute-start(f32[2048]{0:T(1024)} %param.14), channel_id=1, source_target_pairs={{0,2},{4,6},{8,10},{12,14},{16,18},{20,22},{24,26},{28,30},{2,0},{... | collective-permute-start | bytes 24584 | tf_op jit(solution)/shard_map/ppermute | solution.py:389
  8.9 1.9 %copy-start = (f32[2048,400]{0,1:T(8,128)S(1)}, f32[2048,400]{0,1:T(8,128)}, u32[]{:S(2)}) copy-start(f32[2048,400]{0,1:T(8,128)} %param.11) | copy-start | bytes 9830404
  10.8 0.8 copy-start.1
  11.6 0.7 copy-start.3
  12.3 0.7 copy-start.5
  13.0 0.7 copy-start.6
  13.7 0.7 copy-start.7
  14.4 0.7 copy-start.8
  15.1 0.7 copy-start.9
  15.8 30.4 %copy-start.2 = (f32[32,400]{1,0:T(8,128)S(1)}, f32[32,400]{1,0:T(8,128)}, u32[]{:S(2)}) copy-start(f32[32,400]{1,0:T(8,128)} %refs_1_.1) | copy-start | bytes 153604
  16.0 61.6 %collective-permute-start.8 = (f32[408,1280]{1,0:T(8,128)S(1)}, f32[408,1280]{1,0:T(8,128)S(1)}, u32[]{:S(2)}, u32[]{:S(2)}) collective-permute-start(f32[408,1280]{1,0:T(8,128)S(1)} %get-tuple-element.60), channel_id=1, source_target_pairs={{2,4},{6,8},{10,12},{14,16},{18,20},{22,24},{26,28},{30,0},{3,5},{... | collective-permute-start | bytes 6266888 | tf_op jit(solution)/shard_map/ppermute | solution.py:394
  17.3 8.8 %collective-permute-start.2 = (f32[2048]{0:T(1024)S(1)}, f32[2048]{0:T(1024)S(1)}, u32[]{:S(2)}, u32[]{:S(2)}) collective-permute-start(f32[2048]{0:T(1024)S(1)} %collective-permute-done), channel_id=1, source_target_pairs={{0,4},{4,8},{8,12},{12,16},{16,20},{20,24},{24,28},{28,0},{1,5},{5... | collective-permute-start | bytes 24584 | tf_op jit(solution)/shard_map/ppermute | solution.py:390
  67.3 9.9 %copy-start.4 = (s32[2,1000]{1,0:T(2,128)S(1)}, s32[2,1000]{1,0:T(2,128)}, u32[]{:S(2)}) copy-start(s32[2,1000]{1,0:T(2,128)} %refs_5_.7) | copy-start | bytes 24004
  67.3 9.8 %collective-permute-start.4 = (f32[408,1024]{1,0:T(8,128)S(1)}, f32[408,1024]{1,0:T(8,128)S(1)}, u32[]{:S(2)}, u32[]{:S(2)}) collective-permute-start(f32[408,1024]{1,0:T(8,128)S(1)} %get-tuple-element.49), channel_id=1, source_target_pairs={{0,2},{4,6},{8,10},{12,14},{16,18},{20,22},{24,26},{28,30},{1,3},{... | collective-permute-start | bytes 5013512 | tf_op jit(solution)/shard_map/ppermute | solution.py:398
  68.7 8.5 %collective-permute-start.5 = (f32[408,1024]{1,0:T(8,128)S(1)}, f32[408,1024]{1,0:T(8,128)S(1)}, u32[]{:S(2)}, u32[]{:S(2)}) collective-permute-start(f32[408,1024]{1,0:T(8,128)S(1)} %get-tuple-element.50), channel_id=1, source_target_pairs={{0,2},{4,6},{8,10},{12,14},{16,18},{20,22},{24,26},{28,30},{1,3},{... | collective-permute-start | bytes 5013512 | tf_op jit(solution)/shard_map/ppermute | solution.py:398
  70.1 16.5 %collective-permute-start.7 = (f32[408,512]{1,0:T(8,128)S(1)}, f32[408,512]{1,0:T(8,128)S(1)}, u32[]{:S(2)}, u32[]{:S(2)}) collective-permute-start(f32[408,512]{1,0:T(8,128)S(1)} %get-tuple-element.59), channel_id=1, source_target_pairs={{2,4},{6,8},{10,12},{14,16},{18,20},{22,24},{26,28},{30,0},{3,5},{... | collective-permute-start | bytes 2506760 | tf_op jit(solution)/shard_map/ppermute | solution.py:394
  71.4 19.7 %collective-permute-start.6 = (f32[408,256]{1,0:T(8,128)S(1)}, f32[408,256]{1,0:T(8,128)S(1)}, u32[]{:S(2)}, u32[]{:S(2)}) collective-permute-start(f32[408,256]{1,0:T(8,128)S(1)} %get-tuple-element.54), channel_id=1, source_target_pairs={{2,4},{6,8},{10,12},{14,16},{18,20},{22,24},{26,28},{30,0},{3,5},{... | collective-permute-start | bytes 1253384 | tf_op jit(solution)/shard_map/ppermute | solution.py:394
  97.4 9.1 %collective-permute-start.9 = (f32[32,400]{1,0:T(8,128)S(1)}, f32[32,400]{1,0:T(8,128)S(1)}, u32[]{:S(2)}, u32[]{:S(2)}) collective-permute-start(f32[32,400]{1,0:T(8,128)S(1)} %get-tuple-element.82), channel_id=1, source_target_pairs={{0,1},{1,0},{2,3},{3,2},{4,5},{5,4},{6,7},{7,6},{8,9},{9,8},{10,11... | collective-permute-start | bytes 153608 | tf_op jit(solution)/shard_map/ppermute | solution.py:402
  99.9 6.8 %copy-start.10 = (f32[32]{0:T(128)S(1)}, f32[32]{0:T(128)}, u32[]{:S(2)}) copy-start(f32[32]{0:T(128)} %param.16) | copy-start | bytes 388
where the time goes:
time: 108 us; the launch traced here: 107 us
  Pallas kernels  43.5 us (40%)
  waiting for transfers between devices  35 us (32%)
  starting transfers between devices  20.3 us (19%)
  local copies, waits for them, and re-layouts  6.91 us (6%)
    pallas_call x9, Pallas kernels, call(): pl.pallas_call(kernel, out_shape=tuple(shapes), in_specs=[large if i in i...  43.5 us
    ppermute x1, waiting for transfers between devices, local(): right_far = lax.ppermute(right, 'blk', across)  20.1 us
    ppermute x3, waiting for transfers between devices, local(): far = [lax.ppermute(piece, 'blk', across) for piece in far]  9.04 us
    unnamed x22, local copies, waits for them, and re-layouts  6.91 us
    ppermute x1, waiting for transfers between devices, local(): state_far = lax.ppermute(state_near, 'blk', skip).reshape(1, rows)  4.8 us
    ppermute x1, starting transfers between devices, local(): state_far = lax.ppermute(state_near, 'blk', skip).reshape(1, rows)  4.04 us
    ppermute x3, starting transfers between devices, local(): far = [lax.ppermute(piece, 'blk', across) for piece in far]  3.88 us
    ppermute x1, starting transfers between devices, local(): state_near = lax.ppermute(right_state, 'blk', swap)  3.32 us
  transfers between devices with their start and end apart: 10, of which 5 were waited for; matrix products, arithmetic and copies ran while one was open for 0% of the time, Pallas kernels for 35%

commit v1 on v0

--- a/solution.py
+++ b/solution.py
@@ -11,9 +11,9 @@
 F32 = jnp.float32
 BF16 = jnp.bfloat16
 LANES = 128
-STEP = 256
 NEAR = (4, 4)
-FAR = (5, 2, 1)
+NEAR_FIRST = (4, 4)
+FAR = (6, 1, 1)
 VMEM_LIMIT = 30 * 2**20
 
 NN = (((1,), (0,)), ((), ()))
@@ -38,6 +38,10 @@
     return pl.ds(pl.multiple_of(i * size, size), size)
 
 
+def step_of(rows):
+    return 512 if rows % 512 == 0 else 256
+
+
 def row_onehot(idx, table):
     count, rows = table.shape
     col = jnp.broadcast_to(idx, (LANES, count)).T
@@ -60,8 +64,8 @@
     return mul(high_hit, low_hit, NT)
 
 
-def times_at(counts, i):
-    tiles = STEP // LANES
+def times_at(counts, i, size):
+    tiles = size // LANES
     return jnp.concatenate([counts[pl.ds(i * tiles + t, 1), :] for t in range(tiles)], axis=1)
 
 
@@ -89,14 +93,16 @@
     weight[...] = sum(mul(part, kind[...], TN) for part in split(relations[...], 3))
     source[...] = jnp.zeros_like(source)
 
+    size = step_of(rows)
+
     def part(i, carry):
-        cut = lanes_at(i, STEP)
+        cut = lanes_at(i, size)
         parts = split(left[:, cut], 3)
         left16[:, cut] = parts[0]
         source[...] += sum(mul(p, oh_src[:, cut], NT) for p in parts)
         return carry
 
-    lax.fori_loop(0, rows // STEP, part, 0)
+    lax.fori_loop(0, rows // size, part, 0)
     product = source[...] * weight[...]
     query[...] = product.astype(BF16)
     query_rows[...] = half_rows(product.astype(BF16).astype(F32))
@@ -108,17 +114,19 @@
         target[...] = jnp.zeros_like(target)
         gq[...] = jnp.zeros_like(gq)
 
+    size = step_of(piece.shape[1])
+
     def part(i, carry):
-        cut = lanes_at(i, STEP)
+        cut = lanes_at(i, size)
         parts = split(piece[0:depth, cut], 3)
-        hits = oh_dst[:, lanes_at(i + start // STEP, STEP)]
+        hits = oh_dst[:, lanes_at(i + start // size, size)]
         target[...] += sum(mul(p, hits, NT) for p in parts)
-        times = times_at(count_r, i + start // STEP)
+        times = times_at(count_r, i + start // size, size)
         rgrad[:, cut], more = negatives(parts[0], query[...], query_rows[...], times, number)
         gq[...] += more
         return carry
 
-    lax.fori_loop(0, piece.shape[1] // STEP, part, 0)
+    lax.fori_loop(0, piece.shape[1] // size, part, 0)
 
 
 def join(number, weight, source, target, gq, left16, count_l, kind, rel_in, probe, probe_rows, gp, lgrad, to_src, to_dst, rel_out):
@@ -128,13 +136,15 @@
     probe_rows[...] = half_rows(product.astype(BF16).astype(F32))
     gp[...] = jnp.zeros_like(gp)
 
+    size = step_of(rows)
+
     def part(i, carry):
-        cut = lanes_at(i, STEP)
-        lgrad[:, cut], more = negatives(left16[:, cut], probe[...], probe_rows[...], times_at(count_l, i), number)
+        cut = lanes_at(i, size)
+        lgrad[:, cut], more = negatives(left16[:, cut], probe[...], probe_rows[...], times_at(count_l, i, size), number)
         gp[...] += more
         return carry
 
-    lax.fori_loop(0, rows // STEP, part, 0)
+    lax.fori_loop(0, rows // size, part, 0)
     depth = weight.shape[0]
     w, s, t = weight[...], source[...], target[...]
     coef = -jax.nn.sigmoid(-jnp.sum(s * w * t, axis=0, keepdims=True))
@@ -146,10 +156,11 @@
 
 def adagrad(slab, state, grad, edges, table, start, out, new_state, send=None):
     depth = grad.shape[0]
+    size = step_of(grad.shape[1])
 
     def part(i, carry):
-        cut = lanes_at(i, STEP)
-        hits = table[:, lanes_at(i + start // STEP, STEP)]
+        cut = lanes_at(i, size)
+        hits = table[:, lanes_at(i + start // size, size)]
         g = grad[:, cut] + mul(edges[0:depth, :], hits, NN) + mul(edges[depth:, :], hits, NN)
         new = state[:, cut] + jnp.sum(g * g, axis=0, keepdims=True) * (1.0 / depth)
         new_state[:, cut] = new
@@ -158,14 +169,16 @@
             send(i).start()
         return carry
 
-    lax.fori_loop(0, grad.shape[1] // STEP, part, 0)
+    lax.fori_loop(0, grad.shape[1] // size, part, 0)
 
 
 def sender(result, to, start, sems):
+    size = step_of(result.shape[1])
+
     def copy(i):
-        here = lanes_at(i, STEP)
-        there = lanes_at(i + start // STEP, STEP)
-        return pltpu.make_async_copy(result.at[:, here], to.at[:, there], sems.at[i + start // STEP])
+        here = lanes_at(i, size)
+        there = lanes_at(i + start // size, size)
+        return pltpu.make_async_copy(result.at[:, here], to.at[:, there], sems.at[i + start // size])
 
     return copy
 
@@ -184,11 +197,11 @@
     for piece, state, grad in zip(right, rstate, rgrads):
         copy = sender(grad, right_out, start, sems.at[0])
         adagrad(piece, state, grad, to_dst, oh_dst, start, grad, spare, copy)
-        sent.append((copy, piece.shape[1] // STEP))
+        sent.append((copy, piece.shape[1] // step_of(piece.shape[1])))
         start += piece.shape[1]
     copy = sender(lgrad, left_out, 0, sems.at[1])
     adagrad(left, lstate, lgrad, to_src, oh_src, 0, lgrad, spare, copy)
-    sent.append((copy, left.shape[1] // STEP))
+    sent.append((copy, left.shape[1] // step_of(left.shape[1])))
     for copy, count in sent:
         wait_all(copy, count)
 
@@ -202,23 +215,32 @@
     return [(sum(sizes[:i]), size) for i, size in enumerate(sizes)]
 
 
-def train(parity, step, number, last, kept, takes, gives, *refs):
+def rows_of(pieces, at, size):
+    found = []
+    start = 0
+    for piece in pieces:
+        begin, end = max(at, start), min(at + size, start + piece.shape[1])
+        if begin < end:
+            found.append((piece.at[:, begin - start : end - start], begin, end - begin))
+        start += piece.shape[1]
+    return found
+
+
+def train(parity, number, last, kept, takes, gives, *refs):
     refs = list(refs)
-    (left, lstate, rstate_in, relations, rel_in, src, dst, rid, nsrc, ndst) = refs[:10]
-    right = refs[10 : 10 + takes]
-    refs = refs[10 + takes + kept :]
+    (left, lstate, rstate_in, rel_in) = refs[:4]
+    (weight, source, query, query_rows, left16, oh_src, oh_dst, count_l, count_r, kind) = refs[4:14]
+    right = refs[14 : 14 + takes]
+    refs = refs[14 + takes + kept :]
     left_out, lstate_out, rel_out = refs[:3]
     right_out = refs[3 : 3 + len(gives)]
-    (weight, source, query, query_rows, left16, oh_src, oh_dst, count_l, count_r, kind,
-     target, gq, rgrad, probe, probe_rows, gp, lgrad, to_src, to_dst, spare, sems) = refs[3 + len(gives) :]
+    (target, gq, rgrad, probe, probe_rows, gp, lgrad, to_src, to_dst, spare, sems) = refs[3 + len(gives) :]
     depth, rows = left.shape
     lstate_out[...] = lstate[...]
     rel_out[...] = rel_in[...]
 
     @on_parity(parity)
     def _():
-        prepare(step, left, relations, src, dst, rid, nsrc, ndst,
-                weight, source, query, query_rows, left16, oh_src, oh_dst, count_l, count_r, kind)
         grads = []
         at = 0
         for piece in right:
@@ -231,8 +253,10 @@
             finish_last(left, lstate, right, states, lgrad, grads, to_src, to_dst, oh_src, oh_dst, spare, left_out, right_out[0], sems)
         else:
             for (at, size), out in zip(pieces_of(rows, gives), right_out):
-                cut = slice(at, at + size)
-                adagrad(right[0].at[:, cut], rstate_in.at[:, cut], rgrad.at[:, cut], to_dst, oh_dst, at, out, spare)
+                for old, begin, length in rows_of(right, at, size):
+                    cut = slice(begin, begin + length)
+                    here = slice(begin - at, begin - at + length)
+                    adagrad(old, rstate_in.at[:, cut], rgrad.at[:, cut], to_dst, oh_dst, begin, out.at[:, here], spare.at[:, here])
                 out[depth : depth + 8, :] = jnp.broadcast_to(spare[:, 0:size], (8, size))
             adagrad(left, lstate, lgrad, to_src, oh_src, 0, left_out, lstate_out)
 
@@ -269,10 +293,17 @@
     )(*operands)
 
 
-def trained(parity, step, gives, left, lstate, right, rstate, relations, rel, index, keep=()):
+def prepared(step, left, relations, index):
     depth, rows = left.shape
-    edges = index[0].shape[1]
-    number = float(index[3].shape[1])
+    return call(
+        functools.partial(prepare, step), "prepare%d" % step, [left, relations, *index],
+        prepared_shapes(depth, rows, index[0].shape[1], relations.shape[0]),
+    )
+
+
+def trained(parity, name, number, gives, left, lstate, right, rstate, rel, ready, keep=()):
+    depth, rows = left.shape
+    edges = ready[0].shape[1]
     last = not gives
     blocks = [shape(depth + 8, size) for _at, size in pieces_of(rows, gives)] or [shape(depth, rows)]
     edge = shape(depth, edges)
@@ -281,25 +312,21 @@
     slab = shape(depth, rows)
     inner = [edge, edge, slab, edge16, shape(edges, depth, dtype=BF16), edge, slab, pair16, pair16, shape(1, rows)]
     left_out, lstate_out, rel_out, *right_out = call(
-        functools.partial(train, parity, step, number, last, len(keep), len(right), gives or (8,)),
-        "round%d_parity%d" % (step, parity),
-        [left, lstate, rstate, relations, rel, *index, *right, *keep],
-        [slab, shape(1, rows), shape(*relations.shape), *blocks],
+        functools.partial(train, parity, number, last, len(keep), len(right), gives or (8,)),
+        name,
+        [left, lstate, rstate, rel, *ready, *right, *keep],
+        [slab, shape(1, rows), shape(*rel.shape), *blocks],
         out_large=(0, 3) if last else (),
-        scratch_shapes=[
-            *scratch(prepared_shapes(depth, rows, edges, relations.shape[0])),
-            *scratch(inner),
-            pltpu.SemaphoreType.DMA((2, rows // STEP)),
-        ],
-        aliases={10 + len(right) + i: 0 for i in range(len(keep))},
+        scratch_shapes=[*scratch(inner), pltpu.SemaphoreType.DMA((2, rows // 256))],
+        aliases={14 + len(right) + i: 0 for i in range(len(keep))},
     )
     return left_out, lstate_out, right_out, rel_out
 
 
-def last_round(parity, step, left, lstate, far, relations, rel, index, keep):
+def last_round(parity, number, left, lstate, far, rel, ready, keep):
     depth, rows = left.shape
-    edges = index[0].shape[1]
-    number = float(index[3].shape[1])
+    (weight, source, query, query_rows, left16, oh_src, oh_dst, count_l, count_r, kind) = ready
+    edges = weight.shape[1]
     edge = shape(depth, edges)
     pair16 = shape(2 * depth, edges, dtype=BF16)
     slab = shape(depth, rows)
@@ -312,10 +339,6 @@
 
         return kernel
 
-    (weight, source, query, query_rows, left16, oh_src, oh_dst, count_l, count_r, kind) = call(
-        run(functools.partial(prepare, step)), "last_prepare",
-        [left, relations, *index], prepared_shapes(depth, rows, edges, relations.shape[0]),
-    )
     target = gq = None
     rgrads = []
     at = 0
@@ -345,7 +368,7 @@
     lgrad, to_src, to_dst, rel = call(
         join_body, "last_join",
         [weight, source, target, gq, left16, count_l, kind, rel],
-        [slab, pair16, pair16, shape(*relations.shape)],
+        [slab, pair16, pair16, shape(*rel.shape)],
         scratch_shapes=scratch([shape(depth, edges, dtype=BF16), shape(edges, depth, dtype=BF16), edge]),
     )
 
@@ -363,7 +386,7 @@
         places = (len(operands) - 2, len(operands) - 1)
         return call(
             run(body), "last_update", operands, [slab, slab], in_large=places, out_large=(0, 1),
-            scratch_shapes=[pltpu.VMEM((1, rows), F32), pltpu.SemaphoreType.DMA((2, rows // STEP))],
+            scratch_shapes=[pltpu.VMEM((1, rows), F32), pltpu.SemaphoreType.DMA((2, rows // 256))],
             aliases={places[0]: 0, places[1]: 1},
         )
 
@@ -384,20 +407,23 @@
     right = right_slab.T
     rows = left.shape[1]
     lstate = left_state.reshape(1, rows)
+    number = float(neg_source.shape[1])
     right_far = lax.ppermute(right, "blk", across)
-    right_near = lax.ppermute(right, "blk", inside)
+    right_near = [lax.ppermute(right[:, at : at + size], "blk", inside) for at, size in pieces_of(rows, NEAR_FIRST)]
     state_near = lax.ppermute(right_state, "blk", swap)
     state_far = lax.ppermute(state_near, "blk", skip).reshape(1, rows)
     state_near = state_near.reshape(1, rows)
     rel = jnp.zeros(relations.shape, F32)
-    left_a, lstate, far, rel = trained(1, 0, FAR, left, lstate, [right_near], state_near, relations, rel, index)
+    ready = prepared(0, left, relations, index)
+    left_a, lstate, far, rel = trained(1, "first_near", number, FAR, left, lstate, right_near, state_near, rel, ready)
     far = [lax.ppermute(piece, "blk", across) for piece in far]
     left_a, lstate, near, rel = trained(
-        0, 0, NEAR, left, lstate, [right_far], state_far, relations, rel, index, (left_a,)
+        0, "first_far", number, NEAR, left, lstate, [right_far], state_far, rel, ready, (left_a,)
     )
     near = [lax.ppermute(piece, "blk", inside) for piece in near]
-    left_b, lstate, right_b, rel = trained(1, 1, (), left_a, lstate, near, state_near, relations, rel, index)
-    rel, update = last_round(0, 1, left_a, lstate, far, relations, rel, index, (left_b, *right_b))
+    ready = prepared(1, left_a, relations, index)
+    left_b, lstate, right_b, rel = trained(1, "last_near", number, (), left_a, lstate, near, state_near, rel, ready)
+    rel, update = last_round(0, number, left_a, lstate, far, rel, ready, (left_b, *right_b))
     if lax.axis_size("rel") == 2:
         rel = rel + lax.ppermute(rel, "rel", [(0, 1), (1, 0)])
     else:

time: 108 us -> 96.3 us (0.89)
  the two profiles are of different devices: /device:TPU:0 before, /device:TPU:1 now
where the time goes in v1:
time: 96.3 us; the launch traced here: 96 us
  Pallas kernels  35.6 us (37%)
  starting transfers between devices  34.6 us (36%)
  waiting for transfers between devices  21.6 us (22%)
  local copies, waits for them, and re-layouts  2.37 us (2%)
    pallas_call x10, Pallas kernels, call(): pl.pallas_call(kernel, out_shape=tuple(shapes), in_specs=[large if i in i...  35.6 us
    ppermute x3, starting transfers between devices, local(): far = [lax.ppermute(piece, 'blk', across) for piece in far]  21.1 us
    ppermute x1, waiting for transfers between devices, local(): right_far = lax.ppermute(right, 'blk', across)  9.97 us
    ppermute x3, waiting for transfers between devices, local(): far = [lax.ppermute(piece, 'blk', across) for piece in far]  9.75 us
    ppermute x1, starting transfers between devices, local(): right_far = lax.ppermute(right, 'blk', across)  4.98 us
    ppermute x2, starting transfers between devices, local(): lax.ppermute(right[:, at:at + size], 'blk', inside)  2.58 us
    ppermute x2, starting transfers between devices, local(): near = [lax.ppermute(piece, 'blk', inside) for piece in near]  2.58 us
    slice x1, local copies, waits for them, and re-layouts, local(): right[:, at:at + size]  2.32 us
  transfers between devices with their start and end apart: 11, of which 6 were waited for; matrix products, arithmetic and copies ran while one was open for 2% of the time, Pallas kernels for 22%

profile of v1, /device:TPU:1, one launch (start us, length us, event | category | flops | bytes accessed | tf_op | source)
XLA Modules:
  0.0 96.0 jit_solution(9926211399777627360)
XLA Ops:
  0.6 0.0 copy-start.8
  0.6 0.0 copy-start
  0.7 0.0 copy-start.1
  0.7 0.0 copy-start.2
  0.7 0.0 copy-start.3
  0.7 0.0 copy-start.5
  0.7 0.0 copy-start.6
  0.7 0.0 copy-start.7
  0.7 5.0 %collective-permute-start.4 = (f32[400,2048]{1,0:T(8,128)}, f32[400,2048]{1,0:T(8,128)S(1)}, u32[]{:S(2)}, u32[]{:S(2)}) collective-permute-start(f32[400,2048]{1,0:T(8,128)} %bitcast.18), channel_id=1, source_target_pairs={{2,4},{6,8},{10,12},{14,16},{18,20},{22,24},{26,28},{30,0},{3,5},{... | collective-permute-start | bytes 9830408 | tf_op jit(solution)/shard_map/ppermute | solution.py:411
  5.7 2.3 %fusion = (f32[400,1024]{1,0:T(8,128)S(1)}, f32[400,1024]{1,0:T(8,128)S(1)}) fusion(f32[400,2048]{1,0:T(8,128)} %bitcast.19), kind=kLoop, calls=%fused_computation.3 | loop fusion | bytes 6553600 | tf_op jit(solution)/shard_map/slice | solution.py:412
  8.0 0.0 copy-start.4
  8.0 1.3 %collective-permute-start.2 = (f32[400,1024]{1,0:T(8,128)S(1)}, f32[400,1024]{1,0:T(8,128)S(1)}, u32[]{:S(2)}, u32[]{:S(2)}) collective-permute-start(f32[400,1024]{1,0:T(8,128)S(1)} %get-tuple-element.103), channel_id=1, source_target_pairs={{0,2},{4,6},{8,10},{12,14},{16,18},{20,22},{24,26},{28,30},{1,3},{... | collective-permute-start | bytes 4915208 | tf_op jit(solution)/shard_map/ppermute | solution.py:412
  9.3 1.3 %collective-permute-start.1 = (f32[400,1024]{1,0:T(8,128)S(1)}, f32[400,1024]{1,0:T(8,128)S(1)}, u32[]{:S(2)}, u32[]{:S(2)}) collective-permute-start(f32[400,1024]{1,0:T(8,128)S(1)} %get-tuple-element.104), channel_id=1, source_target_pairs={{0,2},{4,6},{8,10},{12,14},{16,18},{20,22},{24,26},{28,30},{1,3},{... | collective-permute-start | bytes 4915208 | tf_op jit(solution)/shard_map/ppermute | solution.py:412
  10.6 0.0 copy-done.8
  10.7 1.4 %collective-permute-start = (f32[2048]{0:T(1024)S(1)}, f32[2048]{0:T(1024)S(1)}, u32[]{:S(2)}, u32[]{:S(2)}) collective-permute-start(f32[2048]{0:T(1024)S(1)} %copy-done.8), channel_id=1, source_target_pairs={{0,2},{4,6},{8,10},{12,14},{16,18},{20,22},{24,26},{28,30},{2,0},{... | collective-permute-start | bytes 24584 | tf_op jit(solution)/shard_map/ppermute | solution.py:413
  12.0 0.0 copy-done
  12.0 0.0 copy-done.1
  12.1 0.0 copy-done.2
  12.1 0.0 copy-done.3
  12.1 0.0 copy-done.5
  12.1 0.0 copy-done.6
  12.1 0.0 copy-done.7
  12.1 3.6 %prepare0.1 = (f32[400,256]{1,0:T(8,128)S(1)}, f32[400,256]{1,0:T(8,128)S(1)}, bf16[400,256]{1,0:T(8,128)(2,1)S(1)}, bf16[256,400]{1,0:T(8,128)(2,1)S(1)}, bf16[...) custom-call(f32[400,2048]{1,0:T(8,128)S(1)} %bitcast.9, ...), custom_call_target="tpu_custom_call" | custom-call | flops 1000000 | bytes 100000 | tf_op jit(solution)/shard_map/prepare0/pallas_call | solution.py:283
  15.6 0.1 collective-permute-done
  15.8 0.0 collective-permute-done.2.refs_15_
  15.8 0.0 collective-permute-done.1.refs_14_
  15.8 0.0 copy-done.4
  15.8 13.6 %first_near.1 = (f32[400,2048]{1,0:T(8,128)S(1)}, f32[1,2048]{1,0:T(1,128)S(1)}, f32[32,400]{1,0:T(8,128)S(1)}, f32[408,1536]{1,0:T(8,128)S(1)}, f32[408,256]{1,0:T(8,128)S(1)}, /*index=5*/f32[408,256]{1,0:T(8,128)S(1)}) custom-call(f32[400,2048]{1,0:T(8,128)S(1)} %bitcast.10, f32[1,2048]{1,0:T(1,128)S(1)} %bitcast.14, f32[1,2048]{1,0:T(1,128)S(1)} %bitcast.12, ...), custom_call_target="tpu_custom_call" | custom-call | flops 1000000 | bytes 100000 | tf_op jit(solution)/shard_map/first_near/pallas_call | solution.py:283
  29.4 1.5 %collective-permute-start.9 = (f32[408,1536]{1,0:T(8,128)S(1)}, f32[408,1536]{1,0:T(8,128)S(1)}, u32[]{:S(2)}, u32[]{:S(2)}) collective-permute-start(f32[408,1536]{1,0:T(8,128)S(1)} %get-tuple-element.84), channel_id=1, source_target_pairs={{2,4},{6,8},{10,12},{14,16},{18,20},{22,24},{26,28},{30,0},{3,5},{... | collective-permute-start | bytes 7520264 | tf_op jit(solution)/shard_map/ppermute | solution.py:419
  30.8 0.7 collective-permute-start.3
  31.5 0.0 collective-permute-done.3
  31.5 10.0 %collective-permute-done.4.refs_14_ = f32[400,2048]{1,0:T(8,128)S(1)} collective-permute-done((f32[400,2048]{1,0:T(8,128)}, f32[400,2048]{1,0:T(8,128)S(1)}, u32[]{:S(2)}, u32[]{:S(2)}) %collective-permute-start.4) | collective-permute-done | bytes 3276832 | tf_op jit(solution)/shard_map/ppermute | solution.py:411
  41.5 0.1 first_far.1
  41.7 1.3 %collective-permute-start.5 = (f32[408,1024]{1,0:T(8,128)S(1)}, f32[408,1024]{1,0:T(8,128)S(1)}, u32[]{:S(2)}, u32[]{:S(2)}) collective-permute-start(f32[408,1024]{1,0:T(8,128)S(1)} %get-tuple-element.79), channel_id=1, source_target_pairs={{0,2},{4,6},{8,10},{12,14},{16,18},{20,22},{24,26},{28,30},{1,3},{... | collective-permute-start | bytes 5013512 | tf_op jit(solution)/shard_map/ppermute | solution.py:423
  43.0 1.3 %collective-permute-start.6 = (f32[408,1024]{1,0:T(8,128)S(1)}, f32[408,1024]{1,0:T(8,128)S(1)}, u32[]{:S(2)}, u32[]{:S(2)}) collective-permute-start(f32[408,1024]{1,0:T(8,128)S(1)} %get-tuple-element.80), channel_id=1, source_target_pairs={{0,2},{4,6},{8,10},{12,14},{16,18},{20,22},{24,26},{28,30},{1,3},{... | collective-permute-start | bytes 5013512 | tf_op jit(solution)/shard_map/ppermute | solution.py:423
  44.3 18.3 %collective-permute-start.8 = (f32[408,256]{1,0:T(8,128)S(1)}, f32[408,256]{1,0:T(8,128)S(1)}, u32[]{:S(2)}, u32[]{:S(2)}) collective-permute-start(f32[408,256]{1,0:T(8,128)S(1)} %get-tuple-element.83), channel_id=1, source_target_pairs={{2,4},{6,8},{10,12},{14,16},{18,20},{22,24},{26,28},{30,0},{3,5},{... | collective-permute-start | bytes 1253384 | tf_op jit(solution)/shard_map/ppermute | solution.py:419
  62.6 1.3 %collective-permute-start.7 = (f32[408,256]{1,0:T(8,128)S(1)}, f32[408,256]{1,0:T(8,128)S(1)}, u32[]{:S(2)}, u32[]{:S(2)}) collective-permute-start(f32[408,256]{1,0:T(8,128)S(1)} %get-tuple-element.82), channel_id=1, source_target_pairs={{2,4},{6,8},{10,12},{14,16},{18,20},{22,24},{26,28},{30,0},{3,5},{... | collective-permute-start | bytes 1253384 | tf_op jit(solution)/shard_map/ppermute | solution.py:419
  63.9 3.5 %prepare1.1 = (f32[400,256]{1,0:T(8,128)S(1)}, f32[400,256]{1,0:T(8,128)S(1)}, bf16[400,256]{1,0:T(8,128)(2,1)S(1)}, bf16[256,400]{1,0:T(8,128)(2,1)S(1)}, bf16[...) custom-call(f32[400,2048]{1,0:T(8,128)S(1)} %get-tuple-element.66.le, ...), custom_call_target="tpu_custom_call" | custom-call | flops 1000000 | bytes 100000 | tf_op jit(solution)/shard_map/prepare1/pallas_call | solution.py:283
  67.4 0.8 collective-permute-done.9.refs_0_.refs_7_
  68.2 4.5 %collective-permute-done.8.refs_0_.refs_8_ = f32[408,256]{1,0:T(8,128)S(1)} collective-permute-done((f32[408,256]{1,0:T(8,128)S(1)}, f32[408,256]{1,0:T(8,128)S(1)}, u32[]{:S(2)}, u32[]{:S(2)}) %collective-permute-start.8) | collective-permute-done | bytes 417824 | tf_op jit(solution)/shard_map/ppermute | solution.py:419
  72.7 4.5 %collective-permute-done.7.refs_0_.refs_9_ = f32[408,256]{1,0:T(8,128)S(1)} collective-permute-done((f32[408,256]{1,0:T(8,128)S(1)}, f32[408,256]{1,0:T(8,128)S(1)}, u32[]{:S(2)}, u32[]{:S(2)}) %collective-permute-start.7) | collective-permute-done | bytes 417824 | tf_op jit(solution)/shard_map/ppermute | solution.py:419
  77.2 0.0 collective-permute-done.5.refs_14_
  77.2 0.0 collective-permute-done.6.refs_15_
  77.2 14.7 %last_near.1 = (f32[400,2048]{1,0:T(8,128)}, f32[1,2048]{1,0:T(1,128)S(1)}, f32[32,400]{1,0:T(8,128)S(1)}, f32[400,2048]{1,0:T(8,128)}) custom-call(f32[400,2048]{1,0:T(8,128)S(1)} %get-tuple-element.66.left.refs_0_, f32[1,2048]{1,0:T(1,128)S(1)} %get-tuple-element.67.refs_1_, f32[1,2048]{1,0:T(1,128)S(1)} %bitcast.13, ...), custom_call_target="tpu_custom_call" | custom-call | flops 1000000 | bytes 100000 | tf_op jit(solution)/shard_map/last_near/pallas_call | solution.py:283
  91.9 1.3 %collective-permute-start.10 = (f32[32,400]{1,0:T(8,128)S(1)}, f32[32,400]{1,0:T(8,128)S(1)}, u32[]{:S(2)}, u32[]{:S(2)}) collective-permute-start(f32[32,400]{1,0:T(8,128)S(1)} %get-tuple-element.102), channel_id=1, source_target_pairs={{0,1},{1,0},{2,3},{3,2},{4,5},{5,4},{6,7},{7,6},{8,9},{9,8},{10,11... | collective-permute-start | bytes 153608 | tf_op jit(solution)/shard_map/ppermute | solution.py:428
  93.2 0.0 copy-start.9
  93.2 0.1 last_update.1
  93.4 1.7 %collective-permute-done.10 = f32[32,400]{1,0:T(8,128)S(1)} collective-permute-done((f32[32,400]{1,0:T(8,128)S(1)}, f32[32,400]{1,0:T(8,128)S(1)}, u32[]{:S(2)}, u32[]{:S(2)}) %collective-permute-start.10) | collective-permute-done | bytes 51232 | tf_op jit(solution)/shard_map/ppermute | solution.py:428
  95.1 0.1 multiply_reduce_fusion
  95.2 0.0 copy-done.9
  95.2 0.7 subtract_bitcast_fusion
  (6 shorter events, 0.0 us)
Async XLA Ops:
  0.6 10.0 %copy-start.8 = (f32[2048]{0:T(1024)S(1)}, f32[2048]{0:T(1024)}, u32[]{:S(2)}) copy-start(f32[2048]{0:T(1024)} %param.14) | copy-start | bytes 24580
  0.6 11.4 %copy-start = (f32[2048,400]{0,1:T(8,128)S(1)}, f32[2048,400]{0,1:T(8,128)}, u32[]{:S(2)}) copy-start(f32[2048,400]{0,1:T(8,128)} %param.11) | copy-start | bytes 9830404
  0.7 11.4 %copy-start.1 = (f32[32,400]{1,0:T(8,128)S(1)}, f32[32,400]{1,0:T(8,128)}, u32[]{:S(2)}) copy-start(f32[32,400]{1,0:T(8,128)} %relations.3) | copy-start | bytes 153604
  0.7 11.4 %copy-start.2 = (s32[2,1000]{1,0:T(2,128)S(1)}, s32[2,1000]{1,0:T(2,128)}, u32[]{:S(2)}) copy-start(s32[2,1000]{1,0:T(2,128)} %nsrc.3) | copy-start | bytes 24004
  0.7 11.4 %copy-start.3 = (s32[2,1000]{1,0:T(2,128)S(1)}, s32[2,1000]{1,0:T(2,128)}, u32[]{:S(2)}) copy-start(s32[2,1000]{1,0:T(2,128)} %ndst.3) | copy-start | bytes 24004
  0.7 11.4 %copy-start.5 = (s32[2,256]{1,0:T(2,128)S(1)}, s32[2,256]{1,0:T(2,128)}, u32[]{:S(2)}) copy-start(s32[2,256]{1,0:T(2,128)} %src.3) | copy-start | bytes 6148
  0.7 11.4 %copy-start.6 = (s32[2,256]{1,0:T(2,128)S(1)}, s32[2,256]{1,0:T(2,128)}, u32[]{:S(2)}) copy-start(s32[2,256]{1,0:T(2,128)} %dst.3) | copy-start | bytes 6148
  0.7 11.4 %copy-start.7 = (s32[2,256]{1,0:T(2,128)S(1)}, s32[2,256]{1,0:T(2,128)}, u32[]{:S(2)}) copy-start(s32[2,256]{1,0:T(2,128)} %rid.3) | copy-start | bytes 6148
  0.7 40.8 %collective-permute-start.4 = (f32[400,2048]{1,0:T(8,128)}, f32[400,2048]{1,0:T(8,128)S(1)}, u32[]{:S(2)}, u32[]{:S(2)}) collective-permute-start(f32[400,2048]{1,0:T(8,128)} %bitcast.18), channel_id=1, source_target_pairs={{2,4},{6,8},{10,12},{14,16},{18,20},{22,24},{26,28},{30,0},{3,5},{... | collective-permute-start | bytes 9830408 | tf_op jit(solution)/shard_map/ppermute | solution.py:411
  8.0 7.8 %copy-start.4 = (f32[2048]{0:T(1024)S(1)}, f32[2048]{0:T(1024)}, u32[]{:S(2)}) copy-start(f32[2048]{0:T(1024)} %param.12) | copy-start | bytes 24580
  8.0 7.8 %collective-permute-start.2 = (f32[400,1024]{1,0:T(8,128)S(1)}, f32[400,1024]{1,0:T(8,128)S(1)}, u32[]{:S(2)}, u32[]{:S(2)}) collective-permute-start(f32[400,1024]{1,0:T(8,128)S(1)} %get-tuple-element.103), channel_id=1, source_target_pairs={{0,2},{4,6},{8,10},{12,14},{16,18},{20,22},{24,26},{28,30},{1,3},{... | collective-permute-start | bytes 4915208 | tf_op jit(solution)/shard_map/ppermute | solution.py:412
  9.3 6.5 %collective-permute-start.1 = (f32[400,1024]{1,0:T(8,128)S(1)}, f32[400,1024]{1,0:T(8,128)S(1)}, u32[]{:S(2)}, u32[]{:S(2)}) collective-permute-start(f32[400,1024]{1,0:T(8,128)S(1)} %get-tuple-element.104), channel_id=1, source_target_pairs={{0,2},{4,6},{8,10},{12,14},{16,18},{20,22},{24,26},{28,30},{1,3},{... | collective-permute-start | bytes 4915208 | tf_op jit(solution)/shard_map/ppermute | solution.py:412
  10.7 5.1 %collective-permute-start = (f32[2048]{0:T(1024)S(1)}, f32[2048]{0:T(1024)S(1)}, u32[]{:S(2)}, u32[]{:S(2)}) collective-permute-start(f32[2048]{0:T(1024)S(1)} %copy-done.8), channel_id=1, source_target_pairs={{0,2},{4,6},{8,10},{12,14},{16,18},{20,22},{24,26},{28,30},{2,0},{... | collective-permute-start | bytes 24584 | tf_op jit(solution)/shard_map/ppermute | solution.py:413
  29.4 38.9 %collective-permute-start.9 = (f32[408,1536]{1,0:T(8,128)S(1)}, f32[408,1536]{1,0:T(8,128)S(1)}, u32[]{:S(2)}, u32[]{:S(2)}) collective-permute-start(f32[408,1536]{1,0:T(8,128)S(1)} %get-tuple-element.84), channel_id=1, source_target_pairs={{2,4},{6,8},{10,12},{14,16},{18,20},{22,24},{26,28},{30,0},{3,5},{... | collective-permute-start | bytes 7520264 | tf_op jit(solution)/shard_map/ppermute | solution.py:419
  30.8 0.7 collective-permute-start.3
  41.7 35.6 %collective-permute-start.5 = (f32[408,1024]{1,0:T(8,128)S(1)}, f32[408,1024]{1,0:T(8,128)S(1)}, u32[]{:S(2)}, u32[]{:S(2)}) collective-permute-start(f32[408,1024]{1,0:T(8,128)S(1)} %get-tuple-element.79), channel_id=1, source_target_pairs={{0,2},{4,6},{8,10},{12,14},{16,18},{20,22},{24,26},{28,30},{1,3},{... | collective-permute-start | bytes 5013512 | tf_op jit(solution)/shard_map/ppermute | solution.py:423
  43.0 34.3 %collective-permute-start.6 = (f32[408,1024]{1,0:T(8,128)S(1)}, f32[408,1024]{1,0:T(8,128)S(1)}, u32[]{:S(2)}, u32[]{:S(2)}) collective-permute-start(f32[408,1024]{1,0:T(8,128)S(1)} %get-tuple-element.80), channel_id=1, source_target_pairs={{0,2},{4,6},{8,10},{12,14},{16,18},{20,22},{24,26},{28,30},{1,3},{... | collective-permute-start | bytes 5013512 | tf_op jit(solution)/shard_map/ppermute | solution.py:423
  44.3 28.5 %collective-permute-start.8 = (f32[408,256]{1,0:T(8,128)S(1)}, f32[408,256]{1,0:T(8,128)S(1)}, u32[]{:S(2)}, u32[]{:S(2)}) collective-permute-start(f32[408,256]{1,0:T(8,128)S(1)} %get-tuple-element.83), channel_id=1, source_target_pairs={{2,4},{6,8},{10,12},{14,16},{18,20},{22,24},{26,28},{30,0},{3,5},{... | collective-permute-start | bytes 1253384 | tf_op jit(solution)/shard_map/ppermute | solution.py:419
  62.6 14.6 %collective-permute-start.7 = (f32[408,256]{1,0:T(8,128)S(1)}, f32[408,256]{1,0:T(8,128)S(1)}, u32[]{:S(2)}, u32[]{:S(2)}) collective-permute-start(f32[408,256]{1,0:T(8,128)S(1)} %get-tuple-element.82), channel_id=1, source_target_pairs={{2,4},{6,8},{10,12},{14,16},{18,20},{22,24},{26,28},{30,0},{3,5},{... | collective-permute-start | bytes 1253384 | tf_op jit(solution)/shard_map/ppermute | solution.py:419
  91.9 3.2 %collective-permute-start.10 = (f32[32,400]{1,0:T(8,128)S(1)}, f32[32,400]{1,0:T(8,128)S(1)}, u32[]{:S(2)}, u32[]{:S(2)}) collective-permute-start(f32[32,400]{1,0:T(8,128)S(1)} %get-tuple-element.102), channel_id=1, source_target_pairs={{0,1},{1,0},{2,3},{3,2},{4,5},{5,4},{6,7},{7,6},{8,9},{9,8},{10,11... | collective-permute-start | bytes 153608 | tf_op jit(solution)/shard_map/ppermute | solution.py:428
  93.2 2.0 %copy-start.9 = (f32[32]{0:T(128)S(1)}, f32[32]{0:T(128)}, u32[]{:S(2)}) copy-start(f32[32]{0:T(128)} %param.16) | copy-start | bytes 388

commit v2 on v1

--- a/solution.py
+++ b/solution.py
@@ -12,6 +12,7 @@
 BF16 = jnp.bfloat16
 LANES = 128
 NEAR = (4, 4)
+STATE = 1
 NEAR_FIRST = (4, 4)
 FAR = (6, 1, 1)
 VMEM_LIMIT = 30 * 2**20
@@ -35,11 +36,26 @@
 
 
 def lanes_at(i, size):
+    if isinstance(i, int):
+        return slice(i * size, (i + 1) * size)
     return pl.ds(pl.multiple_of(i * size, size), size)
 
 
 def step_of(rows):
     return 512 if rows % 512 == 0 else 256
+
+
+def each(count, body, fixed=False):
+    if fixed:
+        for i in range(count):
+            body(i)
+        return
+
+    def one(i, carry):
+        body(i)
+        return carry
+
+    lax.fori_loop(0, count, one, 0)
 
 
 def row_onehot(idx, table):
@@ -47,12 +63,11 @@
     col = jnp.broadcast_to(idx, (LANES, count)).T
     lane = lax.broadcasted_iota(jnp.int32, (count, LANES), 1)
 
-    def tile(t, carry):
+    def tile(t):
         hit = col == lane + t * LANES
         table[:, lanes_at(t, LANES)] = jnp.where(hit, 1.0, 0.0).astype(BF16)
-        return carry
-
-    lax.fori_loop(0, rows // LANES, tile, 0)
+
+    each(rows // LANES, tile)
 
 
 def row_counts(idx, rows):
@@ -95,20 +110,19 @@
 
     size = step_of(rows)
 
-    def part(i, carry):
+    def part(i):
         cut = lanes_at(i, size)
         parts = split(left[:, cut], 3)
         left16[:, cut] = parts[0]
         source[...] += sum(mul(p, oh_src[:, cut], NT) for p in parts)
-        return carry
-
-    lax.fori_loop(0, rows // size, part, 0)
+
+    each(rows // size, part)
     product = source[...] * weight[...]
     query[...] = product.astype(BF16)
     query_rows[...] = half_rows(product.astype(BF16).astype(F32))
 
 
-def take_piece(number, start, piece, query, query_rows, oh_dst, count_r, target, gq, rgrad):
+def take_piece(number, start, piece, query, query_rows, oh_dst, count_r, target, gq, rgrad, fixed=False):
     depth = target.shape[0]
     if start == 0:
         target[...] = jnp.zeros_like(target)
@@ -116,7 +130,7 @@
 
     size = step_of(piece.shape[1])
 
-    def part(i, carry):
+    def part(i):
         cut = lanes_at(i, size)
         parts = split(piece[0:depth, cut], 3)
         hits = oh_dst[:, lanes_at(i + start // size, size)]
@@ -124,12 +138,12 @@
         times = times_at(count_r, i + start // size, size)
         rgrad[:, cut], more = negatives(parts[0], query[...], query_rows[...], times, number)
         gq[...] += more
-        return carry
-
-    lax.fori_loop(0, piece.shape[1] // size, part, 0)
-
-
-def join(number, weight, source, target, gq, left16, count_l, kind, rel_in, probe, probe_rows, gp, lgrad, to_src, to_dst, rel_out):
+
+    each(piece.shape[1] // size, part, fixed)
+
+
+def join(number, weight, source, target, gq, left16, count_l, kind, rel_in,
+         probe, probe_rows, gp, lgrad, to_src, to_dst, rel_out, fixed=False):
     rows = left16.shape[1]
     product = weight[...] * target[...]
     probe[...] = product.astype(BF16)
@@ -138,13 +152,12 @@
 
     size = step_of(rows)
 
-    def part(i, carry):
+    def part(i):
         cut = lanes_at(i, size)
         lgrad[:, cut], more = negatives(left16[:, cut], probe[...], probe_rows[...], times_at(count_l, i, size), number)
         gp[...] += more
-        return carry
-
-    lax.fori_loop(0, rows // size, part, 0)
+
+    each(rows // size, part, fixed)
     depth = weight.shape[0]
     w, s, t = weight[...], source[...], target[...]
     coef = -jax.nn.sigmoid(-jnp.sum(s * w * t, axis=0, keepdims=True))
@@ -154,11 +167,11 @@
     rel_out[...] = rel_in[...] + sum(mul(kind[...], p, NT) for p in split(g_weight, 2))
 
 
-def adagrad(slab, state, grad, edges, table, start, out, new_state, send=None):
+def adagrad(slab, state, grad, edges, table, start, out, new_state, send=None, fixed=False):
     depth = grad.shape[0]
     size = step_of(grad.shape[1])
 
-    def part(i, carry):
+    def part(i):
         cut = lanes_at(i, size)
         hits = table[:, lanes_at(i + start // size, size)]
         g = grad[:, cut] + mul(edges[0:depth, :], hits, NN) + mul(edges[depth:, :], hits, NN)
@@ -167,9 +180,8 @@
         out[0:depth, cut] = slab[0:depth, cut] - g * (rate * lax.rsqrt(new))
         if send is not None:
             send(i).start()
-        return carry
-
-    lax.fori_loop(0, grad.shape[1] // size, part, 0)
+
+    each(grad.shape[1] // size, part, fixed)
 
 
 def sender(result, to, start, sems):
@@ -183,27 +195,34 @@
     return copy
 
 
-def wait_all(copy, count):
-    def one(i, carry):
-        copy(i).wait()
-        return carry
-
-    lax.fori_loop(0, count, one, 0)
-
-
-def finish_last(left, lstate, right, rstate, lgrad, rgrads, to_src, to_dst, oh_src, oh_dst, spare, left_out, right_out, sems):
+def update_and_send(pieces, state, grads, edges, table, new_state, to, sems, fixed=False):
     start = 0
     sent = []
-    for piece, state, grad in zip(right, rstate, rgrads):
-        copy = sender(grad, right_out, start, sems.at[0])
-        adagrad(piece, state, grad, to_dst, oh_dst, start, grad, spare, copy)
-        sent.append((copy, piece.shape[1] // step_of(piece.shape[1])))
-        start += piece.shape[1]
-    copy = sender(lgrad, left_out, 0, sems.at[1])
-    adagrad(left, lstate, lgrad, to_src, oh_src, 0, lgrad, spare, copy)
-    sent.append((copy, left.shape[1] // step_of(left.shape[1])))
-    for copy, count in sent:
-        wait_all(copy, count)
+    for piece, grad in zip(pieces, grads):
+        rows = grad.shape[1]
+        copy = sender(grad, to, start, sems)
+        cut = slice(start, start + rows)
+        adagrad(piece, state.at[:, cut], grad, edges, table, start, grad, new_state.at[:, cut], copy, fixed)
+        sent.append((copy, rows // step_of(rows)))
+        start += rows
+
+    def wait():
+        for copy, count in sent:
+            each(count, lambda i, copy=copy: copy(i).wait(), fixed)
+
+    return wait
+
+
+def pack_state(state, piece, depth):
+    size = state.shape[1] // 8
+    for k in range(8):
+        piece[depth + k : depth + k + 1, 0:size] = state[:, k * size : (k + 1) * size]
+
+
+def unpack_state(piece, depth, state):
+    size = state.shape[1] // 8
+    for k in range(8):
+        state[:, k * size : (k + 1) * size] = piece[depth + k : depth + k + 1, 0:size]
 
 
 def on_parity(parity):
@@ -234,7 +253,7 @@
     refs = refs[14 + takes + kept :]
     left_out, lstate_out, rel_out = refs[:3]
     right_out = refs[3 : 3 + len(gives)]
-    (target, gq, rgrad, probe, probe_rows, gp, lgrad, to_src, to_dst, spare, sems) = refs[3 + len(gives) :]
+    (target, gq, rgrad, probe, probe_rows, gp, lgrad, to_src, to_dst, rstate, spare, sems) = refs[3 + len(gives) :]
     depth, rows = left.shape
     lstate_out[...] = lstate[...]
     rel_out[...] = rel_in[...]
@@ -247,17 +266,21 @@
             grads.append(rgrad.at[:, at : at + piece.shape[1]])
             take_piece(number, at, piece, query, query_rows, oh_dst, count_r, target, gq, grads[-1])
             at += piece.shape[1]
-        join(number, weight, source, target, gq, left16, count_l, kind, rel_in, probe, probe_rows, gp, lgrad, to_src, to_dst, rel_out)
+        join(number, weight, source, target, gq, left16, count_l, kind, rel_in,
+             probe, probe_rows, gp, lgrad, to_src, to_dst, rel_out)
         if last:
-            states = [piece.at[depth : depth + 1] for piece in right]
-            finish_last(left, lstate, right, states, lgrad, grads, to_src, to_dst, oh_src, oh_dst, spare, left_out, right_out[0], sems)
+            unpack_state(right[STATE], depth, rstate)
+            wait_right = update_and_send(right, rstate, grads, to_dst, oh_dst, spare, right_out[0], sems.at[0])
+            wait_left = update_and_send([left], lstate, [lgrad], to_src, oh_src, spare, left_out, sems.at[1])
+            wait_right()
+            wait_left()
         else:
             for (at, size), out in zip(pieces_of(rows, gives), right_out):
                 for old, begin, length in rows_of(right, at, size):
                     cut = slice(begin, begin + length)
                     here = slice(begin - at, begin - at + length)
-                    adagrad(old, rstate_in.at[:, cut], rgrad.at[:, cut], to_dst, oh_dst, begin, out.at[:, here], spare.at[:, here])
-                out[depth : depth + 8, :] = jnp.broadcast_to(spare[:, 0:size], (8, size))
+                    adagrad(old, rstate_in.at[:, cut], rgrad.at[:, cut], to_dst, oh_dst, begin, out.at[:, here], spare.at[:, cut])
+            pack_state(spare, right_out[STATE], depth)
             adagrad(left, lstate, lgrad, to_src, oh_src, 0, left_out, lstate_out)
 
 
@@ -305,12 +328,14 @@
     depth, rows = left.shape
     edges = ready[0].shape[1]
     last = not gives
-    blocks = [shape(depth + 8, size) for _at, size in pieces_of(rows, gives)] or [shape(depth, rows)]
+    blocks = [shape(depth, size) for _at, size in pieces_of(rows, gives or (8,))]
+    if not last:
+        blocks[STATE] = shape(depth + 8, blocks[STATE].shape[1])
     edge = shape(depth, edges)
     edge16 = shape(depth, edges, dtype=BF16)
     pair16 = shape(2 * depth, edges, dtype=BF16)
     slab = shape(depth, rows)
-    inner = [edge, edge, slab, edge16, shape(edges, depth, dtype=BF16), edge, slab, pair16, pair16, shape(1, rows)]
+    inner = [edge, edge, slab, edge16, shape(edges, depth, dtype=BF16), edge, slab, pair16, pair16, shape(1, rows), shape(1, rows)]
     left_out, lstate_out, rel_out, *right_out = call(
         functools.partial(train, parity, number, last, len(keep), len(right), gives or (8,)),
         name,
@@ -323,74 +348,112 @@
     return left_out, lstate_out, right_out, rel_out
 
 
-def last_round(parity, number, left, lstate, far, rel, ready, keep):
-    depth, rows = left.shape
-    (weight, source, query, query_rows, left16, oh_src, oh_dst, count_l, count_r, kind) = ready
-    edges = weight.shape[1]
-    edge = shape(depth, edges)
-    pair16 = shape(2 * depth, edges, dtype=BF16)
-    slab = shape(depth, rows)
-
-    def run(body):
-        def kernel(*refs):
-            @on_parity(parity)
-            def _():
-                body(*refs)
-
-        return kernel
-
+def only_on(parity, body):
+    def kernel(*refs):
+        @on_parity(parity)
+        def _():
+            body(*refs)
+
+    return kernel
+
+
+def last_pieces(parity, number, far, ready, after):
+    (_weight, _source, query, query_rows, _left16, _oh_src, oh_dst, _count_l, count_r, _kind) = ready
+    depth, edges = query.shape
     target = gq = None
     rgrads = []
     at = 0
     for i, piece in enumerate(far):
-        held = [] if i == 0 else [target, gq]
+        held = [after] if i == 0 else [target, gq]
 
         def body(piece, query, query_rows, oh_dst, count_r, *rest, at=at, held=len(held)):
-            take_piece(number, at, piece, query, query_rows, oh_dst, count_r, *rest[held:])
+            take_piece(number, at, piece, query, query_rows, oh_dst, count_r, *rest[held:], fixed=True)
 
         target, gq, rgrad = call(
-            run(body), "last_piece%d" % i,
+            only_on(parity, body), "last_piece%d" % i,
             [piece, query, query_rows, oh_dst, count_r, *held],
-            [edge, edge, shape(depth, piece.shape[1])],
-            aliases={5 + k: k for k in range(len(held))},
+            [shape(depth, edges), shape(depth, edges), shape(depth, piece.shape[1])],
+            aliases={5: 0, 6: 1} if i else {},
         )
         rgrads.append(rgrad)
         at += piece.shape[1]
-
-    def join_body(weight, source, target, gq, left16, count_l, kind, rel_in, lgrad, to_src, to_dst, rel_out, probe, probe_rows, gp):
+    return target, gq, rgrads
+
+
+def last_join(parity, number, target, gq, rel, ready):
+    (weight, source, _query, _query_rows, left16, _oh_src, _oh_dst, count_l, _count_r, kind) = ready
+    depth, rows = left16.shape
+    edges = weight.shape[1]
+    pair16 = shape(2 * depth, edges, dtype=BF16)
+
+    def body(weight, source, target, gq, left16, count_l, kind, rel_in, lgrad, to_src, to_dst, rel_out, probe, probe_rows, gp):
         rel_out[...] = rel_in[...]
 
         @on_parity(parity)
         def _():
             join(number, weight, source, target, gq, left16, count_l, kind, rel_in,
-                 probe, probe_rows, gp, lgrad, to_src, to_dst, rel_out)
-
-    lgrad, to_src, to_dst, rel = call(
-        join_body, "last_join",
+                 probe, probe_rows, gp, lgrad, to_src, to_dst, rel_out, fixed=True)
+
+    return call(
+        body, "last_join",
         [weight, source, target, gq, left16, count_l, kind, rel],
-        [slab, pair16, pair16, shape(*rel.shape)],
-        scratch_shapes=scratch([shape(depth, edges, dtype=BF16), shape(edges, depth, dtype=BF16), edge]),
-    )
-
-    def update():
-        count = len(far)
-
-        def body(left, lstate, lgrad, to_src, to_dst, oh_src, oh_dst, *rest):
-            pieces = rest[:count]
-            grads = rest[count : 2 * count]
-            left_out, right_out, spare, sems = rest[2 * count + 2 :]
-            states = [piece.at[depth : depth + 1] for piece in pieces]
-            finish_last(left, lstate, pieces, states, lgrad, grads, to_src, to_dst, oh_src, oh_dst, spare, left_out, right_out, sems)
-
-        operands = [left, lstate, lgrad, to_src, to_dst, oh_src, oh_dst, *far, *rgrads, *keep]
-        places = (len(operands) - 2, len(operands) - 1)
-        return call(
-            run(body), "last_update", operands, [slab, slab], in_large=places, out_large=(0, 1),
-            scratch_shapes=[pltpu.VMEM((1, rows), F32), pltpu.SemaphoreType.DMA((2, rows // 256))],
-            aliases={places[0]: 0, places[1]: 1},
-        )
-
-    return rel, update
+        [shape(depth, rows), pair16, pair16, shape(*rel.shape)],
+        scratch_shapes=scratch([shape(depth, edges, dtype=BF16), shape(edges, depth, dtype=BF16), shape(depth, edges)]),
+    )
+
+
+def last_right(parity, far, rgrads, to_dst, oh_dst, keep):
+    count = len(far)
+    depth, rows = keep.shape
+
+    def body(to_dst, oh_dst, *rest):
+        pieces, grads = rest[:count], rest[count : 2 * count]
+        out, state, spare, sems = rest[2 * count + 1 :]
+        unpack_state(pieces[STATE], depth, state)
+        update_and_send(pieces, state, grads, to_dst, oh_dst, spare, out, sems, fixed=True)()
+
+    operands = [to_dst, oh_dst, *far, *rgrads, keep]
+    place = len(operands) - 1
+    return call(
+        only_on(parity, body), "last_right", operands, [shape(depth, rows)], in_large=(place,), out_large=(0,),
+        scratch_shapes=[*scratch([shape(1, rows), shape(1, rows)]), pltpu.SemaphoreType.DMA((rows // 256,))],
+        aliases={place: 0},
+    )[0]
+
+
+def last_left(parity, left, lstate, lgrad, to_src, oh_src, relations, relation_state, rels, keep):
+    depth, rows = left.shape
+    kinds = relations.shape[0]
+
+    def body(left, lstate, lgrad, to_src, oh_src, relations, relation_state, *rest):
+        rels = rest[: len(rest) - 7]
+        left_out, relations_out, new_relations, spare, sems, sem = rest[len(rest) - 6 :]
+        grad = sum(ref[...] for ref in rels)
+        first = lax.broadcasted_iota(jnp.int32, (kinds, kinds), 0)
+        second = lax.broadcasted_iota(jnp.int32, (kinds, kinds), 1)
+        old = jnp.sum(jnp.where(first == second, relation_state[...], 0.0), axis=1, keepdims=True)
+        new = old + jnp.sum(grad * grad, axis=1, keepdims=True) * (1.0 / depth)
+        new_relations[...] = relations[...] - grad * (rate * lax.rsqrt(new))
+        copy = pltpu.make_async_copy(new_relations, relations_out, sem)
+        copy.start()
+
+        @on_parity(parity)
+        def _():
+            update_and_send([left], lstate, [lgrad], to_src, oh_src, spare, left_out, sems, fixed=True)()
+
+        copy.wait()
+
+    operands = [left, lstate, lgrad, to_src, oh_src, relations, relation_state, *rels, keep]
+    place = len(operands) - 1
+    return call(
+        body, "last_left", operands, [shape(depth, rows), shape(*relations.shape)], in_large=(place,), out_large=(0, 1),
+        scratch_shapes=[
+            *scratch([shape(*relations.shape), shape(1, rows)]),
+            pltpu.SemaphoreType.DMA((rows // 256,)),
+            pltpu.SemaphoreType.DMA,
+        ],
+        aliases={place: 0},
+    )
 
 
 def local(
@@ -423,14 +486,16 @@
     near = [lax.ppermute(piece, "blk", inside) for piece in near]
     ready = prepared(1, left_a, relations, index)
     left_b, lstate, right_b, rel = trained(1, "last_near", number, (), left_a, lstate, near, state_near, rel, ready)
-    rel, update = last_round(0, number, left_a, lstate, far, rel, ready, (left_b, *right_b))
+    target, gq, rgrads = last_pieces(0, number, far, ready, lstate)
+    lgrad, to_src, to_dst, rel = last_join(0, number, target, gq, rel, ready)
     if lax.axis_size("rel") == 2:
-        rel = rel + lax.ppermute(rel, "rel", [(0, 1), (1, 0)])
+        rels = [rel, lax.ppermute(rel, "rel", [(0, 1), (1, 0)])]
     else:
-        rel = lax.psum(rel, "rel")
-    left_b, right_b = update()
-    new_rstate = relation_state + jnp.mean(rel * rel, axis=1)
-    relations_out = relations - rate * rel / jnp.sqrt(new_rstate)[:, None]
+        rels = [lax.psum(rel, "rel")]
+    right_b = last_right(0, far, rgrads, to_dst, ready[6], right_b[0])
+    left_b, relations_out = last_left(
+        0, left_a, lstate, lgrad, to_src, ready[5], relations, relation_state.reshape(1, -1), rels, left_b
+    )
     return (left_b.T, right_b.T, relations_out[None])
 
 

time: 96.3 us -> 90.9 us (0.944)
  the two profiles are of different devices: /device:TPU:1 before, /device:TPU:0 now
where the time goes in v2:
time: 90.9 us; the launch traced here: 90.6 us
  Pallas kernels  32.9 us (36%)
  waiting for transfers between devices  32.4 us (36%)
  starting transfers between devices  21.9 us (24%)
  local copies, waits for them, and re-layouts  2.21 us (2%)
  between operations  1.16 us (1%)
    pallas_call x11, Pallas kernels, call(): pl.pallas_call(kernel, out_shape=tuple(shapes), in_specs=[large if i in i...  32.9 us
    ppermute x1, waiting for transfers between devices, local(): right_far = lax.ppermute(right, 'blk', across)  18.7 us
    ppermute x3, waiting for transfers between devices, local(): far = [lax.ppermute(piece, 'blk', across) for piece in far]  8.54 us
    ppermute x2, starting transfers between devices, local(): lax.ppermute(right[:, at:at + size], 'blk', inside)  7.28 us
    ppermute x1, waiting for transfers between devices, local(): state_far = lax.ppermute(state_near, 'blk', skip).reshape(1, rows)  4.93 us
    ppermute x3, starting transfers between devices, local(): far = [lax.ppermute(piece, 'blk', across) for piece in far]  4.06 us
    ppermute x1, starting transfers between devices, local(): state_far = lax.ppermute(state_near, 'blk', skip).reshape(1, rows)  3.46 us
    ppermute x2, starting transfers between devices, local(): near = [lax.ppermute(piece, 'blk', inside) for piece in near]  2.79 us
  transfers between devices with their start and end apart: 11, of which 6 were waited for; matrix products, arithmetic and copies ran while one was open for 2% of the time, Pallas kernels for 30%

profile of v2, /device:TPU:0, one launch (start us, length us, event | category | flops | bytes accessed | tf_op | source)
XLA Modules:
  0.0 90.6 jit_solution(12075296708094953687)
XLA Ops:
  0.6 0.0 copy-start.9
  0.6 0.0 copy-start
  0.7 0.0 copy-start.1
  0.7 0.0 copy-start.2
  0.7 0.0 copy-start.3
  0.7 0.0 copy-start.5
  0.7 0.0 copy-start.6
  0.7 0.0 copy-start.7
  0.7 1.6 %collective-permute-start.4 = (f32[400,2048]{1,0:T(8,128)}, f32[400,2048]{1,0:T(8,128)S(1)}, u32[]{:S(2)}, u32[]{:S(2)}) collective-permute-start(f32[400,2048]{1,0:T(8,128)} %bitcast.17), channel_id=1, source_target_pairs={{2,4},{6,8},{10,12},{14,16},{18,20},{22,24},{26,28},{30,0},{3,5},{... | collective-permute-start | bytes 9830408 | tf_op jit(solution)/shard_map/ppermute | solution.py:474
  2.3 2.2 %fusion = (f32[400,1024]{1,0:T(8,128)S(1)}, f32[400,1024]{1,0:T(8,128)S(1)}) fusion(f32[400,2048]{1,0:T(8,128)} %bitcast.18), kind=kLoop, calls=%fused_computation | loop fusion | bytes 6553600 | tf_op jit(solution)/shard_map/slice | solution.py:475
  4.4 0.0 copy-start.4
  4.5 5.9 %collective-permute-start.2 = (f32[400,1024]{1,0:T(8,128)S(1)}, f32[400,1024]{1,0:T(8,128)S(1)}, u32[]{:S(2)}, u32[]{:S(2)}) collective-permute-start(f32[400,1024]{1,0:T(8,128)S(1)} %get-tuple-element.103), channel_id=1, source_target_pairs={{0,2},{4,6},{8,10},{12,14},{16,18},{20,22},{24,26},{28,30},{1,3},{... | collective-permute-start | bytes 4915208 | tf_op jit(solution)/shard_map/ppermute | solution.py:475
  10.3 1.4 %collective-permute-start.1 = (f32[400,1024]{1,0:T(8,128)S(1)}, f32[400,1024]{1,0:T(8,128)S(1)}, u32[]{:S(2)}, u32[]{:S(2)}) collective-permute-start(f32[400,1024]{1,0:T(8,128)S(1)} %get-tuple-element.104), channel_id=1, source_target_pairs={{0,2},{4,6},{8,10},{12,14},{16,18},{20,22},{24,26},{28,30},{1,3},{... | collective-permute-start | bytes 4915208 | tf_op jit(solution)/shard_map/ppermute | solution.py:475
  11.7 0.0 copy-done.9
  11.8 0.1 collective-permute-start
  11.8 0.0 copy-done
  11.8 0.0 copy-done.1
  11.9 0.0 copy-done.2
  11.9 0.0 copy-done.3
  11.9 0.0 copy-done.5
  11.9 0.0 copy-done.6
  11.9 0.0 copy-done.7
  11.9 3.6 %prepare0.1 = (f32[400,256]{1,0:T(8,128)S(1)}, f32[400,256]{1,0:T(8,128)S(1)}, bf16[400,256]{1,0:T(8,128)(2,1)S(1)}, bf16[256,400]{1,0:T(8,128)(2,1)S(1)}, bf16[...) custom-call(f32[400,2048]{1,0:T(8,128)S(1)} %bitcast.9, ...), custom_call_target="tpu_custom_call" | custom-call | flops 1000000 | bytes 100000 | tf_op jit(solution)/shard_map/prepare0/pallas_call | solution.py:306
  15.5 0.2 collective-permute-done
  15.7 0.0 collective-permute-done.2.refs_15_
  15.7 0.0 collective-permute-done.1.refs_14_
  15.7 0.0 copy-done.4
  15.7 0.2 first_near.1
  15.9 1.3 %collective-permute-start.9 = (f32[400,1536]{1,0:T(8,128)S(1)}, f32[400,1536]{1,0:T(8,128)S(1)}, u32[]{:S(2)}, u32[]{:S(2)}) collective-permute-start(f32[400,1536]{1,0:T(8,128)S(1)} %get-tuple-element.84), channel_id=1, source_target_pairs={{2,4},{6,8},{10,12},{14,16},{18,20},{22,24},{26,28},{30,0},{3,5},{... | collective-permute-start | bytes 7372808 | tf_op jit(solution)/shard_map/ppermute | solution.py:482
  17.2 3.5 %collective-permute-start.3 = (f32[2048]{0:T(1024)S(1)}, f32[2048]{0:T(1024)S(1)}, u32[]{:S(2)}, u32[]{:S(2)}) collective-permute-start(f32[2048]{0:T(1024)S(1)} %collective-permute-done), channel_id=1, source_target_pairs={{0,4},{4,8},{8,12},{12,16},{16,20},{20,24},{24,28},{28,0},{1,5},{5... | collective-permute-start | bytes 24584 | tf_op jit(solution)/shard_map/ppermute | solution.py:477
  20.7 4.9 %collective-permute-done.3 = f32[2048]{0:T(1024)S(1)} collective-permute-done((f32[2048]{0:T(1024)S(1)}, f32[2048]{0:T(1024)S(1)}, u32[]{:S(2)}, u32[]{:S(2)}) %collective-permute-start.3) | collective-permute-done | bytes 8224 | tf_op jit(solution)/shard_map/ppermute | solution.py:477
  25.6 18.7 %collective-permute-done.4.refs_14_ = f32[400,2048]{1,0:T(8,128)S(1)} collective-permute-done((f32[400,2048]{1,0:T(8,128)}, f32[400,2048]{1,0:T(8,128)S(1)}, u32[]{:S(2)}, u32[]{:S(2)}) %collective-permute-start.4) | collective-permute-done | bytes 3276832 | tf_op jit(solution)/shard_map/ppermute | solution.py:474
  44.3 13.8 %first_far.1 = (f32[400,2048]{1,0:T(8,128)S(1)}, f32[1,2048]{1,0:T(1,128)S(1)}, f32[32,400]{1,0:T(8,128)S(1)}, f32[400,1024]{1,0:T(8,128)S(1)}, f32[408,1024]{1,0:T(8,128)S(1)}) custom-call(f32[400,2048]{1,0:T(8,128)S(1)} %bitcast.11, f32[1,2048]{1,0:T(1,128)S(1)} %get-tuple-element.63.refs_1_, ...), custom_call_target="tpu_custom_call", output_to_operand_aliasing={{0}: (15, {})} | custom-call | flops 1000000 | bytes 100000 | tf_op jit(solution)/shard_map/first_far/pallas_call | solution.py:306
  58.1 1.4 %collective-permute-start.6 = (f32[408,1024]{1,0:T(8,128)S(1)}, f32[408,1024]{1,0:T(8,128)S(1)}, u32[]{:S(2)}, u32[]{:S(2)}) collective-permute-start(f32[408,1024]{1,0:T(8,128)S(1)} %get-tuple-element.80), channel_id=1, source_target_pairs={{0,2},{4,6},{8,10},{12,14},{16,18},{20,22},{24,26},{28,30},{1,3},{... | collective-permute-start | bytes 5013512 | tf_op jit(solution)/shard_map/ppermute | solution.py:486
  59.5 1.4 %collective-permute-start.5 = (f32[400,1024]{1,0:T(8,128)S(1)}, f32[400,1024]{1,0:T(8,128)S(1)}, u32[]{:S(2)}, u32[]{:S(2)}) collective-permute-start(f32[400,1024]{1,0:T(8,128)S(1)} %get-tuple-element.79), channel_id=1, source_target_pairs={{0,2},{4,6},{8,10},{12,14},{16,18},{20,22},{24,26},{28,30},{1,3},{... | collective-permute-start | bytes 4915208 | tf_op jit(solution)/shard_map/ppermute | solution.py:486
  60.9 1.5 %collective-permute-start.8 = (f32[408,256]{1,0:T(8,128)S(1)}, f32[408,256]{1,0:T(8,128)S(1)}, u32[]{:S(2)}, u32[]{:S(2)}) collective-permute-start(f32[408,256]{1,0:T(8,128)S(1)} %get-tuple-element.83), channel_id=1, source_target_pairs={{2,4},{6,8},{10,12},{14,16},{18,20},{22,24},{26,28},{30,0},{3,5},{... | collective-permute-start | bytes 1253384 | tf_op jit(solution)/shard_map/ppermute | solution.py:482
  62.4 1.3 %collective-permute-start.7 = (f32[400,256]{1,0:T(8,128)S(1)}, f32[400,256]{1,0:T(8,128)S(1)}, u32[]{:S(2)}, u32[]{:S(2)}) collective-permute-start(f32[400,256]{1,0:T(8,128)S(1)} %get-tuple-element.82), channel_id=1, source_target_pairs={{2,4},{6,8},{10,12},{14,16},{18,20},{22,24},{26,28},{30,0},{3,5},{... | collective-permute-start | bytes 1228808 | tf_op jit(solution)/shard_map/ppermute | solution.py:482
  63.7 3.5 %prepare1.1 = (f32[400,256]{1,0:T(8,128)S(1)}, f32[400,256]{1,0:T(8,128)S(1)}, bf16[400,256]{1,0:T(8,128)(2,1)S(1)}, bf16[256,400]{1,0:T(8,128)(2,1)S(1)}, bf16[...) custom-call(f32[400,2048]{1,0:T(8,128)S(1)} %get-tuple-element.66.le, ...), custom_call_target="tpu_custom_call" | custom-call | flops 1000000 | bytes 100000 | tf_op jit(solution)/shard_map/prepare1/pallas_call | solution.py:306
  67.2 0.0 collective-permute-done.5.refs_14_
  67.3 0.0 collective-permute-done.6.refs_15_
  67.3 0.2 last_near.1
  67.4 3.2 %collective-permute-done.9.refs_0_.refs_2_ = f32[400,1536]{1,0:T(8,128)S(1)} collective-permute-done((f32[400,1536]{1,0:T(8,128)S(1)}, f32[400,1536]{1,0:T(8,128)S(1)}, u32[]{:S(2)}, u32[]{:S(2)}) %collective-permute-start.9) | collective-permute-done | bytes 2457632 | tf_op jit(solution)/shard_map/ppermute | solution.py:482
  70.7 2.9 %last_piece0.1 = (f32[400,256]{1,0:T(8,128)S(1)}, f32[400,256]{1,0:T(8,128)S(1)}, f32[400,1536]{1,0:T(8,128)S(1)}) custom-call(f32[400,1536]{1,0:T(8,128)S(1)} %collective-permute-done.9.refs_0_.refs_2_, bf16[400,256]{1,0:T(8,128)(2,1)S(1)} %get-tuple-element.71.refs_6_.refs_1_, bf16[256,400]{1,0:T(8,128)(2,1)S(1)} %get-tuple-element.72.refs_7_.refs_2_, ...), custom_call_target="tpu_custom_call" | custom-call | flops 1000000 | bytes 100000 | tf_op jit(solution)/shard_map/last_piece0/pallas_call | solution.py:306
  73.5 1.6 %collective-permute-done.8.refs_0_.refs_3_ = f32[408,256]{1,0:T(8,128)S(1)} collective-permute-done((f32[408,256]{1,0:T(8,128)S(1)}, f32[408,256]{1,0:T(8,128)S(1)}, u32[]{:S(2)}, u32[]{:S(2)}) %collective-permute-start.8) | collective-permute-done | bytes 417824 | tf_op jit(solution)/shard_map/ppermute | solution.py:482
  75.1 0.6 last_piece1.1
  75.8 3.7 %collective-permute-done.7.refs_0_.refs_4_ = f32[400,256]{1,0:T(8,128)S(1)} collective-permute-done((f32[400,256]{1,0:T(8,128)S(1)}, f32[400,256]{1,0:T(8,128)S(1)}, u32[]{:S(2)}, u32[]{:S(2)}) %collective-permute-start.7) | collective-permute-done | bytes 409632 | tf_op jit(solution)/shard_map/ppermute | solution.py:482
  79.5 0.6 last_piece2.1
  80.2 2.6 %last_join.1 = (f32[400,2048]{1,0:T(8,128)S(1)}, bf16[800,256]{1,0:T(8,128)(2,1)S(1)}, bf16[800,256]{1,0:T(8,128)(2,1)S(1)}, f32[32,400]{1,0:T(8,128)S(1)}) custom-call(f32[400,256]{1,0:T(8,128)S(1)} %get-tuple-element.69.refs_4_.weight, f32[400,256]{1,0:T(8,128)S(1)} %get-tuple-element.70.refs_5_.source, f32[400,256]{1,0:T(8,128)S(1)} %get-tuple-element.89.target, ...), custom_call_target="tpu_custom_call" | custom-call | flops 1000000 | bytes 100000 | tf_op jit(solution)/shard_map/last_join/pallas_call | solution.py:306
  82.8 2.7 %collective-permute-start.10 = (f32[32,400]{1,0:T(8,128)S(1)}, f32[32,400]{1,0:T(8,128)S(1)}, u32[]{:S(2)}, u32[]{:S(2)}) collective-permute-start(f32[32,400]{1,0:T(8,128)S(1)} %get-tuple-element.94.rest_0_), channel_id=1, source_target_pairs={{0,1},{1,0},{2,3},{3,2},{4,5},{5,4},{6,7},{7,6},{8,9},{9,8},{10,11... | collective-permute-start | bytes 153608 | tf_op jit(solution)/shard_map/ppermute | solution.py:492
  85.5 0.0 copy-start.8
  85.5 2.4 %last_right.1 = f32[400,2048]{1,0:T(8,128)} custom-call(bf16[800,256]{1,0:T(8,128)(2,1)S(1)} %get-tuple-element.97.refs_0_, bf16[256,2048]{1,0:T(8,128)(2,1)S(1)} %get-tuple-element.75.refs_10_.refs_3_.refs_1_, f32[400,1536]{1,0:T(8,128)S(1)} %collective-permute-done.9.refs_0_.refs_2_, ...), custom_call_target="tpu_custom_call", output_to_operand_aliasing={{}: (8, {})} | custom-call | flops 1000000 | bytes 100000 | tf_op jit(solution)/shard_map/last_right/pallas_call | solution.py:306
  87.9 0.0 collective-permute-done.10.rest_1_
  87.9 0.0 copy-done.8
  87.9 2.5 %last_left.1 = (f32[400,2048]{1,0:T(8,128)}, f32[32,400]{1,0:T(8,128)}) custom-call(f32[400,2048]{1,0:T(8,128)S(1)} %get-tuple-element.66.left.refs_0_, f32[1,2048]{1,0:T(1,128)S(1)} %get-tuple-element.81.refs_5_.lstate, f32[400,2048]{1,0:T(8,128)S(1)} %get-tuple-element.92.lgrad, ...), custom_call_target="tpu_custom_call", output_to_operand_aliasing={{0}: (9, {})} | custom-call | flops 1000000 | bytes 100000 | tf_op jit(solution)/shard_map/last_left/pallas_call | solution.py:306
  (1 shorter events, 0.0 us)
Async XLA Ops:
  0.6 11.1 %copy-start.9 = (f32[2048]{0:T(1024)S(1)}, f32[2048]{0:T(1024)}, u32[]{:S(2)}) copy-start(f32[2048]{0:T(1024)} %param.14) | copy-start | bytes 24580
  0.6 11.2 %copy-start = (f32[2048,400]{0,1:T(8,128)S(1)}, f32[2048,400]{0,1:T(8,128)}, u32[]{:S(2)}) copy-start(f32[2048,400]{0,1:T(8,128)} %param.11) | copy-start | bytes 9830404
  0.7 11.2 %copy-start.1 = (f32[32,400]{1,0:T(8,128)S(1)}, f32[32,400]{1,0:T(8,128)}, u32[]{:S(2)}) copy-start(f32[32,400]{1,0:T(8,128)} %relations.5) | copy-start | bytes 153604
  0.7 11.2 %copy-start.2 = (s32[2,1000]{1,0:T(2,128)S(1)}, s32[2,1000]{1,0:T(2,128)}, u32[]{:S(2)}) copy-start(s32[2,1000]{1,0:T(2,128)} %nsrc.3) | copy-start | bytes 24004
  0.7 11.2 %copy-start.3 = (s32[2,1000]{1,0:T(2,128)S(1)}, s32[2,1000]{1,0:T(2,128)}, u32[]{:S(2)}) copy-start(s32[2,1000]{1,0:T(2,128)} %ndst.3) | copy-start | bytes 24004
  0.7 11.2 %copy-start.5 = (s32[2,256]{1,0:T(2,128)S(1)}, s32[2,256]{1,0:T(2,128)}, u32[]{:S(2)}) copy-start(s32[2,256]{1,0:T(2,128)} %src.3) | copy-start | bytes 6148
  0.7 11.2 %copy-start.6 = (s32[2,256]{1,0:T(2,128)S(1)}, s32[2,256]{1,0:T(2,128)}, u32[]{:S(2)}) copy-start(s32[2,256]{1,0:T(2,128)} %dst.3) | copy-start | bytes 6148
  0.7 11.2 %copy-start.7 = (s32[2,256]{1,0:T(2,128)S(1)}, s32[2,256]{1,0:T(2,128)}, u32[]{:S(2)}) copy-start(s32[2,256]{1,0:T(2,128)} %rid.3) | copy-start | bytes 6148
  0.7 43.6 %collective-permute-start.4 = (f32[400,2048]{1,0:T(8,128)}, f32[400,2048]{1,0:T(8,128)S(1)}, u32[]{:S(2)}, u32[]{:S(2)}) collective-permute-start(f32[400,2048]{1,0:T(8,128)} %bitcast.17), channel_id=1, source_target_pairs={{2,4},{6,8},{10,12},{14,16},{18,20},{22,24},{26,28},{30,0},{3,5},{... | collective-permute-start | bytes 9830408 | tf_op jit(solution)/shard_map/ppermute | solution.py:474
  4.4 11.3 %copy-start.4 = (f32[2048]{0:T(1024)S(1)}, f32[2048]{0:T(1024)}, u32[]{:S(2)}) copy-start(f32[2048]{0:T(1024)} %param.12) | copy-start | bytes 24580
  4.5 11.3 %collective-permute-start.2 = (f32[400,1024]{1,0:T(8,128)S(1)}, f32[400,1024]{1,0:T(8,128)S(1)}, u32[]{:S(2)}, u32[]{:S(2)}) collective-permute-start(f32[400,1024]{1,0:T(8,128)S(1)} %get-tuple-element.103), channel_id=1, source_target_pairs={{0,2},{4,6},{8,10},{12,14},{16,18},{20,22},{24,26},{28,30},{1,3},{... | collective-permute-start | bytes 4915208 | tf_op jit(solution)/shard_map/ppermute | solution.py:475
  10.3 5.4 %collective-permute-start.1 = (f32[400,1024]{1,0:T(8,128)S(1)}, f32[400,1024]{1,0:T(8,128)S(1)}, u32[]{:S(2)}, u32[]{:S(2)}) collective-permute-start(f32[400,1024]{1,0:T(8,128)S(1)} %get-tuple-element.104), channel_id=1, source_target_pairs={{0,2},{4,6},{8,10},{12,14},{16,18},{20,22},{24,26},{28,30},{1,3},{... | collective-permute-start | bytes 4915208 | tf_op jit(solution)/shard_map/ppermute | solution.py:475
  11.8 4.0 %collective-permute-start = (f32[2048]{0:T(1024)S(1)}, f32[2048]{0:T(1024)S(1)}, u32[]{:S(2)}, u32[]{:S(2)}) collective-permute-start(f32[2048]{0:T(1024)S(1)} %copy-done.9), channel_id=1, source_target_pairs={{0,2},{4,6},{8,10},{12,14},{16,18},{20,22},{24,26},{28,30},{2,0},{... | collective-permute-start | bytes 24584 | tf_op jit(solution)/shard_map/ppermute | solution.py:476
  15.9 54.7 %collective-permute-start.9 = (f32[400,1536]{1,0:T(8,128)S(1)}, f32[400,1536]{1,0:T(8,128)S(1)}, u32[]{:S(2)}, u32[]{:S(2)}) collective-permute-start(f32[400,1536]{1,0:T(8,128)S(1)} %get-tuple-element.84), channel_id=1, source_target_pairs={{2,4},{6,8},{10,12},{14,16},{18,20},{22,24},{26,28},{30,0},{3,5},{... | collective-permute-start | bytes 7372808 | tf_op jit(solution)/shard_map/ppermute | solution.py:482
  17.2 8.4 %collective-permute-start.3 = (f32[2048]{0:T(1024)S(1)}, f32[2048]{0:T(1024)S(1)}, u32[]{:S(2)}, u32[]{:S(2)}) collective-permute-start(f32[2048]{0:T(1024)S(1)} %collective-permute-done), channel_id=1, source_target_pairs={{0,4},{4,8},{8,12},{12,16},{16,20},{20,24},{24,28},{28,0},{1,5},{5... | collective-permute-start | bytes 24584 | tf_op jit(solution)/shard_map/ppermute | solution.py:477
  58.1 9.2 %collective-permute-start.6 = (f32[408,1024]{1,0:T(8,128)S(1)}, f32[408,1024]{1,0:T(8,128)S(1)}, u32[]{:S(2)}, u32[]{:S(2)}) collective-permute-start(f32[408,1024]{1,0:T(8,128)S(1)} %get-tuple-element.80), channel_id=1, source_target_pairs={{0,2},{4,6},{8,10},{12,14},{16,18},{20,22},{24,26},{28,30},{1,3},{... | collective-permute-start | bytes 5013512 | tf_op jit(solution)/shard_map/ppermute | solution.py:486
  59.5 7.7 %collective-permute-start.5 = (f32[400,1024]{1,0:T(8,128)S(1)}, f32[400,1024]{1,0:T(8,128)S(1)}, u32[]{:S(2)}, u32[]{:S(2)}) collective-permute-start(f32[400,1024]{1,0:T(8,128)S(1)} %get-tuple-element.79), channel_id=1, source_target_pairs={{0,2},{4,6},{8,10},{12,14},{16,18},{20,22},{24,26},{28,30},{1,3},{... | collective-permute-start | bytes 4915208 | tf_op jit(solution)/shard_map/ppermute | solution.py:486
  60.9 14.2 %collective-permute-start.8 = (f32[408,256]{1,0:T(8,128)S(1)}, f32[408,256]{1,0:T(8,128)S(1)}, u32[]{:S(2)}, u32[]{:S(2)}) collective-permute-start(f32[408,256]{1,0:T(8,128)S(1)} %get-tuple-element.83), channel_id=1, source_target_pairs={{2,4},{6,8},{10,12},{14,16},{18,20},{22,24},{26,28},{30,0},{3,5},{... | collective-permute-start | bytes 1253384 | tf_op jit(solution)/shard_map/ppermute | solution.py:482
  62.4 17.1 %collective-permute-start.7 = (f32[400,256]{1,0:T(8,128)S(1)}, f32[400,256]{1,0:T(8,128)S(1)}, u32[]{:S(2)}, u32[]{:S(2)}) collective-permute-start(f32[400,256]{1,0:T(8,128)S(1)} %get-tuple-element.82), channel_id=1, source_target_pairs={{2,4},{6,8},{10,12},{14,16},{18,20},{22,24},{26,28},{30,0},{3,5},{... | collective-permute-start | bytes 1228808 | tf_op jit(solution)/shard_map/ppermute | solution.py:482
  82.8 5.1 %collective-permute-start.10 = (f32[32,400]{1,0:T(8,128)S(1)}, f32[32,400]{1,0:T(8,128)S(1)}, u32[]{:S(2)}, u32[]{:S(2)}) collective-permute-start(f32[32,400]{1,0:T(8,128)S(1)} %get-tuple-element.94.rest_0_), channel_id=1, source_target_pairs={{0,1},{1,0},{2,3},{3,2},{4,5},{5,4},{6,7},{7,6},{8,9},{9,8},{10,11... | collective-permute-start | bytes 153608 | tf_op jit(solution)/shard_map/ppermute | solution.py:492
  85.5 2.4 %copy-start.8 = (f32[32]{0:T(128)S(1)}, f32[32]{0:T(128)}, u32[]{:S(2)}) copy-start(f32[32]{0:T(128)} %param.16) | copy-start | bytes 388

commit v3 on v2

--- a/solution.py
+++ b/solution.py
@@ -12,7 +12,7 @@
 BF16 = jnp.bfloat16
 LANES = 128
 NEAR = (4, 4)
-STATE = 1
+STATE = 0
 NEAR_FIRST = (4, 4)
 FAR = (6, 1, 1)
 VMEM_LIMIT = 30 * 2**20
@@ -88,11 +88,18 @@
     return (0.5 * x).T.astype(BF16)
 
 
+def negative_weights(rows16, query_rows, number):
+    half = 0.5 / number
+    return (jnp.tanh(mul(query_rows, rows16, NN)) * half + half).astype(BF16)
+
+
+def often(weight, times):
+    return (weight.astype(F32) * times).astype(BF16)
+
+
 def negatives(rows16, query, query_rows, times, number):
-    half = 0.5 / number
-    weight = (jnp.tanh(mul(query_rows, rows16, NN)) * half + half).astype(BF16)
-    often = (weight.astype(F32) * times).astype(BF16)
-    return mul(query, weight, NN) * times, mul(rows16, often, NT)
+    weight = negative_weights(rows16, query_rows, number)
+    return mul(query, weight, NN) * times, mul(rows16, often(weight, times), NT)
 
 
 def prepare(step, left, relations, src, dst, rid, nsrc, ndst,
@@ -167,7 +174,7 @@
     rel_out[...] = rel_in[...] + sum(mul(kind[...], p, NT) for p in split(g_weight, 2))
 
 
-def adagrad(slab, state, grad, edges, table, start, out, new_state, send=None, fixed=False):
+def adagrad(slab, state, grad, edges, table, start, out, new_state, send=None, fixed=False, more=None):
     depth = grad.shape[0]
     size = step_of(grad.shape[1])
 
@@ -175,6 +182,8 @@
         cut = lanes_at(i, size)
         hits = table[:, lanes_at(i + start // size, size)]
         g = grad[:, cut] + mul(edges[0:depth, :], hits, NN) + mul(edges[depth:, :], hits, NN)
+        if more is not None:
+            g = g + more(i, size)
         new = state[:, cut] + jnp.sum(g * g, axis=0, keepdims=True) * (1.0 / depth)
         new_state[:, cut] = new
         out[0:depth, cut] = slab[0:depth, cut] - g * (rate * lax.rsqrt(new))
@@ -195,14 +204,13 @@
     return copy
 
 
-def update_and_send(pieces, state, grads, edges, table, new_state, to, sems, fixed=False):
-    start = 0
+def update_and_send(pieces, state, grads, edges, table, new_state, to, sems, fixed=False, start=0, more=None):
     sent = []
     for piece, grad in zip(pieces, grads):
         rows = grad.shape[1]
         copy = sender(grad, to, start, sems)
         cut = slice(start, start + rows)
-        adagrad(piece, state.at[:, cut], grad, edges, table, start, grad, new_state.at[:, cut], copy, fixed)
+        adagrad(piece, state.at[:, cut], grad, edges, table, start, grad, new_state.at[:, cut], copy, fixed, more)
         sent.append((copy, rows // step_of(rows)))
         start += rows
 
@@ -245,7 +253,7 @@
     return found
 
 
-def train(parity, number, last, kept, takes, gives, *refs):
+def train(parity, number, last, fixed, kept, takes, gives, *refs):
     refs = list(refs)
     (left, lstate, rstate_in, rel_in) = refs[:4]
     (weight, source, query, query_rows, left16, oh_src, oh_dst, count_l, count_r, kind) = refs[4:14]
@@ -264,14 +272,14 @@
         at = 0
         for piece in right:
             grads.append(rgrad.at[:, at : at + piece.shape[1]])
-            take_piece(number, at, piece, query, query_rows, oh_dst, count_r, target, gq, grads[-1])
+            take_piece(number, at, piece, query, query_rows, oh_dst, count_r, target, gq, grads[-1], fixed)
             at += piece.shape[1]
         join(number, weight, source, target, gq, left16, count_l, kind, rel_in,
-             probe, probe_rows, gp, lgrad, to_src, to_dst, rel_out)
+             probe, probe_rows, gp, lgrad, to_src, to_dst, rel_out, fixed)
         if last:
             unpack_state(right[STATE], depth, rstate)
-            wait_right = update_and_send(right, rstate, grads, to_dst, oh_dst, spare, right_out[0], sems.at[0])
-            wait_left = update_and_send([left], lstate, [lgrad], to_src, oh_src, spare, left_out, sems.at[1])
+            wait_right = update_and_send(right, rstate, grads, to_dst, oh_dst, spare, right_out[0], sems.at[0], fixed)
+            wait_left = update_and_send([left], lstate, [lgrad], to_src, oh_src, spare, left_out, sems.at[1], fixed)
             wait_right()
             wait_left()
         else:
@@ -279,9 +287,9 @@
                 for old, begin, length in rows_of(right, at, size):
                     cut = slice(begin, begin + length)
                     here = slice(begin - at, begin - at + length)
-                    adagrad(old, rstate_in.at[:, cut], rgrad.at[:, cut], to_dst, oh_dst, begin, out.at[:, here], spare.at[:, cut])
+                    adagrad(old, rstate_in.at[:, cut], rgrad.at[:, cut], to_dst, oh_dst, begin, out.at[:, here], spare.at[:, cut], None, fixed)
             pack_state(spare, right_out[STATE], depth)
-            adagrad(left, lstate, lgrad, to_src, oh_src, 0, left_out, lstate_out)
+            adagrad(left, lstate, lgrad, to_src, oh_src, 0, left_out, lstate_out, None, fixed)
 
 
 def shape(*dims, dtype=F32):
@@ -324,7 +332,7 @@
     )
 
 
-def trained(parity, name, number, gives, left, lstate, right, rstate, rel, ready, keep=()):
+def trained(parity, name, number, fixed, gives, left, lstate, right, rstate, rel, ready, keep=()):
     depth, rows = left.shape
     edges = ready[0].shape[1]
     last = not gives
@@ -337,7 +345,7 @@
     slab = shape(depth, rows)
     inner = [edge, edge, slab, edge16, shape(edges, depth, dtype=BF16), edge, slab, pair16, pair16, shape(1, rows), shape(1, rows)]
     left_out, lstate_out, rel_out, *right_out = call(
-        functools.partial(train, parity, number, last, len(keep), len(right), gives or (8,)),
+        functools.partial(train, parity, number, last, fixed, len(keep), len(right), gives or (8,)),
         name,
         [left, lstate, rstate, rel, *ready, *right, *keep],
         [slab, shape(1, rows), shape(*rel.shape), *blocks],
@@ -357,103 +365,144 @@
     return kernel
 
 
-def last_pieces(parity, number, far, ready, after):
+def last_piece(parity, name, number, at, piece, ready, after, held=()):
     (_weight, _source, query, query_rows, _left16, _oh_src, oh_dst, _count_l, count_r, _kind) = ready
     depth, edges = query.shape
-    target = gq = None
-    rgrads = []
-    at = 0
-    for i, piece in enumerate(far):
-        held = [after] if i == 0 else [target, gq]
-
-        def body(piece, query, query_rows, oh_dst, count_r, *rest, at=at, held=len(held)):
-            take_piece(number, at, piece, query, query_rows, oh_dst, count_r, *rest[held:], fixed=True)
-
-        target, gq, rgrad = call(
-            only_on(parity, body), "last_piece%d" % i,
-            [piece, query, query_rows, oh_dst, count_r, *held],
-            [shape(depth, edges), shape(depth, edges), shape(depth, piece.shape[1])],
-            aliases={5: 0, 6: 1} if i else {},
-        )
-        rgrads.append(rgrad)
-        at += piece.shape[1]
-    return target, gq, rgrads
-
-
-def last_join(parity, number, target, gq, rel, ready):
-    (weight, source, _query, _query_rows, left16, _oh_src, _oh_dst, count_l, _count_r, kind) = ready
+
+    def body(piece, query, query_rows, oh_dst, count_r, *rest):
+        take_piece(number, at, piece, query, query_rows, oh_dst, count_r, *rest[len(held) + 1 :], fixed=True)
+
+    operands = [piece, query, query_rows, oh_dst, count_r, *held, after]
+    return call(
+        only_on(parity, body), name, operands,
+        [shape(depth, edges), shape(depth, edges), shape(depth, piece.shape[1])],
+        in_large=(len(operands) - 1,), aliases={5: 0, 6: 1} if held else {},
+    )
+
+
+def early_edges(parity, number, step, bound, target, ready, dst):
+    (weight, source, _query, _query_rows, left16, _oh_src, _oh_dst, count_l, _count_r, _kind) = ready
+    depth, rows = left16.shape
+    edges = weight.shape[1]
+
+    def body(weight, source, target, left16, count_l, dst, lgrad, to_dst, gp, probe, probe_rows):
+        w, s, t = weight[...], source[...], target[...]
+        product = (w * t).astype(BF16)
+        probe[...] = product
+        probe_rows[...] = half_rows(product.astype(F32))
+        gp[...] = jnp.zeros_like(gp)
+        size = step_of(rows)
+        for i in range(rows // size):
+            cut = lanes_at(i, size)
+            lgrad[:, cut], more = negatives(left16[:, cut], probe[...], probe_rows[...], times_at(count_l, i, size), number)
+            gp[...] += more
+        early = dst[step : step + 1, :] < bound
+        gp[...] = jnp.where(early, gp[...], 0.0)
+        coef = -jax.nn.sigmoid(-jnp.sum(s * w * t, axis=0, keepdims=True))
+        to_dst[0:depth, :], to_dst[depth:, :] = split(jnp.where(early, coef * w * s + gp[...] * w, 0.0), 2)
+
+    return call(
+        only_on(parity, body), "early_edges", [weight, source, target, left16, count_l, dst],
+        [shape(depth, rows), shape(2 * depth, edges, dtype=BF16), shape(depth, edges)],
+        scratch_shapes=scratch([shape(depth, edges, dtype=BF16), shape(edges, depth, dtype=BF16)]),
+    )
+
+
+def early_right(parity, piece, rgrad, to_dst, oh_dst, keep):
+    depth, rows = keep.shape
+
+    def body(piece, rgrad, to_dst, oh_dst, _keep, out, state, spare, sems):
+        unpack_state(piece, depth, state)
+        update_and_send([piece], state, [rgrad], to_dst, oh_dst, spare, out, sems, fixed=True)()
+
+    return call(
+        only_on(parity, body), "early_right", [piece, rgrad, to_dst, oh_dst, keep], [shape(depth, rows), shape(1, rows)],
+        in_large=(4,), out_large=(0,),
+        scratch_shapes=[*scratch([shape(1, rows)]), pltpu.SemaphoreType.DMA((rows // 256,))],
+        aliases={4: 0},
+    )
+
+
+def late_edges(parity, number, step, at, bound, piece, ready, dst, target, gq, gp, rel):
+    (weight, source, query, query_rows, left16, _oh_src, oh_dst, count_l, count_r, kind) = ready
     depth, rows = left16.shape
     edges = weight.shape[1]
     pair16 = shape(2 * depth, edges, dtype=BF16)
 
-    def body(weight, source, target, gq, left16, count_l, kind, rel_in, lgrad, to_src, to_dst, rel_out, probe, probe_rows, gp):
+    def body(piece, weight, source, query, query_rows, left16, oh_dst, count_l, count_r, kind, dst, held_t, held_q, held_p, rel_in,
+             rgrad, to_src, to_dst, rel_out, probe, weights, target, gq, gp, probe_rows):
         rel_out[...] = rel_in[...]
 
         @on_parity(parity)
         def _():
-            join(number, weight, source, target, gq, left16, count_l, kind, rel_in,
-                 probe, probe_rows, gp, lgrad, to_src, to_dst, rel_out, fixed=True)
+            target[...] = held_t[...]
+            gq[...] = held_q[...]
+            take_piece(number, at, piece, query, query_rows, oh_dst, count_r, target, gq, rgrad, fixed=True)
+            late = dst[step : step + 1, :] >= bound
+            w, s, t = weight[...], source[...], target[...]
+            product = jnp.where(late, w * t, 0.0).astype(BF16)
+            probe[...] = product
+            probe_rows[...] = half_rows(product.astype(F32))
+            gp[...] = jnp.zeros_like(gp)
+            size = step_of(rows)
+            for i in range(rows // size):
+                cut = lanes_at(i, size)
+                rows16 = left16[:, cut]
+                part = negative_weights(rows16, probe_rows[...], number)
+                weights[:, cut] = part
+                gp[...] += mul(rows16, often(part, times_at(count_l, i, size)), NT)
+            all_gp = held_p[...] + jnp.where(late, gp[...], 0.0)
+            coef = -jax.nn.sigmoid(-jnp.sum(s * w * t, axis=0, keepdims=True))
+            g_weight = coef * s * t + gq[...] * s + all_gp * t
+            rel_out[...] = rel_in[...] + sum(mul(kind[...], p, NT) for p in split(g_weight, 2))
+            to_src[0:depth, :], to_src[depth:, :] = split(coef * w * t + gq[...] * w, 2)
+            to_dst[0:depth, :], to_dst[depth:, :] = split(jnp.where(late, coef * w * s + all_gp * w, 0.0), 2)
 
     return call(
-        body, "last_join",
-        [weight, source, target, gq, left16, count_l, kind, rel],
-        [shape(depth, rows), pair16, pair16, shape(*rel.shape)],
-        scratch_shapes=scratch([shape(depth, edges, dtype=BF16), shape(edges, depth, dtype=BF16), shape(depth, edges)]),
-    )
-
-
-def last_right(parity, far, rgrads, to_dst, oh_dst, keep):
+        body, "late_edges",
+        [piece, weight, source, query, query_rows, left16, oh_dst, count_l, count_r, kind, dst, target, gq, gp, rel],
+        [shape(depth, piece.shape[1]), pair16, pair16, shape(*rel.shape), shape(depth, edges, dtype=BF16), shape(edges, rows, dtype=BF16)],
+        scratch_shapes=scratch([shape(depth, edges)] * 3 + [shape(edges, depth, dtype=BF16)]),
+    )
+
+
+def late_slabs(parity, at, left, lstate, lgrad, to_src, oh_src, probe, weights, count_l, far, state, rgrads, to_dst, oh_dst, keep_left, keep_right):
+    depth, rows = left.shape
     count = len(far)
-    depth, rows = keep.shape
-
-    def body(to_dst, oh_dst, *rest):
+
+    def body(left, lstate, lgrad, to_src, oh_src, probe, weights, count_l, state, to_dst, oh_dst, *rest):
         pieces, grads = rest[:count], rest[count : 2 * count]
-        out, state, spare, sems = rest[2 * count + 1 :]
-        unpack_state(pieces[STATE], depth, state)
-        update_and_send(pieces, state, grads, to_dst, oh_dst, spare, out, sems, fixed=True)()
-
-    operands = [to_dst, oh_dst, *far, *rgrads, keep]
-    place = len(operands) - 1
+        left_out, right_out, spare, sems = rest[2 * count + 2 :]
+
+        def more(i, size):
+            return mul(probe[...], weights[:, lanes_at(i, size)], NN) * times_at(count_l, i, size)
+
+        wait_left = update_and_send([left], lstate, [lgrad], to_src, oh_src, spare, left_out, sems.at[0], fixed=True, more=more)
+        wait_right = update_and_send(pieces, state, grads, to_dst, oh_dst, spare, right_out, sems.at[1], fixed=True, start=at)
+        wait_left()
+        wait_right()
+
+    operands = [left, lstate, lgrad, to_src, oh_src, probe, weights, count_l, state, to_dst, oh_dst, *far, *rgrads, keep_left, keep_right]
+    places = (len(operands) - 2, len(operands) - 1)
     return call(
-        only_on(parity, body), "last_right", operands, [shape(depth, rows)], in_large=(place,), out_large=(0,),
-        scratch_shapes=[*scratch([shape(1, rows), shape(1, rows)]), pltpu.SemaphoreType.DMA((rows // 256,))],
-        aliases={place: 0},
-    )[0]
-
-
-def last_left(parity, left, lstate, lgrad, to_src, oh_src, relations, relation_state, rels, keep):
-    depth, rows = left.shape
-    kinds = relations.shape[0]
-
-    def body(left, lstate, lgrad, to_src, oh_src, relations, relation_state, *rest):
-        rels = rest[: len(rest) - 7]
-        left_out, relations_out, new_relations, spare, sems, sem = rest[len(rest) - 6 :]
-        grad = sum(ref[...] for ref in rels)
+        only_on(parity, body), "late_slabs", operands, [shape(depth, rows), shape(depth, rows)], in_large=places, out_large=(0, 1),
+        scratch_shapes=[*scratch([shape(1, rows)]), pltpu.SemaphoreType.DMA((2, rows // 256))],
+        aliases={places[0]: 0, places[1]: 1},
+    )
+
+
+def relation_update(relations, relation_state, rels):
+    kinds, depth = relations.shape
+
+    def body(relations, relation_state, *rest):
+        grad = sum(ref[...] for ref in rest[:-1])
         first = lax.broadcasted_iota(jnp.int32, (kinds, kinds), 0)
         second = lax.broadcasted_iota(jnp.int32, (kinds, kinds), 1)
         old = jnp.sum(jnp.where(first == second, relation_state[...], 0.0), axis=1, keepdims=True)
         new = old + jnp.sum(grad * grad, axis=1, keepdims=True) * (1.0 / depth)
-        new_relations[...] = relations[...] - grad * (rate * lax.rsqrt(new))
-        copy = pltpu.make_async_copy(new_relations, relations_out, sem)
-        copy.start()
-
-        @on_parity(parity)
-        def _():
-            update_and_send([left], lstate, [lgrad], to_src, oh_src, spare, left_out, sems, fixed=True)()
-
-        copy.wait()
-
-    operands = [left, lstate, lgrad, to_src, oh_src, relations, relation_state, *rels, keep]
-    place = len(operands) - 1
-    return call(
-        body, "last_left", operands, [shape(depth, rows), shape(*relations.shape)], in_large=(place,), out_large=(0, 1),
-        scratch_shapes=[
-            *scratch([shape(*relations.shape), shape(1, rows)]),
-            pltpu.SemaphoreType.DMA((rows // 256,)),
-            pltpu.SemaphoreType.DMA,
-        ],
-        aliases={place: 0},
-    )
+        rest[-1][...] = relations[...] - grad * (rate * lax.rsqrt(new))
+
+    return call(body, "relation_update", [relations, relation_state, *rels], [shape(kinds, depth)])[0]
 
 
 def local(
@@ -478,24 +527,37 @@
     state_near = state_near.reshape(1, rows)
     rel = jnp.zeros(relations.shape, F32)
     ready = prepared(0, left, relations, index)
-    left_a, lstate, far, rel = trained(1, "first_near", number, FAR, left, lstate, right_near, state_near, rel, ready)
+    left_a, lstate, far, rel = trained(1, "first_near", number, False, FAR, left, lstate, right_near, state_near, rel, ready)
     far = [lax.ppermute(piece, "blk", across) for piece in far]
     left_a, lstate, near, rel = trained(
-        0, "first_far", number, NEAR, left, lstate, [right_far], state_far, rel, ready, (left_a,)
+        0, "first_far", number, True, NEAR, left, lstate, [right_far], state_far, rel, ready, (left_a,)
     )
     near = [lax.ppermute(piece, "blk", inside) for piece in near]
     ready = prepared(1, left_a, relations, index)
-    left_b, lstate, right_b, rel = trained(1, "last_near", number, (), left_a, lstate, near, state_near, rel, ready)
-    target, gq, rgrads = last_pieces(0, number, far, ready, lstate)
-    lgrad, to_src, to_dst, rel = last_join(0, number, target, gq, rel, ready)
+    first_lstate = lstate
+    left_b, lstate, right_b, rel = trained(1, "last_near", number, True, (), left_a, lstate, near, state_near, rel, ready)
+    cuts = pieces_of(rows, FAR)
+    bound = cuts[1][0]
+    target, gq, rgrad = last_piece(0, "last_piece0", number, 0, far[0], ready, lstate)
+    rgrads = [rgrad]
+    lgrad, to_dst, gp = early_edges(0, number, 1, bound, target, ready, dst_index)
+    right_b, state = early_right(0, far[0], rgrad, to_dst, ready[6], right_b[0])
+    for i in range(1, len(far) - 1):
+        target, gq, rgrad = last_piece(0, "last_piece%d" % i, number, cuts[i][0], far[i], ready, right_b, (target, gq))
+        rgrads.append(rgrad)
+    rgrad, to_src, to_dst, rel, probe, weights = late_edges(
+        0, number, 1, cuts[-1][0], bound, far[-1], ready, dst_index, target, gq, gp, rel
+    )
+    rgrads.append(rgrad)
     if lax.axis_size("rel") == 2:
         rels = [rel, lax.ppermute(rel, "rel", [(0, 1), (1, 0)])]
     else:
         rels = [lax.psum(rel, "rel")]
-    right_b = last_right(0, far, rgrads, to_dst, ready[6], right_b[0])
-    left_b, relations_out = last_left(
-        0, left_a, lstate, lgrad, to_src, ready[5], relations, relation_state.reshape(1, -1), rels, left_b
-    )
+    left_b, right_b = late_slabs(
+        0, bound, left_a, first_lstate, lgrad, to_src, ready[5], probe, weights, ready[7],
+        far[1:], state, rgrads[1:], to_dst, ready[6], left_b, right_b,
+    )
+    relations_out = relation_update(relations, relation_state.reshape(1, -1), rels)
     return (left_b.T, right_b.T, relations_out[None])
 
 

time: 90.9 us -> 91.3 us (level)
  Pallas kernels: 32.9 us -> 30.7 us
  local copies, waits for them, and re-layouts: 2.21 us -> 4.13 us
  waiting for transfers between devices: 32.4 us -> 33.4 us
    pallas_call x11 -> x12, Pallas kernels: 32.9 us -> 30.7 us  [call(): pl.pallas_call(kernel, out_shape=tuple(shapes), in_specs=[large if i in i...]
    unnamed x20 -> x22, local copies, waits for them, and re-layouts: 0.04 us -> 1.97 us
    ppermute x3, waiting for transfers between devices: 8.54 us -> 9.53 us  [local(): far = [lax.ppermute(piece, 'blk', across) for piece in far]]
  transfers between devices with their start and end apart: 11 -> 11, of which waited for: 6 -> 4; matrix products, arithmetic and copies ran while one was open for 2% -> 2% of each run, Pallas kernels for 30% -> 30%
where the time goes in v3:
time: 91.3 us; the launch traced here: 91 us
  waiting for transfers between devices  33.4 us (37%)
  Pallas kernels  30.7 us (34%)
  starting transfers between devices  21.7 us (24%)
  local copies, waits for them, and re-layouts  4.13 us (5%)
  between operations  1.01 us (1%)
    pallas_call x12, Pallas kernels, call(): pl.pallas_call(kernel, out_shape=tuple(shapes), in_specs=[large if i in i...  30.7 us
    ppermute x1, waiting for transfers between devices, local(): right_far = lax.ppermute(right, 'blk', across)  18.7 us
    ppermute x3, waiting for transfers between devices, local(): far = [lax.ppermute(piece, 'blk', across) for piece in far]  9.53 us
    ppermute x2, starting transfers between devices, local(): lax.ppermute(right[:, at:at + size], 'blk', inside)  7.28 us
    ppermute x1, waiting for transfers between devices, local(): state_far = lax.ppermute(state_near, 'blk', skip).reshape(1, rows)  4.93 us
    ppermute x3, starting transfers between devices, local(): far = [lax.ppermute(piece, 'blk', across) for piece in far]  3.88 us
    ppermute x1, starting transfers between devices, local(): state_far = lax.ppermute(state_near, 'blk', skip).reshape(1, rows)  3.46 us
    ppermute x2, starting transfers between devices, local(): near = [lax.ppermute(piece, 'blk', inside) for piece in near]  2.79 us
  transfers between devices with their start and end apart: 11, of which 4 were waited for; matrix products, arithmetic and copies ran while one was open for 2% of the time, Pallas kernels for 30%

profile of v3, /device:TPU:0, one launch (start us, length us, event | category | flops | bytes accessed | tf_op | source)
XLA Modules:
  0.0 91.0 jit_solution(17387972060445382751)
XLA Ops:
  0.6 0.0 copy-start.10
  0.6 0.0 copy-start.1
  0.7 0.0 copy-start.2
  0.7 0.0 copy-start.3
  0.7 0.0 copy-start.4
  0.7 0.0 copy-start.5
  0.7 0.0 copy-start.7
  0.7 0.0 copy-start.8
  0.7 1.6 %collective-permute-start.4 = (f32[400,2048]{1,0:T(8,128)}, f32[400,2048]{1,0:T(8,128)S(1)}, u32[]{:S(2)}, u32[]{:S(2)}) collective-permute-start(f32[400,2048]{1,0:T(8,128)} %bitcast.19), channel_id=1, source_target_pairs={{2,4},{6,8},{10,12},{14,16},{18,20},{22,24},{26,28},{30,0},{3,5},{... | collective-permute-start | bytes 9830408 | tf_op jit(solution)/shard_map/ppermute | solution.py:523
  2.3 2.2 %fusion = (f32[400,1024]{1,0:T(8,128)S(1)}, f32[400,1024]{1,0:T(8,128)S(1)}) fusion(f32[400,2048]{1,0:T(8,128)} %bitcast.20), kind=kLoop, calls=%fused_computation | loop fusion | bytes 6553600 | tf_op jit(solution)/shard_map/slice | solution.py:524
  4.4 0.0 copy-start.6
  4.5 5.9 %collective-permute-start.2 = (f32[400,1024]{1,0:T(8,128)S(1)}, f32[400,1024]{1,0:T(8,128)S(1)}, u32[]{:S(2)}, u32[]{:S(2)}) collective-permute-start(f32[400,1024]{1,0:T(8,128)S(1)} %get-tuple-element.111), channel_id=1, source_target_pairs={{0,2},{4,6},{8,10},{12,14},{16,18},{20,22},{24,26},{28,30},{1,3},{... | collective-permute-start | bytes 4915208 | tf_op jit(solution)/shard_map/ppermute | solution.py:524
  10.3 1.4 %collective-permute-start.1 = (f32[400,1024]{1,0:T(8,128)S(1)}, f32[400,1024]{1,0:T(8,128)S(1)}, u32[]{:S(2)}, u32[]{:S(2)}) collective-permute-start(f32[400,1024]{1,0:T(8,128)S(1)} %get-tuple-element.112), channel_id=1, source_target_pairs={{0,2},{4,6},{8,10},{12,14},{16,18},{20,22},{24,26},{28,30},{1,3},{... | collective-permute-start | bytes 4915208 | tf_op jit(solution)/shard_map/ppermute | solution.py:524
  11.7 0.0 copy-done.10
  11.8 0.1 collective-permute-start
  11.8 0.0 copy-done.1
  11.8 0.0 copy-done.2
  11.9 0.0 copy-done.3
  11.9 0.0 copy-done.4
  11.9 0.0 copy-done.5
  11.9 0.0 copy-done.7
  11.9 0.0 copy-done.8
  11.9 3.6 %prepare0.1 = (f32[400,256]{1,0:T(8,128)S(1)}, f32[400,256]{1,0:T(8,128)S(1)}, bf16[400,256]{1,0:T(8,128)(2,1)S(1)}, bf16[256,400]{1,0:T(8,128)(2,1)S(1)}, bf16[...) custom-call(f32[400,2048]{1,0:T(8,128)S(1)} %bitcast.10, ...), custom_call_target="tpu_custom_call" | custom-call | flops 1000000 | bytes 100000 | tf_op jit(solution)/shard_map/prepare0/pallas_call | solution.py:314
  15.5 0.2 collective-permute-done
  15.7 0.0 collective-permute-done.2.refs_15_
  15.7 0.0 collective-permute-done.1.refs_14_
  15.7 0.0 copy-done.6
  15.7 0.2 first_near.1
  15.9 1.3 %collective-permute-start.5 = (f32[408,1536]{1,0:T(8,128)S(1)}, f32[408,1536]{1,0:T(8,128)S(1)}, u32[]{:S(2)}, u32[]{:S(2)}) collective-permute-start(f32[408,1536]{1,0:T(8,128)S(1)} %get-tuple-element.74), channel_id=1, source_target_pairs={{2,4},{6,8},{10,12},{14,16},{18,20},{22,24},{26,28},{30,0},{3,5},{... | collective-permute-start | bytes 7520264 | tf_op jit(solution)/shard_map/ppermute | solution.py:531
  17.2 3.5 %collective-permute-start.3 = (f32[2048]{0:T(1024)S(1)}, f32[2048]{0:T(1024)S(1)}, u32[]{:S(2)}, u32[]{:S(2)}) collective-permute-start(f32[2048]{0:T(1024)S(1)} %collective-permute-done), channel_id=1, source_target_pairs={{0,4},{4,8},{8,12},{12,16},{16,20},{20,24},{24,28},{28,0},{1,5},{5... | collective-permute-start | bytes 24584 | tf_op jit(solution)/shard_map/ppermute | solution.py:526
  20.7 4.9 %collective-permute-done.3 = f32[2048]{0:T(1024)S(1)} collective-permute-done((f32[2048]{0:T(1024)S(1)}, f32[2048]{0:T(1024)S(1)}, u32[]{:S(2)}, u32[]{:S(2)}) %collective-permute-start.3) | collective-permute-done | bytes 8224 | tf_op jit(solution)/shard_map/ppermute | solution.py:526
  25.6 18.7 %collective-permute-done.4.refs_14_ = f32[400,2048]{1,0:T(8,128)S(1)} collective-permute-done((f32[400,2048]{1,0:T(8,128)}, f32[400,2048]{1,0:T(8,128)S(1)}, u32[]{:S(2)}, u32[]{:S(2)}) %collective-permute-start.4) | collective-permute-done | bytes 3276832 | tf_op jit(solution)/shard_map/ppermute | solution.py:523
  44.3 8.0 %first_far.1 = (f32[400,2048]{1,0:T(8,128)S(1)}, f32[1,2048]{1,0:T(1,128)S(1)}, f32[32,400]{1,0:T(8,128)S(1)}, f32[408,1024]{1,0:T(8,128)S(1)}, f32[400,1024]{1,0:T(8,128)S(1)}) custom-call(f32[400,2048]{1,0:T(8,128)S(1)} %bitcast.12, f32[1,2048]{1,0:T(1,128)S(1)} %get-tuple-element.67.refs_1_, ...), custom_call_target="tpu_custom_call", output_to_operand_aliasing={{0}: (15, {})} | custom-call | flops 1000000 | bytes 100000 | tf_op jit(solution)/shard_map/first_far/pallas_call | solution.py:314
  52.3 1.4 %collective-permute-start.6 = (f32[408,1024]{1,0:T(8,128)S(1)}, f32[408,1024]{1,0:T(8,128)S(1)}, u32[]{:S(2)}, u32[]{:S(2)}) collective-permute-start(f32[408,1024]{1,0:T(8,128)S(1)} %get-tuple-element.84), channel_id=1, source_target_pairs={{0,2},{4,6},{8,10},{12,14},{16,18},{20,22},{24,26},{28,30},{1,3},{... | collective-permute-start | bytes 5013512 | tf_op jit(solution)/shard_map/ppermute | solution.py:535
  53.7 1.4 %collective-permute-start.7 = (f32[400,1024]{1,0:T(8,128)S(1)}, f32[400,1024]{1,0:T(8,128)S(1)}, u32[]{:S(2)}, u32[]{:S(2)}) collective-permute-start(f32[400,1024]{1,0:T(8,128)S(1)} %get-tuple-element.85), channel_id=1, source_target_pairs={{0,2},{4,6},{8,10},{12,14},{16,18},{20,22},{24,26},{28,30},{1,3},{... | collective-permute-start | bytes 4915208 | tf_op jit(solution)/shard_map/ppermute | solution.py:535
  55.1 1.3 %collective-permute-start.9 = (f32[400,256]{1,0:T(8,128)S(1)}, f32[400,256]{1,0:T(8,128)S(1)}, u32[]{:S(2)}, u32[]{:S(2)}) collective-permute-start(f32[400,256]{1,0:T(8,128)S(1)} %get-tuple-element.90), channel_id=1, source_target_pairs={{2,4},{6,8},{10,12},{14,16},{18,20},{22,24},{26,28},{30,0},{3,5},{... | collective-permute-start | bytes 1228808 | tf_op jit(solution)/shard_map/ppermute | solution.py:531
  56.4 1.3 %collective-permute-start.8 = (f32[400,256]{1,0:T(8,128)S(1)}, f32[400,256]{1,0:T(8,128)S(1)}, u32[]{:S(2)}, u32[]{:S(2)}) collective-permute-start(f32[400,256]{1,0:T(8,128)S(1)} %get-tuple-element.89), channel_id=1, source_target_pairs={{2,4},{6,8},{10,12},{14,16},{18,20},{22,24},{26,28},{30,0},{3,5},{... | collective-permute-start | bytes 1228808 | tf_op jit(solution)/shard_map/ppermute | solution.py:531
  57.7 3.5 %prepare1.1 = (f32[400,256]{1,0:T(8,128)S(1)}, f32[400,256]{1,0:T(8,128)S(1)}, bf16[400,256]{1,0:T(8,128)(2,1)S(1)}, bf16[256,400]{1,0:T(8,128)(2,1)S(1)}, bf16[...) custom-call(f32[400,2048]{1,0:T(8,128)S(1)} %get-tuple-element.70.le, ...), custom_call_target="tpu_custom_call" | custom-call | flops 1000000 | bytes 100000 | tf_op jit(solution)/shard_map/prepare1/pallas_call | solution.py:314
  61.2 0.0 collective-permute-done.7.refs_15_
  61.3 0.0 collective-permute-done.6.refs_14_
  61.3 0.4 last_near.1
  61.7 9.5 %collective-permute-done.5.refs_0_ = f32[408,1536]{1,0:T(8,128)S(1)} collective-permute-done((f32[408,1536]{1,0:T(8,128)S(1)}, f32[408,1536]{1,0:T(8,128)S(1)}, u32[]{:S(2)}, u32[]{:S(2)}) %collective-permute-start.5) | collective-permute-done | bytes 2506784 | tf_op jit(solution)/shard_map/ppermute | solution.py:531
  71.2 2.9 %last_piece0.1 = (f32[400,256]{1,0:T(8,128)S(1)}, f32[400,256]{1,0:T(8,128)S(1)}, f32[400,1536]{1,0:T(8,128)S(1)}) custom-call(f32[408,1536]{1,0:T(8,128)S(1)} %collective-permute-done.5.refs_0_, bf16[400,256]{1,0:T(8,128)(2,1)S(1)} %get-tuple-element.75.refs_6_.refs_1_.query, bf16[256,400]{1,0:T(8,128)(2,1)S(1)} %get-tuple-element.76.refs_7_.refs_2_.query_rows, ...), custom_call_target="tpu_custom_call" | custom-call | flops 1000000 | bytes 100000 | tf_op jit(solution)/shard_map/last_piece0/pallas_call | solution.py:314
  74.0 2.3 %early_edges.1 = (f32[400,2048]{1,0:T(8,128)S(1)}, bf16[800,256]{1,0:T(8,128)(2,1)S(1)}, f32[400,256]{1,0:T(8,128)S(1)}) custom-call(f32[400,256]{1,0:T(8,128)S(1)} %get-tuple-element.72.refs_4_.refs_0_.weight, f32[400,256]{1,0:T(8,128)S(1)} %get-tuple-element.73.refs_5_.refs_1_.source, f32[400,256]{1,0:T(8,128)S(1)} %get-tuple-element.87.refs_2_.refs_5_, ...), custom_call_target="tpu_custom_call" | custom-call | flops 1000000 | bytes 100000 | tf_op jit(solution)/shard_map/early_edges/pallas_call | solution.py:314
  76.4 2.4 %early_right.1 = (f32[400,2048]{1,0:T(8,128)}, f32[1,2048]{1,0:T(1,128)S(1)}) custom-call(f32[408,1536]{1,0:T(8,128)S(1)} %collective-permute-done.5.refs_0_, f32[400,1536]{1,0:T(8,128)S(1)} %get-tuple-element.92.refs_1_, bf16[800,256]{1,0:T(8,128)(2,1)S(1)} %get-tuple-element.93.refs_2_, ...), custom_call_target="tpu_custom_call", output_to_operand_aliasing={{0}: (4, {})} | custom-call | flops 1000000 | bytes 100000 | tf_op jit(solution)/shard_map/early_right/pallas_call | solution.py:314
  78.8 0.0 collective-permute-done.9.refs_0_.refs_11_
  78.8 0.0 copy-start
  78.8 1.9 %copy-done = f32[400,2048]{1,0:T(8,128)S(1)} copy-done((f32[400,2048]{1,0:T(8,128)S(1)}, f32[400,2048]{1,0:T(8,128)}, u32[]{:S(2)}) %copy-start) | copy-done | bytes 3276824
  80.7 0.6 last_piece1.1
  81.4 0.0 collective-permute-done.8.piece.refs_12_
  81.4 2.7 %late_edges.1 = (f32[400,256]{1,0:T(8,128)S(1)}, bf16[800,256]{1,0:T(8,128)(2,1)S(1)}, bf16[800,256]{1,0:T(8,128)(2,1)S(1)}, f32[32,400]{1,0:T(8,128)S(1)}, bf16...) custom-call(f32[400,256]{1,0:T(8,128)S(1)} %collective-permute-done.8.piece.refs_12_, ...), custom_call_target="tpu_custom_call" | custom-call | flops 1000000 | bytes 100000 | tf_op jit(solution)/shard_map/late_edges/pallas_call | solution.py:314
  84.1 2.7 %collective-permute-start.10 = (f32[32,400]{1,0:T(8,128)S(1)}, f32[32,400]{1,0:T(8,128)S(1)}, u32[]{:S(2)}, u32[]{:S(2)}) collective-permute-start(f32[32,400]{1,0:T(8,128)S(1)} %get-tuple-element.110.rest_0_), channel_id=1, source_target_pairs={{0,1},{1,0},{2,3},{3,2},{4,5},{5,4},{6,7},{7,6},{8,9},{9,8},{10,11... | collective-permute-start | bytes 153608 | tf_op jit(solution)/shard_map/ppermute | solution.py:553
  86.7 0.0 copy-start.9
  86.7 3.5 %late_slabs.1 = (f32[400,2048]{1,0:T(8,128)}, f32[400,2048]{1,0:T(8,128)}) custom-call(f32[400,2048]{1,0:T(8,128)S(1)} %get-tuple-element.70.left.refs_0_, f32[1,2048]{1,0:T(1,128)S(1)} %get-tuple-element.71.refs_1_, f32[400,2048]{1,0:T(8,128)S(1)} %get-tuple-element.88.refs_2_, ...), custom_call_target="tpu_custom_call", output_to_operand_aliasing={{0}: (15, {}), {1}: (16, {})} | custom-call | flops 1000000 | bytes 100000 | tf_op jit(solution)/shard_map/late_slabs/pallas_call | solution.py:314
  90.2 0.0 collective-permute-done.10.rest_1_
  90.2 0.0 copy-done.9
  90.2 0.7 relation_update.1
  (1 shorter events, 0.0 us)
Async XLA Ops:
  0.6 11.1 %copy-start.10 = (f32[2048]{0:T(1024)S(1)}, f32[2048]{0:T(1024)}, u32[]{:S(2)}) copy-start(f32[2048]{0:T(1024)} %param.14) | copy-start | bytes 24580
  0.6 11.2 %copy-start.1 = (f32[2048,400]{0,1:T(8,128)S(1)}, f32[2048,400]{0,1:T(8,128)}, u32[]{:S(2)}) copy-start(f32[2048,400]{0,1:T(8,128)} %param.11) | copy-start | bytes 9830404
  0.7 11.2 %copy-start.2 = (f32[32,400]{1,0:T(8,128)S(1)}, f32[32,400]{1,0:T(8,128)}, u32[]{:S(2)}) copy-start(f32[32,400]{1,0:T(8,128)} %relations.5) | copy-start | bytes 153604
  0.7 11.2 %copy-start.3 = (s32[2,1000]{1,0:T(2,128)S(1)}, s32[2,1000]{1,0:T(2,128)}, u32[]{:S(2)}) copy-start(s32[2,1000]{1,0:T(2,128)} %nsrc.3) | copy-start | bytes 24004
  0.7 11.2 %copy-start.4 = (s32[2,1000]{1,0:T(2,128)S(1)}, s32[2,1000]{1,0:T(2,128)}, u32[]{:S(2)}) copy-start(s32[2,1000]{1,0:T(2,128)} %ndst.3) | copy-start | bytes 24004
  0.7 11.2 %copy-start.5 = (s32[2,256]{1,0:T(2,128)S(1)}, s32[2,256]{1,0:T(2,128)}, u32[]{:S(2)}) copy-start(s32[2,256]{1,0:T(2,128)} %dst.5) | copy-start | bytes 6148
  0.7 11.2 %copy-start.7 = (s32[2,256]{1,0:T(2,128)S(1)}, s32[2,256]{1,0:T(2,128)}, u32[]{:S(2)}) copy-start(s32[2,256]{1,0:T(2,128)} %src.3) | copy-start | bytes 6148
  0.7 11.2 %copy-start.8 = (s32[2,256]{1,0:T(2,128)S(1)}, s32[2,256]{1,0:T(2,128)}, u32[]{:S(2)}) copy-start(s32[2,256]{1,0:T(2,128)} %rid.3) | copy-start | bytes 6148
  0.7 43.6 %collective-permute-start.4 = (f32[400,2048]{1,0:T(8,128)}, f32[400,2048]{1,0:T(8,128)S(1)}, u32[]{:S(2)}, u32[]{:S(2)}) collective-permute-start(f32[400,2048]{1,0:T(8,128)} %bitcast.19), channel_id=1, source_target_pairs={{2,4},{6,8},{10,12},{14,16},{18,20},{22,24},{26,28},{30,0},{3,5},{... | collective-permute-start | bytes 9830408 | tf_op jit(solution)/shard_map/ppermute | solution.py:523
  4.4 11.3 %copy-start.6 = (f32[2048]{0:T(1024)S(1)}, f32[2048]{0:T(1024)}, u32[]{:S(2)}) copy-start(f32[2048]{0:T(1024)} %param.12) | copy-start | bytes 24580
  4.5 11.3 %collective-permute-start.2 = (f32[400,1024]{1,0:T(8,128)S(1)}, f32[400,1024]{1,0:T(8,128)S(1)}, u32[]{:S(2)}, u32[]{:S(2)}) collective-permute-start(f32[400,1024]{1,0:T(8,128)S(1)} %get-tuple-element.111), channel_id=1, source_target_pairs={{0,2},{4,6},{8,10},{12,14},{16,18},{20,22},{24,26},{28,30},{1,3},{... | collective-permute-start | bytes 4915208 | tf_op jit(solution)/shard_map/ppermute | solution.py:524
  10.3 5.4 %collective-permute-start.1 = (f32[400,1024]{1,0:T(8,128)S(1)}, f32[400,1024]{1,0:T(8,128)S(1)}, u32[]{:S(2)}, u32[]{:S(2)}) collective-permute-start(f32[400,1024]{1,0:T(8,128)S(1)} %get-tuple-element.112), channel_id=1, source_target_pairs={{0,2},{4,6},{8,10},{12,14},{16,18},{20,22},{24,26},{28,30},{1,3},{... | collective-permute-start | bytes 4915208 | tf_op jit(solution)/shard_map/ppermute | solution.py:524
  11.8 4.0 %collective-permute-start = (f32[2048]{0:T(1024)S(1)}, f32[2048]{0:T(1024)S(1)}, u32[]{:S(2)}, u32[]{:S(2)}) collective-permute-start(f32[2048]{0:T(1024)S(1)} %copy-done.10), channel_id=1, source_target_pairs={{0,2},{4,6},{8,10},{12,14},{16,18},{20,22},{24,26},{28,30},{2,0},{... | collective-permute-start | bytes 24584 | tf_op jit(solution)/shard_map/ppermute | solution.py:525
  15.9 55.3 %collective-permute-start.5 = (f32[408,1536]{1,0:T(8,128)S(1)}, f32[408,1536]{1,0:T(8,128)S(1)}, u32[]{:S(2)}, u32[]{:S(2)}) collective-permute-start(f32[408,1536]{1,0:T(8,128)S(1)} %get-tuple-element.74), channel_id=1, source_target_pairs={{2,4},{6,8},{10,12},{14,16},{18,20},{22,24},{26,28},{30,0},{3,5},{... | collective-permute-start | bytes 7520264 | tf_op jit(solution)/shard_map/ppermute | solution.py:531
  17.2 8.4 %collective-permute-start.3 = (f32[2048]{0:T(1024)S(1)}, f32[2048]{0:T(1024)S(1)}, u32[]{:S(2)}, u32[]{:S(2)}) collective-permute-start(f32[2048]{0:T(1024)S(1)} %collective-permute-done), channel_id=1, source_target_pairs={{0,4},{4,8},{8,12},{12,16},{16,20},{20,24},{24,28},{28,0},{1,5},{5... | collective-permute-start | bytes 24584 | tf_op jit(solution)/shard_map/ppermute | solution.py:526
  52.3 9.0 %collective-permute-start.6 = (f32[408,1024]{1,0:T(8,128)S(1)}, f32[408,1024]{1,0:T(8,128)S(1)}, u32[]{:S(2)}, u32[]{:S(2)}) collective-permute-start(f32[408,1024]{1,0:T(8,128)S(1)} %get-tuple-element.84), channel_id=1, source_target_pairs={{0,2},{4,6},{8,10},{12,14},{16,18},{20,22},{24,26},{28,30},{1,3},{... | collective-permute-start | bytes 5013512 | tf_op jit(solution)/shard_map/ppermute | solution.py:535
  53.7 7.5 %collective-permute-start.7 = (f32[400,1024]{1,0:T(8,128)S(1)}, f32[400,1024]{1,0:T(8,128)S(1)}, u32[]{:S(2)}, u32[]{:S(2)}) collective-permute-start(f32[400,1024]{1,0:T(8,128)S(1)} %get-tuple-element.85), channel_id=1, source_target_pairs={{0,2},{4,6},{8,10},{12,14},{16,18},{20,22},{24,26},{28,30},{1,3},{... | collective-permute-start | bytes 4915208 | tf_op jit(solution)/shard_map/ppermute | solution.py:535
  55.1 23.7 %collective-permute-start.9 = (f32[400,256]{1,0:T(8,128)S(1)}, f32[400,256]{1,0:T(8,128)S(1)}, u32[]{:S(2)}, u32[]{:S(2)}) collective-permute-start(f32[400,256]{1,0:T(8,128)S(1)} %get-tuple-element.90), channel_id=1, source_target_pairs={{2,4},{6,8},{10,12},{14,16},{18,20},{22,24},{26,28},{30,0},{3,5},{... | collective-permute-start | bytes 1228808 | tf_op jit(solution)/shard_map/ppermute | solution.py:531
  56.4 25.0 %collective-permute-start.8 = (f32[400,256]{1,0:T(8,128)S(1)}, f32[400,256]{1,0:T(8,128)S(1)}, u32[]{:S(2)}, u32[]{:S(2)}) collective-permute-start(f32[400,256]{1,0:T(8,128)S(1)} %get-tuple-element.89), channel_id=1, source_target_pairs={{2,4},{6,8},{10,12},{14,16},{18,20},{22,24},{26,28},{30,0},{3,5},{... | collective-permute-start | bytes 1228808 | tf_op jit(solution)/shard_map/ppermute | solution.py:531
  78.8 1.9 %copy-start = (f32[400,2048]{1,0:T(8,128)S(1)}, f32[400,2048]{1,0:T(8,128)}, u32[]{:S(2)}) copy-start(f32[400,2048]{1,0:T(8,128)} %get-tuple-element.95.refs_7_.refs_16_) | copy-start | bytes 9830404
  84.1 6.2 %collective-permute-start.10 = (f32[32,400]{1,0:T(8,128)S(1)}, f32[32,400]{1,0:T(8,128)S(1)}, u32[]{:S(2)}, u32[]{:S(2)}) collective-permute-start(f32[32,400]{1,0:T(8,128)S(1)} %get-tuple-element.110.rest_0_), channel_id=1, source_target_pairs={{0,1},{1,0},{2,3},{3,2},{4,5},{5,4},{6,7},{7,6},{8,9},{9,8},{10,11... | collective-permute-start | bytes 153608 | tf_op jit(solution)/shard_map/ppermute | solution.py:553
  86.7 3.5 %copy-start.9 = (f32[32]{0:T(128)S(1)}, f32[32]{0:T(128)}, u32[]{:S(2)}) copy-start(f32[32]{0:T(128)} %param.16) | copy-start | bytes 388

commit v4 on v3

--- a/solution.py
+++ b/solution.py
@@ -33,6 +33,11 @@
         out.append(part)
         x = x - part.astype(F32)
     return out
+
+
+def mul_parts(parts, table, dims):
+    along = dims[0][1][0]
+    return mul(jnp.concatenate(parts, axis=1), jnp.concatenate([table] * len(parts), axis=along), dims)
 
 
 def lanes_at(i, size):
@@ -121,7 +126,7 @@
         cut = lanes_at(i, size)
         parts = split(left[:, cut], 3)
         left16[:, cut] = parts[0]
-        source[...] += sum(mul(p, oh_src[:, cut], NT) for p in parts)
+        source[...] += mul_parts(parts, oh_src[:, cut], NT)
 
     each(rows // size, part)
     product = source[...] * weight[...]
@@ -141,7 +146,7 @@
         cut = lanes_at(i, size)
         parts = split(piece[0:depth, cut], 3)
         hits = oh_dst[:, lanes_at(i + start // size, size)]
-        target[...] += sum(mul(p, hits, NT) for p in parts)
+        target[...] += mul_parts(parts, hits, NT)
         times = times_at(count_r, i + start // size, size)
         rgrad[:, cut], more = negatives(parts[0], query[...], query_rows[...], times, number)
         gq[...] += more
@@ -181,7 +186,7 @@
     def part(i):
         cut = lanes_at(i, size)
         hits = table[:, lanes_at(i + start // size, size)]
-        g = grad[:, cut] + mul(edges[0:depth, :], hits, NN) + mul(edges[depth:, :], hits, NN)
+        g = grad[:, cut] + mul_parts([edges[0:depth, :], edges[depth:, :]], hits, NN)
         if more is not None:
             g = g + more(i, size)
         new = state[:, cut] + jnp.sum(g * g, axis=0, keepdims=True) * (1.0 / depth)
@@ -376,7 +381,7 @@
     return call(
         only_on(parity, body), name, operands,
         [shape(depth, edges), shape(depth, edges), shape(depth, piece.shape[1])],
-        in_large=(len(operands) - 1,), aliases={5: 0, 6: 1} if held else {},
+        aliases={5: 0, 6: 1} if held else {},
     )
 
 
@@ -466,43 +471,58 @@
     )
 
 
-def late_slabs(parity, at, left, lstate, lgrad, to_src, oh_src, probe, weights, count_l, far, state, rgrads, to_dst, oh_dst, keep_left, keep_right):
+def late_left(parity, left, lstate, lgrad, to_src, oh_src, probe, weights, count_l, keep):
     depth, rows = left.shape
-    count = len(far)
-
-    def body(left, lstate, lgrad, to_src, oh_src, probe, weights, count_l, state, to_dst, oh_dst, *rest):
-        pieces, grads = rest[:count], rest[count : 2 * count]
-        left_out, right_out, spare, sems = rest[2 * count + 2 :]
-
+
+    def body(left, lstate, lgrad, to_src, oh_src, probe, weights, count_l, _keep, out, spare, sems):
         def more(i, size):
             return mul(probe[...], weights[:, lanes_at(i, size)], NN) * times_at(count_l, i, size)
 
-        wait_left = update_and_send([left], lstate, [lgrad], to_src, oh_src, spare, left_out, sems.at[0], fixed=True, more=more)
-        wait_right = update_and_send(pieces, state, grads, to_dst, oh_dst, spare, right_out, sems.at[1], fixed=True, start=at)
-        wait_left()
-        wait_right()
-
-    operands = [left, lstate, lgrad, to_src, oh_src, probe, weights, count_l, state, to_dst, oh_dst, *far, *rgrads, keep_left, keep_right]
-    places = (len(operands) - 2, len(operands) - 1)
-    return call(
-        only_on(parity, body), "late_slabs", operands, [shape(depth, rows), shape(depth, rows)], in_large=places, out_large=(0, 1),
-        scratch_shapes=[*scratch([shape(1, rows)]), pltpu.SemaphoreType.DMA((2, rows // 256))],
-        aliases={places[0]: 0, places[1]: 1},
-    )
-
-
-def relation_update(relations, relation_state, rels):
-    kinds, depth = relations.shape
-
-    def body(relations, relation_state, *rest):
-        grad = sum(ref[...] for ref in rest[:-1])
+        update_and_send([left], lstate, [lgrad], to_src, oh_src, spare, out, sems, fixed=True, more=more)()
+
+    operands = [left, lstate, lgrad, to_src, oh_src, probe, weights, count_l, keep]
+    return call(
+        only_on(parity, body), "late_left", operands, [shape(depth, rows)], in_large=(8,), out_large=(0,),
+        scratch_shapes=[*scratch([shape(1, rows)]), pltpu.SemaphoreType.DMA((rows // 256,))],
+        aliases={8: 0},
+    )[0]
+
+
+def late_right(parity, at, far, state, rgrads, to_dst, oh_dst, relations, relation_state, rels, keep):
+    depth, rows = keep.shape
+    kinds = relations.shape[0]
+    count = len(far)
+
+    def body(state, to_dst, oh_dst, relations, relation_state, *rest):
+        pieces, grads, rels = rest[:count], rest[count : 2 * count], rest[2 * count : 2 * count + len_rels]
+        out, relations_out, new_relations, spare, sems, sem = rest[2 * count + len_rels + 1 :]
+        grad = sum(ref[...] for ref in rels)
         first = lax.broadcasted_iota(jnp.int32, (kinds, kinds), 0)
         second = lax.broadcasted_iota(jnp.int32, (kinds, kinds), 1)
         old = jnp.sum(jnp.where(first == second, relation_state[...], 0.0), axis=1, keepdims=True)
         new = old + jnp.sum(grad * grad, axis=1, keepdims=True) * (1.0 / depth)
-        rest[-1][...] = relations[...] - grad * (rate * lax.rsqrt(new))
-
-    return call(body, "relation_update", [relations, relation_state, *rels], [shape(kinds, depth)])[0]
+        new_relations[...] = relations[...] - grad * (rate * lax.rsqrt(new))
+        copy = pltpu.make_async_copy(new_relations, relations_out, sem)
+        copy.start()
+
+        @on_parity(parity)
+        def _():
+            update_and_send(pieces, state, grads, to_dst, oh_dst, spare, out, sems, fixed=True, start=at)()
+
+        copy.wait()
+
+    len_rels = len(rels)
+    operands = [state, to_dst, oh_dst, relations, relation_state, *far, *rgrads, *rels, keep]
+    place = len(operands) - 1
+    return call(
+        body, "late_right", operands, [shape(depth, rows), shape(kinds, depth)], in_large=(place,), out_large=(0, 1),
+        scratch_shapes=[
+            *scratch([shape(kinds, depth), shape(1, rows)]),
+            pltpu.SemaphoreType.DMA((rows // 256,)),
+            pltpu.SemaphoreType.DMA,
+        ],
+        aliases={place: 0},
+    )
 
 
 def local(
@@ -543,7 +563,7 @@
     lgrad, to_dst, gp = early_edges(0, number, 1, bound, target, ready, dst_index)
     right_b, state = early_right(0, far[0], rgrad, to_dst, ready[6], right_b[0])
     for i in range(1, len(far) - 1):
-        target, gq, rgrad = last_piece(0, "last_piece%d" % i, number, cuts[i][0], far[i], ready, right_b, (target, gq))
+        target, gq, rgrad = last_piece(0, "last_piece%d" % i, number, cuts[i][0], far[i], ready, state, (target, gq))
         rgrads.append(rgrad)
     rgrad, to_src, to_dst, rel, probe, weights = late_edges(
         0, number, 1, cuts[-1][0], bound, far[-1], ready, dst_index, target, gq, gp, rel
@@ -553,11 +573,10 @@
         rels = [rel, lax.ppermute(rel, "rel", [(0, 1), (1, 0)])]
     else:
         rels = [lax.psum(rel, "rel")]
-    left_b, right_b = late_slabs(
-        0, bound, left_a, first_lstate, lgrad, to_src, ready[5], probe, weights, ready[7],
-        far[1:], state, rgrads[1:], to_dst, ready[6], left_b, right_b,
-    )
-    relations_out = relation_update(relations, relation_state.reshape(1, -1), rels)
+    left_b = late_left(0, left_a, first_lstate, lgrad, to_src, ready[5], probe, weights, ready[7], left_b)
+    right_b, relations_out = late_right(
+        0, bound, far[1:], state, rgrads[1:], to_dst, ready[6], relations, relation_state.reshape(1, -1), rels, right_b
+    )
     return (left_b.T, right_b.T, relations_out[None])
 
 

time: 91.3 us -> 90.4 us (level)
  local copies, waits for them, and re-layouts: 4.13 us -> 2.4 us
  Pallas kernels: 30.7 us -> 32.4 us
  waiting for transfers between devices: 33.4 us -> 32.4 us
    unnamed x22 -> x20, local copies, waits for them, and re-layouts: 1.97 us -> 0.04 us
    pallas_call x12, Pallas kernels: 30.7 us -> 32.4 us  [call(): pl.pallas_call(kernel, out_shape=tuple(shapes), in_specs=[large if i in i...]
  transfers between devices with their start and end apart: 11 -> 11, of which waited for: 4 -> 5; matrix products, arithmetic and copies ran while one was open for 2% -> 3% of each run, Pallas kernels for 30% -> 31%
where the time goes in v4:
time: 90.4 us; the launch traced here: 90.1 us
  Pallas kernels  32.4 us (36%)
  waiting for transfers between devices  32.4 us (36%)
  starting transfers between devices  21.7 us (24%)
  local copies, waits for them, and re-layouts  2.4 us (3%)
  between operations  1.19 us (1%)
    pallas_call x12, Pallas kernels, call(): pl.pallas_call(kernel, out_shape=tuple(shapes), in_specs=[large if i in i...  32.4 us
    ppermute x1, waiting for transfers between devices, local(): right_far = lax.ppermute(right, 'blk', across)  18.5 us
    ppermute x3, waiting for transfers between devices, local(): far = [lax.ppermute(piece, 'blk', across) for piece in far]  8.76 us
    ppermute x2, starting transfers between devices, local(): lax.ppermute(right[:, at:at + size], 'blk', inside)  7.28 us
    ppermute x1, waiting for transfers between devices, local(): state_far = lax.ppermute(state_near, 'blk', skip).reshape(1, rows)  4.93 us
    ppermute x3, starting transfers between devices, local(): far = [lax.ppermute(piece, 'blk', across) for piece in far]  3.88 us
    ppermute x1, starting transfers between devices, local(): state_far = lax.ppermute(state_near, 'blk', skip).reshape(1, rows)  3.46 us
    ppermute x2, starting transfers between devices, local(): near = [lax.ppermute(piece, 'blk', inside) for piece in near]  2.79 us
  transfers between devices with their start and end apart: 11, of which 5 were waited for; matrix products, arithmetic and copies ran while one was open for 3% of the time, Pallas kernels for 31%

profile of v4, /device:TPU:0, one launch (start us, length us, event | category | flops | bytes accessed | tf_op | source)
XLA Modules:
  0.0 90.1 jit_solution(12847718432310504017)
XLA Ops:
  0.6 0.0 copy-start.9
  0.6 0.0 copy-start
  0.7 0.0 copy-start.1
  0.7 0.0 copy-start.2
  0.7 0.0 copy-start.3
  0.7 0.0 copy-start.4
  0.7 0.0 copy-start.6
  0.7 0.0 copy-start.7
  0.7 1.6 %collective-permute-start.4 = (f32[400,2048]{1,0:T(8,128)}, f32[400,2048]{1,0:T(8,128)S(1)}, u32[]{:S(2)}, u32[]{:S(2)}) collective-permute-start(f32[400,2048]{1,0:T(8,128)} %bitcast.19), channel_id=1, source_target_pairs={{2,4},{6,8},{10,12},{14,16},{18,20},{22,24},{26,28},{30,0},{3,5},{... | collective-permute-start | bytes 9830408 | tf_op jit(solution)/shard_map/ppermute | solution.py:543
  2.3 2.3 %fusion = (f32[400,1024]{1,0:T(8,128)S(1)}, f32[400,1024]{1,0:T(8,128)S(1)}) fusion(f32[400,2048]{1,0:T(8,128)} %bitcast.20), kind=kLoop, calls=%fused_computation | loop fusion | bytes 6553600 | tf_op jit(solution)/shard_map/slice | solution.py:544
  4.6 0.0 copy-start.5
  4.6 5.9 %collective-permute-start.2 = (f32[400,1024]{1,0:T(8,128)S(1)}, f32[400,1024]{1,0:T(8,128)S(1)}, u32[]{:S(2)}, u32[]{:S(2)}) collective-permute-start(f32[400,1024]{1,0:T(8,128)S(1)} %get-tuple-element.111), channel_id=1, source_target_pairs={{0,2},{4,6},{8,10},{12,14},{16,18},{20,22},{24,26},{28,30},{1,3},{... | collective-permute-start | bytes 4915208 | tf_op jit(solution)/shard_map/ppermute | solution.py:544
  10.5 1.4 %collective-permute-start.1 = (f32[400,1024]{1,0:T(8,128)S(1)}, f32[400,1024]{1,0:T(8,128)S(1)}, u32[]{:S(2)}, u32[]{:S(2)}) collective-permute-start(f32[400,1024]{1,0:T(8,128)S(1)} %get-tuple-element.112), channel_id=1, source_target_pairs={{0,2},{4,6},{8,10},{12,14},{16,18},{20,22},{24,26},{28,30},{1,3},{... | collective-permute-start | bytes 4915208 | tf_op jit(solution)/shard_map/ppermute | solution.py:544
  11.9 0.0 copy-done.9
  11.9 0.1 collective-permute-start
  12.0 0.0 copy-done
  12.0 0.0 copy-done.1
  12.0 0.0 copy-done.2
  12.1 0.0 copy-done.3
  12.1 0.0 copy-done.4
  12.1 0.0 copy-done.6
  12.1 0.0 copy-done.7
  12.1 3.6 %prepare0.1 = (f32[400,256]{1,0:T(8,128)S(1)}, f32[400,256]{1,0:T(8,128)S(1)}, bf16[400,256]{1,0:T(8,128)(2,1)S(1)}, bf16[256,400]{1,0:T(8,128)(2,1)S(1)}, bf16[...) custom-call(f32[400,2048]{1,0:T(8,128)S(1)} %bitcast.9, ...), custom_call_target="tpu_custom_call" | custom-call | flops 1000000 | bytes 100000 | tf_op jit(solution)/shard_map/prepare0/pallas_call | solution.py:319
  15.7 0.2 collective-permute-done
  15.9 0.0 collective-permute-done.2.refs_15_
  15.9 0.0 collective-permute-done.1.refs_14_
  15.9 0.0 copy-done.5
  15.9 0.2 first_near.1
  16.1 1.3 %collective-permute-start.5 = (f32[408,1536]{1,0:T(8,128)S(1)}, f32[408,1536]{1,0:T(8,128)S(1)}, u32[]{:S(2)}, u32[]{:S(2)}) collective-permute-start(f32[408,1536]{1,0:T(8,128)S(1)} %get-tuple-element.74), channel_id=1, source_target_pairs={{2,4},{6,8},{10,12},{14,16},{18,20},{22,24},{26,28},{30,0},{3,5},{... | collective-permute-start | bytes 7520264 | tf_op jit(solution)/shard_map/ppermute | solution.py:551
  17.4 3.5 %collective-permute-start.3 = (f32[2048]{0:T(1024)S(1)}, f32[2048]{0:T(1024)S(1)}, u32[]{:S(2)}, u32[]{:S(2)}) collective-permute-start(f32[2048]{0:T(1024)S(1)} %collective-permute-done), channel_id=1, source_target_pairs={{0,4},{4,8},{8,12},{12,16},{16,20},{20,24},{24,28},{28,0},{1,5},{5... | collective-permute-start | bytes 24584 | tf_op jit(solution)/shard_map/ppermute | solution.py:546
  20.9 4.9 %collective-permute-done.3 = f32[2048]{0:T(1024)S(1)} collective-permute-done((f32[2048]{0:T(1024)S(1)}, f32[2048]{0:T(1024)S(1)}, u32[]{:S(2)}, u32[]{:S(2)}) %collective-permute-start.3) | collective-permute-done | bytes 8224 | tf_op jit(solution)/shard_map/ppermute | solution.py:546
  25.8 18.5 %collective-permute-done.4.refs_14_ = f32[400,2048]{1,0:T(8,128)S(1)} collective-permute-done((f32[400,2048]{1,0:T(8,128)}, f32[400,2048]{1,0:T(8,128)S(1)}, u32[]{:S(2)}, u32[]{:S(2)}) %collective-permute-start.4) | collective-permute-done | bytes 3276832 | tf_op jit(solution)/shard_map/ppermute | solution.py:543
  44.3 9.2 %first_far.1 = (f32[400,2048]{1,0:T(8,128)S(1)}, f32[1,2048]{1,0:T(1,128)S(1)}, f32[32,400]{1,0:T(8,128)S(1)}, f32[408,1024]{1,0:T(8,128)S(1)}, f32[400,1024]{1,0:T(8,128)}) custom-call(f32[400,2048]{1,0:T(8,128)S(1)} %bitcast.11, f32[1,2048]{1,0:T(1,128)S(1)} %get-tuple-element.67.refs_1_, ...), custom_call_target="tpu_custom_call", output_to_operand_aliasing={{0}: (15, {})} | custom-call | flops 1000000 | bytes 100000 | tf_op jit(solution)/shard_map/first_far/pallas_call | solution.py:319
  53.5 1.4 %collective-permute-start.6 = (f32[408,1024]{1,0:T(8,128)S(1)}, f32[408,1024]{1,0:T(8,128)S(1)}, u32[]{:S(2)}, u32[]{:S(2)}) collective-permute-start(f32[408,1024]{1,0:T(8,128)S(1)} %get-tuple-element.84), channel_id=1, source_target_pairs={{0,2},{4,6},{8,10},{12,14},{16,18},{20,22},{24,26},{28,30},{1,3},{... | collective-permute-start | bytes 5013512 | tf_op jit(solution)/shard_map/ppermute | solution.py:555
  54.9 1.4 %collective-permute-start.7 = (f32[400,1024]{1,0:T(8,128)}, f32[400,1024]{1,0:T(8,128)S(1)}, u32[]{:S(2)}, u32[]{:S(2)}) collective-permute-start(f32[400,1024]{1,0:T(8,128)} %get-tuple-element.85), channel_id=1, source_target_pairs={{0,2},{4,6},{8,10},{12,14},{16,18},{20,22},{24,26},{28,30},{1,3},{... | collective-permute-start | bytes 4915208 | tf_op jit(solution)/shard_map/ppermute | solution.py:555
  56.3 1.3 %collective-permute-start.9 = (f32[400,256]{1,0:T(8,128)S(1)}, f32[400,256]{1,0:T(8,128)S(1)}, u32[]{:S(2)}, u32[]{:S(2)}) collective-permute-start(f32[400,256]{1,0:T(8,128)S(1)} %get-tuple-element.90), channel_id=1, source_target_pairs={{2,4},{6,8},{10,12},{14,16},{18,20},{22,24},{26,28},{30,0},{3,5},{... | collective-permute-start | bytes 1228808 | tf_op jit(solution)/shard_map/ppermute | solution.py:551
  57.6 1.3 %collective-permute-start.8 = (f32[400,256]{1,0:T(8,128)S(1)}, f32[400,256]{1,0:T(8,128)S(1)}, u32[]{:S(2)}, u32[]{:S(2)}) collective-permute-start(f32[400,256]{1,0:T(8,128)S(1)} %get-tuple-element.89), channel_id=1, source_target_pairs={{2,4},{6,8},{10,12},{14,16},{18,20},{22,24},{26,28},{30,0},{3,5},{... | collective-permute-start | bytes 1228808 | tf_op jit(solution)/shard_map/ppermute | solution.py:551
  58.9 3.6 %prepare1.1 = (f32[400,256]{1,0:T(8,128)S(1)}, f32[400,256]{1,0:T(8,128)S(1)}, bf16[400,256]{1,0:T(8,128)(2,1)S(1)}, bf16[256,400]{1,0:T(8,128)(2,1)S(1)}, bf16[...) custom-call(f32[400,2048]{1,0:T(8,128)S(1)} %get-tuple-element.70.le, ...), custom_call_target="tpu_custom_call" | custom-call | flops 1000000 | bytes 100000 | tf_op jit(solution)/shard_map/prepare1/pallas_call | solution.py:319
  62.5 0.0 collective-permute-done.7.refs_15_
  62.5 0.0 collective-permute-done.6.refs_14_
  62.5 0.4 last_near.1
  62.9 8.3 %collective-permute-done.5.refs_0_ = f32[408,1536]{1,0:T(8,128)S(1)} collective-permute-done((f32[408,1536]{1,0:T(8,128)S(1)}, f32[408,1536]{1,0:T(8,128)S(1)}, u32[]{:S(2)}, u32[]{:S(2)}) %collective-permute-start.5) | collective-permute-done | bytes 2506784 | tf_op jit(solution)/shard_map/ppermute | solution.py:551
  71.2 2.9 %last_piece0.1 = (f32[400,256]{1,0:T(8,128)S(1)}, f32[400,256]{1,0:T(8,128)S(1)}, f32[400,1536]{1,0:T(8,128)S(1)}) custom-call(f32[408,1536]{1,0:T(8,128)S(1)} %collective-permute-done.5.refs_0_, bf16[400,256]{1,0:T(8,128)(2,1)S(1)} %get-tuple-element.75.refs_6_.refs_1_.query, bf16[256,400]{1,0:T(8,128)(2,1)S(1)} %get-tuple-element.76.refs_7_.refs_2_.query_rows, ...), custom_call_target="tpu_custom_call" | custom-call | flops 1000000 | bytes 100000 | tf_op jit(solution)/shard_map/last_piece0/pallas_call | solution.py:319
  74.1 2.3 %early_edges.1 = (f32[400,2048]{1,0:T(8,128)S(1)}, bf16[800,256]{1,0:T(8,128)(2,1)S(1)}, f32[400,256]{1,0:T(8,128)S(1)}) custom-call(f32[400,256]{1,0:T(8,128)S(1)} %get-tuple-element.72.refs_4_.refs_0_.weight, f32[400,256]{1,0:T(8,128)S(1)} %get-tuple-element.73.refs_5_.refs_1_.source, f32[400,256]{1,0:T(8,128)S(1)} %get-tuple-element.87.refs_2_.refs_5_, ...), custom_call_target="tpu_custom_call" | custom-call | flops 1000000 | bytes 100000 | tf_op jit(solution)/shard_map/early_edges/pallas_call | solution.py:319
  76.4 2.4 %early_right.1 = (f32[400,2048]{1,0:T(8,128)}, f32[1,2048]{1,0:T(1,128)S(1)}) custom-call(f32[408,1536]{1,0:T(8,128)S(1)} %collective-permute-done.5.refs_0_, f32[400,1536]{1,0:T(8,128)S(1)} %get-tuple-element.92.refs_1_, bf16[800,256]{1,0:T(8,128)(2,1)S(1)} %get-tuple-element.93.refs_2_, ...), custom_call_target="tpu_custom_call", output_to_operand_aliasing={{0}: (4, {})} | custom-call | flops 1000000 | bytes 100000 | tf_op jit(solution)/shard_map/early_right/pallas_call | solution.py:319
  78.8 0.0 collective-permute-done.9.refs_0_.rest_0_
  78.8 0.6 last_piece1.1
  79.5 0.5 collective-permute-done.8.piece.rest_1_
  80.0 2.7 %late_edges.1 = (f32[400,256]{1,0:T(8,128)S(1)}, bf16[800,256]{1,0:T(8,128)(2,1)S(1)}, bf16[800,256]{1,0:T(8,128)(2,1)S(1)}, f32[32,400]{1,0:T(8,128)S(1)}, bf16...) custom-call(f32[400,256]{1,0:T(8,128)S(1)} %collective-permute-done.8.piece.rest_1_, ...), custom_call_target="tpu_custom_call" | custom-call | flops 1000000 | bytes 100000 | tf_op jit(solution)/shard_map/late_edges/pallas_call | solution.py:319
  82.6 2.7 %collective-permute-start.10 = (f32[32,400]{1,0:T(8,128)S(1)}, f32[32,400]{1,0:T(8,128)S(1)}, u32[]{:S(2)}, u32[]{:S(2)}) collective-permute-start(f32[32,400]{1,0:T(8,128)S(1)} %get-tuple-element.107.rest_4_), channel_id=1, source_target_pairs={{0,1},{1,0},{2,3},{3,2},{4,5},{5,4},{6,7},{7,6},{8,9},{9,8},{10,11... | collective-permute-start | bytes 153608 | tf_op jit(solution)/shard_map/ppermute | solution.py:573
  85.3 0.0 copy-start.8
  85.3 3.1 %late_left.1 = f32[400,2048]{1,0:T(8,128)} custom-call(f32[400,2048]{1,0:T(8,128)S(1)} %get-tuple-element.70.left.refs_0_, f32[1,2048]{1,0:T(1,128)S(1)} %get-tuple-element.71.refs_1_, f32[400,2048]{1,0:T(8,128)S(1)} %get-tuple-element.88.refs_2_, bf16[800,256]{1,0:T(8,128)(2,1)S(1)} %get-tuple-element.100.refs_3_, ...), custom_call_target="tpu_custom_call", output_to_operand_aliasing={{}: (8, {})} | custom-call | flops 1000000 | bytes 100000 | tf_op jit(solution)/shard_map/late_left/pallas_call | solution.py:319
  88.4 0.0 collective-permute-done.10.rest_5_
  88.4 0.0 copy-done.8
  88.4 1.5 %late_right.1 = (f32[400,2048]{1,0:T(8,128)}, f32[32,400]{1,0:T(8,128)}) custom-call(f32[1,2048]{1,0:T(1,128)S(1)} %get-tuple-element.95.refs_7_.state, bf16[800,256]{1,0:T(8,128)(2,1)S(1)} %get-tuple-element.104.to_dst, bf16[256,2048]{1,0:T(8,128)(2,1)S(1)} %get-tuple-element.77.refs_10_.refs_3_.oh_dst, ...), custom_call_target="tpu_custom_call", output_to_operand_aliasing={{0}: (11, {})} | custom-call | flops 1000000 | bytes 100000 | tf_op jit(solution)/shard_map/late_right/pallas_call | solution.py:319
  (1 shorter events, 0.0 us)
Async XLA Ops:
  0.6 11.3 %copy-start.9 = (f32[2048]{0:T(1024)S(1)}, f32[2048]{0:T(1024)}, u32[]{:S(2)}) copy-start(f32[2048]{0:T(1024)} %param.14) | copy-start | bytes 24580
  0.6 11.4 %copy-start = (f32[2048,400]{0,1:T(8,128)S(1)}, f32[2048,400]{0,1:T(8,128)}, u32[]{:S(2)}) copy-start(f32[2048,400]{0,1:T(8,128)} %param.11) | copy-start | bytes 9830404
  0.7 11.4 %copy-start.1 = (f32[32,400]{1,0:T(8,128)S(1)}, f32[32,400]{1,0:T(8,128)}, u32[]{:S(2)}) copy-start(f32[32,400]{1,0:T(8,128)} %relations.5) | copy-start | bytes 153604
  0.7 11.4 %copy-start.2 = (s32[2,1000]{1,0:T(2,128)S(1)}, s32[2,1000]{1,0:T(2,128)}, u32[]{:S(2)}) copy-start(s32[2,1000]{1,0:T(2,128)} %nsrc.3) | copy-start | bytes 24004
  0.7 11.4 %copy-start.3 = (s32[2,1000]{1,0:T(2,128)S(1)}, s32[2,1000]{1,0:T(2,128)}, u32[]{:S(2)}) copy-start(s32[2,1000]{1,0:T(2,128)} %ndst.3) | copy-start | bytes 24004
  0.7 11.4 %copy-start.4 = (s32[2,256]{1,0:T(2,128)S(1)}, s32[2,256]{1,0:T(2,128)}, u32[]{:S(2)}) copy-start(s32[2,256]{1,0:T(2,128)} %dst.5) | copy-start | bytes 6148
  0.7 11.4 %copy-start.6 = (s32[2,256]{1,0:T(2,128)S(1)}, s32[2,256]{1,0:T(2,128)}, u32[]{:S(2)}) copy-start(s32[2,256]{1,0:T(2,128)} %src.3) | copy-start | bytes 6148
  0.7 11.4 %copy-start.7 = (s32[2,256]{1,0:T(2,128)S(1)}, s32[2,256]{1,0:T(2,128)}, u32[]{:S(2)}) copy-start(s32[2,256]{1,0:T(2,128)} %rid.3) | copy-start | bytes 6148
  0.7 43.6 %collective-permute-start.4 = (f32[400,2048]{1,0:T(8,128)}, f32[400,2048]{1,0:T(8,128)S(1)}, u32[]{:S(2)}, u32[]{:S(2)}) collective-permute-start(f32[400,2048]{1,0:T(8,128)} %bitcast.19), channel_id=1, source_target_pairs={{2,4},{6,8},{10,12},{14,16},{18,20},{22,24},{26,28},{30,0},{3,5},{... | collective-permute-start | bytes 9830408 | tf_op jit(solution)/shard_map/ppermute | solution.py:543
  4.6 11.3 %copy-start.5 = (f32[2048]{0:T(1024)S(1)}, f32[2048]{0:T(1024)}, u32[]{:S(2)}) copy-start(f32[2048]{0:T(1024)} %param.12) | copy-start | bytes 24580
  4.6 11.3 %collective-permute-start.2 = (f32[400,1024]{1,0:T(8,128)S(1)}, f32[400,1024]{1,0:T(8,128)S(1)}, u32[]{:S(2)}, u32[]{:S(2)}) collective-permute-start(f32[400,1024]{1,0:T(8,128)S(1)} %get-tuple-element.111), channel_id=1, source_target_pairs={{0,2},{4,6},{8,10},{12,14},{16,18},{20,22},{24,26},{28,30},{1,3},{... | collective-permute-start | bytes 4915208 | tf_op jit(solution)/shard_map/ppermute | solution.py:544
  10.5 5.4 %collective-permute-start.1 = (f32[400,1024]{1,0:T(8,128)S(1)}, f32[400,1024]{1,0:T(8,128)S(1)}, u32[]{:S(2)}, u32[]{:S(2)}) collective-permute-start(f32[400,1024]{1,0:T(8,128)S(1)} %get-tuple-element.112), channel_id=1, source_target_pairs={{0,2},{4,6},{8,10},{12,14},{16,18},{20,22},{24,26},{28,30},{1,3},{... | collective-permute-start | bytes 4915208 | tf_op jit(solution)/shard_map/ppermute | solution.py:544
  11.9 4.0 %collective-permute-start = (f32[2048]{0:T(1024)S(1)}, f32[2048]{0:T(1024)S(1)}, u32[]{:S(2)}, u32[]{:S(2)}) collective-permute-start(f32[2048]{0:T(1024)S(1)} %copy-done.9), channel_id=1, source_target_pairs={{0,2},{4,6},{8,10},{12,14},{16,18},{20,22},{24,26},{28,30},{2,0},{... | collective-permute-start | bytes 24584 | tf_op jit(solution)/shard_map/ppermute | solution.py:545
  16.1 55.1 %collective-permute-start.5 = (f32[408,1536]{1,0:T(8,128)S(1)}, f32[408,1536]{1,0:T(8,128)S(1)}, u32[]{:S(2)}, u32[]{:S(2)}) collective-permute-start(f32[408,1536]{1,0:T(8,128)S(1)} %get-tuple-element.74), channel_id=1, source_target_pairs={{2,4},{6,8},{10,12},{14,16},{18,20},{22,24},{26,28},{30,0},{3,5},{... | collective-permute-start | bytes 7520264 | tf_op jit(solution)/shard_map/ppermute | solution.py:551
  17.4 8.4 %collective-permute-start.3 = (f32[2048]{0:T(1024)S(1)}, f32[2048]{0:T(1024)S(1)}, u32[]{:S(2)}, u32[]{:S(2)}) collective-permute-start(f32[2048]{0:T(1024)S(1)} %collective-permute-done), channel_id=1, source_target_pairs={{0,4},{4,8},{8,12},{12,16},{16,20},{20,24},{24,28},{28,0},{1,5},{5... | collective-permute-start | bytes 24584 | tf_op jit(solution)/shard_map/ppermute | solution.py:546
  53.5 9.0 %collective-permute-start.6 = (f32[408,1024]{1,0:T(8,128)S(1)}, f32[408,1024]{1,0:T(8,128)S(1)}, u32[]{:S(2)}, u32[]{:S(2)}) collective-permute-start(f32[408,1024]{1,0:T(8,128)S(1)} %get-tuple-element.84), channel_id=1, source_target_pairs={{0,2},{4,6},{8,10},{12,14},{16,18},{20,22},{24,26},{28,30},{1,3},{... | collective-permute-start | bytes 5013512 | tf_op jit(solution)/shard_map/ppermute | solution.py:555
  54.9 7.6 %collective-permute-start.7 = (f32[400,1024]{1,0:T(8,128)}, f32[400,1024]{1,0:T(8,128)S(1)}, u32[]{:S(2)}, u32[]{:S(2)}) collective-permute-start(f32[400,1024]{1,0:T(8,128)} %get-tuple-element.85), channel_id=1, source_target_pairs={{0,2},{4,6},{8,10},{12,14},{16,18},{20,22},{24,26},{28,30},{1,3},{... | collective-permute-start | bytes 4915208 | tf_op jit(solution)/shard_map/ppermute | solution.py:555
  56.3 22.5 %collective-permute-start.9 = (f32[400,256]{1,0:T(8,128)S(1)}, f32[400,256]{1,0:T(8,128)S(1)}, u32[]{:S(2)}, u32[]{:S(2)}) collective-permute-start(f32[400,256]{1,0:T(8,128)S(1)} %get-tuple-element.90), channel_id=1, source_target_pairs={{2,4},{6,8},{10,12},{14,16},{18,20},{22,24},{26,28},{30,0},{3,5},{... | collective-permute-start | bytes 1228808 | tf_op jit(solution)/shard_map/ppermute | solution.py:551
  57.6 22.4 %collective-permute-start.8 = (f32[400,256]{1,0:T(8,128)S(1)}, f32[400,256]{1,0:T(8,128)S(1)}, u32[]{:S(2)}, u32[]{:S(2)}) collective-permute-start(f32[400,256]{1,0:T(8,128)S(1)} %get-tuple-element.89), channel_id=1, source_target_pairs={{2,4},{6,8},{10,12},{14,16},{18,20},{22,24},{26,28},{30,0},{3,5},{... | collective-permute-start | bytes 1228808 | tf_op jit(solution)/shard_map/ppermute | solution.py:551
  82.6 5.8 %collective-permute-start.10 = (f32[32,400]{1,0:T(8,128)S(1)}, f32[32,400]{1,0:T(8,128)S(1)}, u32[]{:S(2)}, u32[]{:S(2)}) collective-permute-start(f32[32,400]{1,0:T(8,128)S(1)} %get-tuple-element.107.rest_4_), channel_id=1, source_target_pairs={{0,1},{1,0},{2,3},{3,2},{4,5},{5,4},{6,7},{7,6},{8,9},{9,8},{10,11... | collective-permute-start | bytes 153608 | tf_op jit(solution)/shard_map/ppermute | solution.py:573
  85.3 3.1 %copy-start.8 = (f32[32]{0:T(128)S(1)}, f32[32]{0:T(128)}, u32[]{:S(2)}) copy-start(f32[32]{0:T(128)} %param.16) | copy-start | bytes 388
